TPU v7x, 512 devices: a whole 4x4x16 slice. The times are simulated.
512 devices in a mesh: gen: 32 (over z_hi, x, core), tp: 16 (over y, z_lo).
Axes of the slice: x: 4, y: 4, z: 16 (z_hi: 4, z_lo: 4; z = z_hi * 4 + z_lo), core: 2. Of those that a mesh axis runs over, the one named last changes fastest.
Arguments:
- embeddings: bfloat16 [2, 2048, 5120], P(None, 'gen', 'tp'), may hold values from -6 to 6
- cache: bfloat16 [2048, 128, 1024], P(('gen', 'tp'))
- lengths: int32 [2048], P(('gen', 'tp')), may hold values from 1 to 128, as said below
- attn_gain: bfloat16 [5120], P('tp'), may hold values from 0.099609375 to 1.8984375
- wqkv: bfloat16 [5120, 3584], P('tp', 'gen'), may hold values from -0.078125 to 0.078125
- wout: bfloat16 [2560, 5120], P('gen', 'tp'), may hold values from -0.125 to 0.125
- final_gain: bfloat16 [5120], replicated, may hold values from 0.099609375 to 1.8984375
- head: bfloat16 [5120, 131072], P(None, ('gen', 'tp'))
- kept: int32 [16, 2048, 2], P('tp', 'gen'), may hold values from 0 to 63, all different within a row; in each aligned block of 64 rows (0 to 63, 64 to 127, ..., all dimensions but the last counted through in order) at most 2 rows name the same one
- chosen: int32 [2, 2048], P(None, 'gen'), may hold values from 0 to 4095
Outputs:
- logprobs: float32 [2, 2048], P(None, ('gen', 'tp'))
- last_hidden: bfloat16 [2048, 5120], P('gen', 'tp')
- new_entries: bfloat16 [2, 2048, 1024], P(None, ('gen', 'tp'))
Inputs may be any that keep to these rules, and one draw needn't show every extreme that they name: Entries of one row within a slice are distinct; among the rows of one generator replica no block of a slice is kept by more than 2 rows, and some block is kept by exactly 2. `lengths`: some row has a full cache of 128 positions.
All inputs are finite; a program needn't handle non-finite values.
Results may differ from a plain program's by a relative error of at most 0.0083.
Values may be sent and summed in bfloat16 or wider, within the bound.
No kernel may reach another device: no remote copies, remote signals or barrier semaphores. Data moves between devices by JAX's collectives and lax.ppermute only.
A program may use at most 64 MiB of HBM per device.

v0:
```python
import jax
import jax.numpy as jnp
from jax import lax
from jax.sharding import PartitionSpec as P

QUERY_HEADS = 20
KEY_VALUE_HEADS = 4
HEAD_SIZE = 128
BLOCK = 128
KPS = 2
STEPS = 2


epsilon = 1e-06
rope_base = 1000000.0


def apply_rotary(vectors, token_positions):
    half_width = HEAD_SIZE // 2
    exponent = jnp.arange(half_width, dtype=jnp.float32) * (2.0 / HEAD_SIZE)
    inverse = jnp.power(jnp.float32(rope_base), -exponent)
    angles = token_positions.astype(jnp.float32)[:, None, None] * inverse[None, None, :]
    cosine = jnp.cos(angles)
    sine = jnp.sin(angles)
    first_half = vectors[..., :half_width]
    second_half = vectors[..., half_width:]
    return jnp.concatenate(
        [first_half * cosine - second_half * sine, second_half * cosine + first_half * sine],
        axis=-1,
    )


def attend(query_rows, cache_entries_held, row_lengths, fresh_keys, fresh_values):
    row_number = query_rows.shape[0]
    key_value_width = KEY_VALUE_HEADS * HEAD_SIZE
    previous_keys = cache_entries_held[:, :, :key_value_width].reshape(
        row_number, -1, KEY_VALUE_HEADS, HEAD_SIZE
    )
    previous_values = cache_entries_held[:, :, key_value_width:].reshape(
        row_number, -1, KEY_VALUE_HEADS, HEAD_SIZE
    )
    grouped_queries = query_rows.reshape(
        row_number, KEY_VALUE_HEADS, QUERY_HEADS // KEY_VALUE_HEADS, HEAD_SIZE
    )
    scale = HEAD_SIZE ** (-0.5)
    old_scores = (
        jnp.einsum(
            "rkgd,rpkd->rkgp", grouped_queries, previous_keys, preferred_element_type=jnp.float32
        )
        * scale
    )
    visible = jnp.arange(previous_keys.shape[1], dtype=jnp.int32)[None, :] < row_lengths[:, None]
    old_scores = jnp.where(visible[:, None, None, :], old_scores, -jnp.inf)
    new_scores = (
        jnp.einsum(
            "rkgd,rnkd->rkgn", grouped_queries, fresh_keys, preferred_element_type=jnp.float32
        )
        * scale
    )
    peak = jnp.maximum(jnp.max(old_scores, axis=-1), jnp.max(new_scores, axis=-1))[..., None]
    old_exp = jnp.exp(old_scores - peak)
    new_exp = jnp.exp(new_scores - peak)
    total = jnp.sum(old_exp, axis=-1, keepdims=True) + jnp.sum(new_exp, axis=-1, keepdims=True)
    old_weights = (old_exp / total).astype(jnp.bfloat16)
    new_weights = (new_exp / total).astype(jnp.bfloat16)
    mixed = jnp.einsum(
        "rkgp,rpkd->rkgd", old_weights, previous_values, preferred_element_type=jnp.float32
    )
    mixed = mixed + jnp.einsum(
        "rkgn,rnkd->rkgd", new_weights, fresh_values, preferred_element_type=jnp.float32
    )
    return mixed.reshape(row_number, QUERY_HEADS * HEAD_SIZE).astype(jnp.bfloat16)


def block_stats(logits, blocks, starting_shifts, held):
    shaped = logits.reshape(logits.shape[0], held, BLOCK)
    pick = jnp.arange(held, dtype=jnp.int32)[None, :] == blocks[:, None]
    selected = jnp.sum(jnp.where(pick[:, :, None], shaped, 0.0), axis=1)
    peak = jnp.max(selected, axis=1)
    total = jnp.sum(jnp.exp(selected - peak[:, None]), axis=1)
    hit = jnp.arange(BLOCK, dtype=jnp.int32)[None, :] == starting_shifts[:, None]
    picked = jnp.sum(jnp.where(hit, selected, 0.0), axis=1)
    return (peak, total, picked)


def body(embeddings, cache, lengths, attn_gain, wqkv, wout, final_gain, head, kept, chosen):
    tp_count = lax.axis_size("tp")
    gen_count = lax.axis_size("gen")
    tensor_shard_rank = lax.axis_index("tp")
    rows_group = embeddings.shape[1]
    local_row_block = rows_group // tp_count
    query_width = QUERY_HEADS * HEAD_SIZE
    key_value_width = KEY_VALUE_HEADS * HEAD_SIZE
    held = head.shape[1] // BLOCK
    most_rows = max(2, rows_group * KPS // (held * gen_count))
    capacity = held * most_rows
    qkv_whole, out_whole = (
        lax.all_gather(wqkv, "gen", axis=1, tiled=True),
        lax.all_gather(wout, "gen", axis=0, tiled=True),
    )
    gain_wide = attn_gain.astype(jnp.float32)
    final_wide = final_gain.astype(jnp.float32)
    pair_blocks = kept[0].reshape(-1)
    pair_count = pair_blocks.shape[0]
    pair_owner = pair_blocks // held
    owner_onehot = (pair_owner[:, None] == jnp.arange(gen_count, dtype=jnp.int32)[None, :]).astype(
        jnp.int32
    )
    earlier = jnp.cumsum(owner_onehot, axis=0) - owner_onehot
    pair_slot = jnp.sum(earlier * owner_onehot, axis=1)
    slot_target = pair_owner * capacity + pair_slot
    routing = jnp.arange(gen_count * capacity, dtype=jnp.int32)[:, None] == slot_target[None, :]
    routing_rows = routing.astype(jnp.bfloat16)
    send_blocks = (
        jnp.sum(jnp.where(routing, (pair_blocks % held)[None, :] + 1, 0), axis=1) - 1
    ).reshape(gen_count, capacity)
    pair_entry = jnp.arange(pair_count, dtype=jnp.int32) % KPS
    key_list = []
    value_list = []
    entry_list = []
    prob_list = []
    layer_out = embeddings[0]
    for step_index in range(STEPS):
        wide_in = embeddings[step_index].astype(jnp.float32)
        scaled = (wide_in * gain_wide).astype(jnp.bfloat16)
        square_sum = jnp.sum(wide_in * wide_in, axis=1)
        partial_value = jnp.dot(scaled, qkv_whole, preferred_element_type=jnp.float32)
        row_squares = lax.psum(square_sum, "tp")
        projected_hidden = lax.psum_scatter(partial_value, "tp", scatter_dimension=0, tiled=True)
        my_squares = lax.dynamic_slice_in_dim(
            row_squares, tensor_shard_rank * local_row_block, local_row_block, 0
        )
        model_width = wide_in.shape[1] * tp_count
        projected_hidden = projected_hidden * lax.rsqrt(my_squares / model_width + epsilon)[:, None]
        token_positions = lengths + step_index
        query_rows = apply_rotary(
            projected_hidden[:, :query_width].reshape(local_row_block, QUERY_HEADS, HEAD_SIZE),
            token_positions,
        ).astype(jnp.bfloat16)
        appended_keys = apply_rotary(
            projected_hidden[:, query_width : query_width + key_value_width].reshape(
                local_row_block, KEY_VALUE_HEADS, HEAD_SIZE
            ),
            token_positions,
        ).astype(jnp.bfloat16)
        appended_values = (
            projected_hidden[:, query_width + key_value_width :]
            .reshape(local_row_block, KEY_VALUE_HEADS, HEAD_SIZE)
            .astype(jnp.bfloat16)
        )
        key_list.append(appended_keys)
        value_list.append(appended_values)
        entry_list.append(
            jnp.concatenate(
                [
                    appended_keys.reshape(local_row_block, key_value_width),
                    appended_values.reshape(local_row_block, key_value_width),
                ],
                axis=1,
            )
        )
        mixed = attend(
            query_rows, cache, lengths, jnp.stack(key_list, axis=1), jnp.stack(value_list, axis=1)
        )
        output_part = jnp.dot(
            lax.all_gather(mixed, "tp", axis=0, tiled=True),
            out_whole,
            preferred_element_type=jnp.float32,
        )
        layer_out = (wide_in + output_part).astype(jnp.bfloat16)
        full_rows = lax.all_gather(layer_out, "tp", axis=1, tiled=True).astype(jnp.float32)
        normed = (
            full_rows
            * lax.rsqrt(jnp.mean(full_rows * full_rows, axis=1) + epsilon)[:, None]
            * final_wide
        ).astype(jnp.bfloat16)
        codes = chosen[step_index]
        code_slice = jnp.repeat(codes // (KPS * BLOCK), KPS)
        code_entry = jnp.repeat(codes // BLOCK % KPS, KPS)
        code_offset = jnp.repeat(codes % BLOCK, KPS)
        pair_offset = jnp.where(
            (code_slice == tensor_shard_rank) & (code_entry == pair_entry), code_offset, -1
        )
        send_offsets = (
            jnp.sum(jnp.where(routing, pair_offset[None, :] + 1, 0), axis=1) - 1
        ).reshape(gen_count, capacity)
        pair_rows = jnp.repeat(normed, KPS, axis=0)
        send_rows = (
            jnp.dot(routing_rows, pair_rows, preferred_element_type=jnp.float32)
            .astype(jnp.bfloat16)
            .reshape(gen_count, capacity, -1)
        )
        arrived_rows, arrived_blocks, arrived_offsets = (
            lax.all_to_all(send_rows, "gen", split_axis=0, concat_axis=0, tiled=True),
            lax.all_to_all(send_blocks, "gen", split_axis=0, concat_axis=0, tiled=True),
            lax.all_to_all(send_offsets, "gen", split_axis=0, concat_axis=0, tiled=True),
        )
        item_count = arrived_rows.shape[1]
        logits = jnp.dot(
            arrived_rows.reshape(-1, arrived_rows.shape[2]),
            head,
            preferred_element_type=jnp.float32,
        )
        peak, total, picked = block_stats(
            logits, arrived_blocks.reshape(-1), arrived_offsets.reshape(-1), held
        )
        back_peak, back_total, back_pick = (
            lax.all_to_all(
                peak.reshape(-1, item_count), "gen", split_axis=0, concat_axis=0, tiled=True
            ),
            lax.all_to_all(
                total.reshape(-1, item_count), "gen", split_axis=0, concat_axis=0, tiled=True
            ),
            lax.all_to_all(
                picked.reshape(-1, item_count), "gen", split_axis=0, concat_axis=0, tiled=True
            ),
        )
        pair_peak = jnp.sum(
            jnp.where(routing, back_peak.reshape(-1)[:, None], 0.0), axis=0
        ).reshape(rows_group, KPS)
        pair_total = jnp.sum(
            jnp.where(routing, back_total.reshape(-1)[:, None], 0.0), axis=0
        ).reshape(rows_group, KPS)
        pair_pick = jnp.sum(
            jnp.where(routing, back_pick.reshape(-1)[:, None], 0.0), axis=0
        ).reshape(rows_group, KPS)
        row_peak = jnp.max(pair_peak, axis=1)
        row_total = jnp.sum(pair_total * jnp.exp(pair_peak - row_peak[:, None]), axis=1)
        row_pick = jnp.sum(pair_pick, axis=1)
        global_peak = lax.pmax(row_peak, "tp")
        mass_sum, pick_sum = lax.psum((row_total * jnp.exp(row_peak - global_peak), row_pick), "tp")
        logprob = pick_sum - global_peak - jnp.log(mass_sum)
        prob_list.append(
            lax.dynamic_slice_in_dim(
                logprob, tensor_shard_rank * local_row_block, local_row_block, 0
            )
        )
    return (jnp.stack(prob_list, axis=0), layer_out, jnp.stack(entry_list, axis=0))


def solution(mesh):
    return jax.shard_map(
        body,
        mesh=mesh,
        in_specs=(
            P(None, "gen", "tp"),
            P(("gen", "tp"), None, None),
            P(("gen", "tp")),
            P("tp"),
            P("tp", "gen"),
            P("gen", "tp"),
            P(),
            P(None, ("gen", "tp")),
            P("tp", "gen", None),
            P(None, "gen"),
        ),
        out_specs=(P(None, ("gen", "tp")), P("gen", "tp"), P(None, ("gen", "tp"), None)),
        check_vma=False,
    )
```

profile of v0, /device:TPU:1, one launch (start us, length us, event | category | flops | bytes accessed | tf_op | source)
XLA Modules:
  0.0 895.7 jit_solution(8148418078200564372)
XLA Ops:
  9.4 89.3 %all-gather.10.cloned.1.call-done = bf16[32,112,320]{1,2,0:T(8,128)(2,1)} async-done(((bf16[1,112,320]{1,2,0:T(8,128)(2,1)}), bf16[32,112,320]{1,2,0:T(8,128)(2,1)}) %all-gather.10.cloned.1.call-update) | async-done | bytes 2293776 | tf_op jit(solution)/shard_map/all_gather | solution.py:98
  98.7 5.0 copy.143
  103.7 5.3 reshape.657
  115.7 9.4 %all-to-all-start.1 = ((s32[32,1,4]{2,1,0:T(1,128)}), s32[32,1,4]{2,1,0:T(1,128)}, u32[]{:S(2)}, u32[]{:S(2)}) async-start(s32[32,1,4]{2,1,0:T(1,128)} %bitcast.2), calls=%async_computation.1 | async-start | bytes 32768 | tf_op jit(solution)/shard_map/all_to_all | solution.py:195
  128.9 35.1 %all-reduce.3 = (f32[64]{0:T(128)S(1)}, f32[64]{0:T(128)S(1)}) all-reduce(f32[64]{0:T(128)S(1)} %get-tuple-element.3, f32[64]{0:T(128)S(1)} %get-tuple-element.4), channel_id=1, replica_groups=mesh['gen'=32,'tp'=16] {'tp'}, use_global_device_ids=true, to_apply=%region_6.7 | all-reduce | flops 128 | bytes 1024 | tf_op jit(solution)/shard_map/psum | solution.py:128
  166.9 116.4 %all-reduce.8.cloned.1.call-done = (f32[64,3584]{1,0:T(8,128)}, f32[64,3584]{1,0:T(8,128)}) async-done(((f32[64,3584]{1,0:T(8,128)}, f32[64,3584]{1,0:T(8,128)}), (f32[64,3584]{1,0:T(8,128)}, f32[64,3584]{1,0:T(8,128)})) %all-reduce.8.cloned.1.call-update) | async-done | bytes 1835024
  287.8 37.2 %all-gather.1 = bf16[16,4,2560]{2,1,0:T(4,128)(2,1)S(1)} all-gather(bf16[1,4,2560]{2,1,0:T(4,128)(2,1)S(1)} %reshape.658), channel_id=1, replica_groups=mesh['gen'=32,'tp'=16] {'tp'}, dimensions={0}, use_global_device_ids=true | all-gather | bytes 348160 | tf_op jit(solution)/shard_map/all_gather | solution.py:166
  325.1 46.8 %all-gather.8.cloned.1.call-done = bf16[2560,320]{1,0:T(8,128)(2,1)} async-done(((bf16[80,320]{1,0:T(8,128)(2,1)}), bf16[2560,320]{1,0:T(8,128)(2,1)}) %all-gather.8.cloned.1.call-update) | async-done | bytes 1638416 | tf_op jit(solution)/shard_map/all_gather | solution.py:99
  373.9 40.8 %all-gather.2 = bf16[16,320,64]{1,2,0:T(8,128)(2,1)S(1)} all-gather(bf16[1,320,64]{1,2,0:T(8,128)(2,1)S(1)} %fusion.8), channel_id=1, replica_groups=mesh['gen'=32,'tp'=16] {'tp'}, dimensions={0}, use_global_device_ids=true | all-gather | bytes 696320 | tf_op jit(solution)/shard_map/all_gather | solution.py:171
  423.4 35.8 %all-gather.3 = bf16[16,4,2560]{2,1,0:T(4,128)(2,1)} all-gather(bf16[1,4,2560]{2,1,0:T(4,128)(2,1)S(1)} %reshape.662), channel_id=1, replica_groups=mesh['gen'=32,'tp'=16] {'tp'}, dimensions={0}, use_global_device_ids=true | all-gather | bytes 348160 | tf_op jit(solution)/shard_map/all_gather | solution.py:166
  462.4 39.5 %all-gather.4 = bf16[16,320,64]{1,2,0:T(8,128)(2,1)S(1)} all-gather(bf16[1,320,64]{1,2,0:T(8,128)(2,1)S(1)} %bitcast.153), channel_id=1, replica_groups=mesh['gen'=32,'tp'=16] {'tp'}, dimensions={0}, use_global_device_ids=true | all-gather | bytes 696320 | tf_op jit(solution)/shard_map/all_gather | solution.py:171
  505.6 30.7 %all-to-all-start.6 = ((s32[32,1,4]{2,1,0:T(1,128)}), s32[32,1,4]{2,1,0:T(1,128)S(1)}, u32[]{:S(2)}, u32[]{:S(2)}) async-start(s32[32,1,4]{2,1,0:T(1,128)} %bitcast.23), calls=%async_computation.6 | async-start | bytes 32768 | tf_op jit(solution)/shard_map/all_to_all | solution.py:196
  537.8 12.6 %all-to-all-done.6 = s32[32,1,4]{2,1,0:T(1,128)S(1)} async-done(((s32[32,1,4]{2,1,0:T(1,128)}), s32[32,1,4]{2,1,0:T(1,128)S(1)}, u32[]{:S(2)}, u32[]{:S(2)}) %all-to-all-start.6) | async-done | bytes 544 | tf_op jit(solution)/shard_map/all_to_all | solution.py:196
  550.4 4.1 all-to-all-start
  556.4 12.4 %all-to-all-done = s32[32,1,4]{2,1,0:T(1,128)S(1)} async-done(((s32[32,1,4]{2,1,0:T(1,128)}), s32[32,1,4]{2,1,0:T(1,128)S(1)}, u32[]{:S(2)}, u32[]{:S(2)}) %all-to-all-start) | async-done | bytes 544 | tf_op jit(solution)/shard_map/all_to_all | solution.py:196
  568.8 4.3 all-to-all-start.7
  578.3 52.6 %all-to-all-done.7 = bf16[32,4,5120]{2,1,0:T(4,128)(2,1)S(1)} async-done(((bf16[32,4,5120]{2,1,0:T(4,128)(2,1)}), bf16[32,4,5120]{2,1,0:T(4,128)(2,1)S(1)}, u32[]{:S(2)}, u32[]{:S(2)}) %all-to-all-start.7) | async-done | bytes 1310752 | tf_op jit(solution)/shard_map/all_to_all | solution.py:194
  632.0 8.4 all-to-all-start.2
  653.8 51.5 %all-to-all-done.2 = bf16[32,4,5120]{2,1,0:T(4,128)(2,1)} async-done(((bf16[32,4,5120]{2,1,0:T(4,128)(2,1)}), bf16[32,4,5120]{2,1,0:T(4,128)(2,1)}, u32[]{:S(2)}, u32[]{:S(2)}) %all-to-all-start.2) | async-done | bytes 1310752 | tf_op jit(solution)/shard_map/all_to_all | solution.py:194
  705.2 6.8 all-to-all-start.8
  716.1 10.1 %all-to-all-done.8 = f32[32,1,4]{2,1,0:T(1,128)S(1)} async-done(((f32[32,1,4]{2,1,0:T(1,128)}), f32[32,1,4]{2,1,0:T(1,128)S(1)}, u32[]{:S(2)}, u32[]{:S(2)}) %all-to-all-start.8) | async-done | bytes 544 | tf_op jit(solution)/shard_map/all_to_all | solution.py:214
  726.2 4.5 all-to-all-start.10
  733.8 11.0 %all-to-all-done.10 = f32[32,1,4]{2,1,0:T(1,128)S(1)} async-done(((f32[32,1,4]{2,1,0:T(1,128)}), f32[32,1,4]{2,1,0:T(1,128)S(1)}, u32[]{:S(2)}, u32[]{:S(2)}) %all-to-all-start.10) | async-done | bytes 544 | tf_op jit(solution)/shard_map/all_to_all | solution.py:211
  744.8 4.1 all-to-all-start.9
  749.8 13.4 %all-to-all-done.9 = f32[32,1,4]{2,1,0:T(1,128)S(1)} async-done(((f32[32,1,4]{2,1,0:T(1,128)}), f32[32,1,4]{2,1,0:T(1,128)S(1)}, u32[]{:S(2)}, u32[]{:S(2)}) %all-to-all-start.9) | async-done | bytes 544 | tf_op jit(solution)/shard_map/all_to_all | solution.py:208
  763.2 4.4 all-to-all-start.3
  768.4 13.4 %all-to-all-done.3 = f32[32,1,4]{2,1,0:T(1,128)S(1)} async-done(((f32[32,1,4]{2,1,0:T(1,128)}), f32[32,1,4]{2,1,0:T(1,128)S(1)}, u32[]{:S(2)}, u32[]{:S(2)}) %all-to-all-start.3) | async-done | bytes 544 | tf_op jit(solution)/shard_map/all_to_all | solution.py:214
  781.8 4.2 all-to-all-start.5
  786.7 13.6 %all-to-all-done.5 = f32[32,1,4]{2,1,0:T(1,128)S(1)} async-done(((f32[32,1,4]{2,1,0:T(1,128)}), f32[32,1,4]{2,1,0:T(1,128)S(1)}, u32[]{:S(2)}, u32[]{:S(2)}) %all-to-all-start.5) | async-done | bytes 544 | tf_op jit(solution)/shard_map/all_to_all | solution.py:211
  809.5 9.1 %all-to-all-done.4 = f32[32,1,4]{2,1,0:T(1,128)S(1)} async-done(((f32[32,1,4]{2,1,0:T(1,128)}), f32[32,1,4]{2,1,0:T(1,128)S(1)}, u32[]{:S(2)}, u32[]{:S(2)}) %all-to-all-start.4) | async-done | bytes 544 | tf_op jit(solution)/shard_map/all_to_all | solution.py:208
  820.4 35.8 %all-reduce.5 = (f32[64]{0:T(128)S(1)}, f32[64]{0:T(128)S(1)}) all-reduce(f32[64]{0:T(128)S(1)} %reduce_max.73, f32[64]{0:T(128)S(1)} %reduce_max.69), channel_id=1, replica_groups=mesh['gen'=32,'tp'=16] {'tp'}, use_global_device_ids=true, to_apply=%region_40.41 | all-reduce | flops 128 | bytes 1024 | tf_op jit(solution)/shard_map/pmax | solution.py:230
  857.1 31.3 %all-reduce.2 = (f32[64]{0:T(128)S(1)}, f32[64]{0:T(128)S(1)}, f32[64]{0:T(128)S(1)}, f32[64]{0:T(128)S(1)}) all-reduce(f32[64]{0:T(128)S(1)} %exponential_multiply_fusion, f32[64]{0:T(128)S(1)} %reduce_sum.269, f32[64]{0:T(128)S(1)} %exponential_multiply_fusion.1, f32[64]{0:T(128)S(1)} %reduce_sum.256), channel_id=1, replica_groups=mesh['gen'=32,'tp'=16] {'tp'}, use_global_device_ids=true, to_apply=%region_44.45 | all-reduce | flops 256 | bytes 2048 | tf_op jit(solution)/shard_map/psum | solution.py:231
  (231 shorter events, 81.6 us)
Async XLA Ops:
  7.2 91.6 %all-gather.10.cloned.1.call-start = ((), (), s32[]{:S(2)}) async-start(), calls=%async_computation.12 | async-start | bytes 2703360 | tf_op jit(solution)/shard_map/all_gather | solution.py:98
  7.9 275.3 %all-reduce.8.cloned.1.call-start = ((), (), s32[]{:S(2)}) async-start(), calls=%async_computation.13 | async-start | bytes 3670016
  103.7 5.3 copy-start.3
  112.0 14.0 %copy-start.22 = (s32[4]{0:T(128)S(1)}, s32[4]{0:T(128)}, u32[]{:S(2)}) copy-start(s32[4]{0:T(128)} %param.12) | copy-start | bytes 52
  112.0 14.1 %copy-start.2 = (bf16[4,128,1024]{2,1,0:T(8,128)(2,1)S(1)}, bf16[4,128,1024]{2,1,0:T(8,128)(2,1)}, u32[]{:S(2)}) copy-start(bf16[4,128,1024]{2,1,0:T(8,128)(2,1)} %param.11) | copy-start | bytes 3145732
  114.7 11.7 %copy-start.15 = (s32[128]{0:T(128)}, s32[128]{0:T(128)S(1)}, u32[]{:S(2)}) copy-start(s32[128]{0:T(128)S(1)} %multiply_add_fusion.1) | copy-start | bytes 1540
  115.7 389.9 %all-to-all-start.1 = ((s32[32,1,4]{2,1,0:T(1,128)}), s32[32,1,4]{2,1,0:T(1,128)}, u32[]{:S(2)}, u32[]{:S(2)}) async-start(s32[32,1,4]{2,1,0:T(1,128)} %bitcast.2), calls=%async_computation.1 | async-start | bytes 32768 | tf_op jit(solution)/shard_map/all_to_all | solution.py:195
  125.1 246.8 %all-gather.8.cloned.1.call-start = ((), (), s32[]{:S(2)}) async-start(), calls=%async_computation.11 | async-start | bytes 2027520 | tf_op jit(solution)/shard_map/all_gather | solution.py:99
  126.1 160.6 %copy-start.18 = (pred[4,128]{1,0:T(4,128)(4,1)}, pred[4,128]{1,0:T(4,128)(4,1)S(1)}, u32[]{:S(2)}) copy-start(pred[4,128]{1,0:T(4,128)(4,1)S(1)} %iota_compare_fusion.6) | copy-start | bytes 1540
  126.9 160.9 %copy-start.4 = (bf16[4,128,512]{1,2,0:T(8,128)(2,1)}, bf16[4,128,512]{1,2,0:T(8,128)(2,1)S(1)}, u32[]{:S(2)}) copy-start(bf16[4,128,512]{1,2,0:T(8,128)(2,1)S(1)} %copy.183) | copy-start | bytes 1572868
  284.3 3.5 copy-start.8
  415.6 2.0 copy-start.12
  415.7 2.0 copy-start.13
  415.7 2.2 copy-start.11
  415.7 2.8 copy-start.19
  418.8 42.1 %copy-start = (bf16[2560,320]{1,0:T(8,128)(2,1)S(1)}, bf16[2560,320]{1,0:T(8,128)(2,1)}, u32[]{:S(2)}) copy-start(bf16[2560,320]{1,0:T(8,128)(2,1)} %all-gather.8.cloned.1.call-done) | copy-start | bytes 4915204
  462.4 41.2 %copy-start.5 = (bf16[64,320]{1,0:T(8,128)(2,1)}, bf16[64,320]{1,0:T(8,128)(2,1)S(1)}, u32[]{:S(2)}) copy-start(bf16[64,320]{1,0:T(8,128)(2,1)S(1)} %fusion.3) | copy-start | bytes 122884
  505.3 30.9 %copy-start.7 = (f32[5120]{0:T(1024)S(1)}, f32[5120]{0:T(1024)}, u32[]{:S(2)}) copy-start(f32[5120]{0:T(1024)} %convert_element_type.160) | copy-start | bytes 61444
  505.3 30.9 %copy-start.21 = (f32[64]{0:T(128)S(1)}, f32[64]{0:T(128)}, u32[]{:S(2)}) copy-start(f32[64]{0:T(128)} %add_rsqrt_fusion.2) | copy-start | bytes 772
  505.6 44.8 %all-to-all-start.6 = ((s32[32,1,4]{2,1,0:T(1,128)}), s32[32,1,4]{2,1,0:T(1,128)S(1)}, u32[]{:S(2)}, u32[]{:S(2)}) async-start(s32[32,1,4]{2,1,0:T(1,128)} %bitcast.23), calls=%async_computation.6 | async-start | bytes 32768 | tf_op jit(solution)/shard_map/all_to_all | solution.py:196
  537.3 17.3 %copy-start.16 = (s32[128]{0:T(128)S(1)}, s32[128]{0:T(128)}, u32[]{:S(2)}) copy-start(s32[128]{0:T(128)} %copy-done.15) | copy-start | bytes 1540
  550.4 18.4 %all-to-all-start = ((s32[32,1,4]{2,1,0:T(1,128)}), s32[32,1,4]{2,1,0:T(1,128)S(1)}, u32[]{:S(2)}, u32[]{:S(2)}) async-start(s32[32,1,4]{2,1,0:T(1,128)} %bitcast.1), calls=%async_computation | async-start | bytes 32768 | tf_op jit(solution)/shard_map/all_to_all | solution.py:196
  568.8 62.1 %all-to-all-start.7 = ((bf16[32,4,5120]{2,1,0:T(4,128)(2,1)}), bf16[32,4,5120]{2,1,0:T(4,128)(2,1)S(1)}, u32[]{:S(2)}, u32[]{:S(2)}) async-start(bf16[32,4,5120]{2,1,0:T(4,128)(2,1)} %reshape.648), calls=%async_computation.7 | async-start | bytes 2621440 | tf_op jit(solution)/shard_map/all_to_all | solution.py:194
  632.0 73.3 %all-to-all-start.2 = ((bf16[32,4,5120]{2,1,0:T(4,128)(2,1)}), bf16[32,4,5120]{2,1,0:T(4,128)(2,1)}, u32[]{:S(2)}, u32[]{:S(2)}) async-start(bf16[32,4,5120]{2,1,0:T(4,128)(2,1)} %reshape.638), calls=%async_computation.2 | async-start | bytes 2621440 | tf_op jit(solution)/shard_map/all_to_all | solution.py:194
  650.4 61.6 %copy-start.9 = (bf16[4,512]{1,0:T(4,128)(2,1)S(1)}, bf16[4,512]{1,0:T(4,128)(2,1)}, u32[]{:S(2)}) copy-start(bf16[4,512]{1,0:T(4,128)(2,1)} %copy-done.8) | copy-start | bytes 12292
  705.2 21.0 %all-to-all-start.8 = ((f32[32,1,4]{2,1,0:T(1,128)}), f32[32,1,4]{2,1,0:T(1,128)S(1)}, u32[]{:S(2)}, u32[]{:S(2)}) async-start(f32[32,1,4]{2,1,0:T(1,128)} %bitcast.35), calls=%async_computation.8 | async-start | bytes 32768 | tf_op jit(solution)/shard_map/all_to_all | solution.py:214
  726.2 18.6 %all-to-all-start.10 = ((f32[32,1,4]{2,1,0:T(1,128)}), f32[32,1,4]{2,1,0:T(1,128)S(1)}, u32[]{:S(2)}, u32[]{:S(2)}) async-start(f32[32,1,4]{2,1,0:T(1,128)} %bitcast.37), calls=%async_computation.10 | async-start | bytes 32768 | tf_op jit(solution)/shard_map/all_to_all | solution.py:211
  730.7 55.3 %copy-start.10 = (bf16[4,512]{1,0:T(4,128)(2,1)S(1)}, bf16[4,512]{1,0:T(4,128)(2,1)}, u32[]{:S(2)}) copy-start(bf16[4,512]{1,0:T(4,128)(2,1)} %slice.132) | copy-start | bytes 12292
  744.8 18.4 %all-to-all-start.9 = ((f32[32,1,4]{2,1,0:T(1,128)}), f32[32,1,4]{2,1,0:T(1,128)S(1)}, u32[]{:S(2)}, u32[]{:S(2)}) async-start(f32[32,1,4]{2,1,0:T(1,128)} %bitcast.36), calls=%async_computation.9 | async-start | bytes 32768 | tf_op jit(solution)/shard_map/all_to_all | solution.py:208
  763.2 18.6 %all-to-all-start.3 = ((f32[32,1,4]{2,1,0:T(1,128)}), f32[32,1,4]{2,1,0:T(1,128)S(1)}, u32[]{:S(2)}, u32[]{:S(2)}) async-start(f32[32,1,4]{2,1,0:T(1,128)} %bitcast.18), calls=%async_computation.3 | async-start | bytes 32768 | tf_op jit(solution)/shard_map/all_to_all | solution.py:214
  781.8 18.4 %all-to-all-start.5 = ((f32[32,1,4]{2,1,0:T(1,128)}), f32[32,1,4]{2,1,0:T(1,128)S(1)}, u32[]{:S(2)}, u32[]{:S(2)}) async-start(f32[32,1,4]{2,1,0:T(1,128)} %bitcast.20), calls=%async_computation.5 | async-start | bytes 32768 | tf_op jit(solution)/shard_map/all_to_all | solution.py:211
  800.2 18.3 %all-to-all-start.4 = ((f32[32,1,4]{2,1,0:T(1,128)}), f32[32,1,4]{2,1,0:T(1,128)S(1)}, u32[]{:S(2)}, u32[]{:S(2)}) async-start(f32[32,1,4]{2,1,0:T(1,128)} %bitcast.19), calls=%async_computation.4 | async-start | bytes 32768 | tf_op jit(solution)/shard_map/all_to_all | solution.py:208
  (5 other events, 4.4 us)
Sparse Core Ops, SparseCore 0:
  11.1 87.5 all-gather.9
  112.1 171.0 all-reduce.7
  286.9 84.9 all-gather.7
where the time goes:
time: 911 us; the launch traced here: 896 us
  waiting for transfers between devices  454 us (50%)
  blocking collectives  256 us (28%)
  starting transfers between devices  85 us (9%)
  local copies, waits for them, and re-layouts  51.1 us (6%)
  matrix products  18.3 us (2%)
  other arithmetic  16.9 us (2%)
  between operations  15.4 us (2%)
    unnamed x4, waiting for transfers between devices  118 us
    all_to_all x2, waiting for transfers between devices, body(): lax.all_to_all(send_rows, 'gen', split_axis=0, concat_axis=0, tiled=True)  104 us
    all_gather x1, waiting for transfers between devices, body(): lax.all_gather(wqkv, 'gen', axis=1, tiled=True)  89.3 us
    all_gather x2, blocking collectives, body(): lax.all_gather(layer_out, 'tp', axis=1, tiled=True).astype(jnp.float32)  80.3 us
    all_gather x2, blocking collectives, body(): lax.all_gather(mixed, 'tp', axis=0, tiled=True)  73 us
    all_gather x1, waiting for transfers between devices, body(): lax.all_gather(wout, 'gen', axis=0, tiled=True)  46.8 us
    pmax x1, blocking collectives, body(): global_peak = lax.pmax(row_peak, 'tp')  35.8 us
    psum x1, blocking collectives, body(): row_squares = lax.psum(square_sum, 'tp')  35.1 us
  transfers between devices with their start and end apart: 14, of which 13 were waited for; matrix products, arithmetic and copies ran while one was open for 7% of the time, Pallas kernels for 0%

commit v1 on v0

v1 whole, which is shorter than its diff:
```python
import jax
import jax.numpy as jnp
from jax import lax
from jax.experimental import pallas as pl
from jax.experimental.pallas import tpu as pltpu
from jax.sharding import PartitionSpec as P

D = 5120
QUERY_HEADS = 20
KEY_VALUE_HEADS = 4
GROUP = QUERY_HEADS // KEY_VALUE_HEADS
HEAD_SIZE = 128
BLOCK = 128
KPS = 2
STEPS = 2
QKV = 3584
GEN = 32
TP = 16
ROWS = 64
OWN = ROWS // TP
PLACES = 128

epsilon = 1e-06
rope_base = 1000000.0

bf16 = jnp.bfloat16
f32 = jnp.float32
i32 = jnp.int32
VMEM_BYTES = 48 * 1024 * 1024


def call(kernel, out_shape, *args, scalars=0, scratch=()):
    specs = [pl.BlockSpec(memory_space=pltpu.SMEM)] * scalars
    specs += [pl.BlockSpec(memory_space=pltpu.VMEM)] * (len(args) - scalars)
    return pl.pallas_call(
        kernel,
        out_shape=out_shape,
        in_specs=specs,
        out_specs=jax.tree.map(lambda _: pl.BlockSpec(memory_space=pltpu.VMEM), out_shape),
        scratch_shapes=list(scratch),
        compiler_params=pltpu.CompilerParams(vmem_limit_bytes=VMEM_BYTES),
    )(*args)


def shape(dims, dtype):
    return jax.ShapeDtypeStruct(dims, dtype)


def nt_dot(a, b):
    return lax.dot_general(a, b, (((1,), (1,)), ((), ())), preferred_element_type=f32)


def project_kernel(me_ref, x_ref, gain_ref, own_ref, other_ref, out_ref):
    me = me_ref[0]
    core = lax.rem(me, 2)
    wide = x_ref[...].astype(f32)
    scaled = (wide * gain_ref[...].astype(f32)).astype(bf16)
    for z in range(4):
        pieces = []
        for x in range(4):
            spot = jnp.bitwise_xor(z * 4 + x, me // 2)
            place = lax.rem(spot, 4) * 4 + spot // 4
            a = own_ref[place]
            b = other_ref[place]
            pieces.append(jnp.where(core == 0, a, b))
            pieces.append(jnp.where(core == 0, b, a))
        part = nt_dot(scaled, jnp.concatenate(pieces, axis=0))
        out_ref[:, z * 896 : (z + 1) * 896] = part.astype(bf16)
    squares = jnp.sum(wide * wide, axis=1, keepdims=True)
    high = squares.astype(bf16)
    low = (squares - high.astype(f32)).astype(bf16)
    lane = lax.broadcasted_iota(i32, (TP * 8, 128), 1)
    extra = jnp.where(lane == 0, high.astype(f32), jnp.where(lane == 1, low.astype(f32), 0.0))
    out_ref[:, QKV:] = extra.astype(bf16)


def attend_kernel(parts_ref, cache_ref, lengths_ref, cos_ref, sin_ref, mixed_ref, entry_ref):
    total = parts_ref[0].astype(f32)
    for t in range(1, TP):
        total = total + parts_ref[t].astype(f32)
    squares = total[:, QKV : QKV + 1] + total[:, QKV + 1 : QKV + 2]
    total = total[:, :QKV] * lax.rsqrt(squares / D + epsilon)
    cosine, sine = cos_ref[...], sin_ref[...]

    def head(index):
        return total[:, index * HEAD_SIZE : (index + 1) * HEAD_SIZE]

    def rotated(index):
        vec = head(index)
        swapped = jnp.concatenate([vec[:, HEAD_SIZE // 2 :], vec[:, : HEAD_SIZE // 2]], axis=1)
        return vec * cosine + swapped * sine

    rows = 8 * GROUP
    row = lax.rem(lax.broadcasted_iota(i32, (8, OWN * PLACES), 0), OWN)
    lane = lax.broadcasted_iota(i32, (8, OWN * PLACES), 1)
    old_ok = jnp.logical_and(lane // PLACES == row, lax.rem(lane, PLACES) < lengths_ref[:, :1])
    old_bias = jnp.tile(jnp.where(old_ok, 0.0, -jnp.inf), (GROUP, 1))
    slot = lax.broadcasted_iota(i32, (8, 8), 1)
    fresh = lax.broadcasted_iota(i32, (8, 8), 0)
    new_ok = jnp.logical_and(lax.rem(slot, OWN) == lax.rem(fresh, OWN), slot // OWN <= fresh // OWN)
    new_bias = jnp.tile(jnp.where(new_ok, 0.0, -jnp.inf), (GROUP, 1))
    scale = HEAD_SIZE ** (-0.5)
    width = KEY_VALUE_HEADS * HEAD_SIZE
    for k in range(KEY_VALUE_HEADS):
        at = k * HEAD_SIZE
        new_k = rotated(QUERY_HEADS + k).astype(bf16)
        new_v = head(QUERY_HEADS + KEY_VALUE_HEADS + k).astype(bf16)
        entry_ref[:, at : at + HEAD_SIZE] = new_k
        entry_ref[:, width + at : width + at + HEAD_SIZE] = new_v
        query = jnp.concatenate([rotated(k * GROUP + h) for h in range(GROUP)], axis=0).astype(bf16)
        old_k = cache_ref[:, :, at : at + HEAD_SIZE].reshape(OWN * PLACES, HEAD_SIZE)
        old_v = cache_ref[:, :, width + at : width + at + HEAD_SIZE].reshape(OWN * PLACES, HEAD_SIZE)
        old_s = nt_dot(query, old_k) * scale + old_bias
        new_s = nt_dot(query, new_k) * scale + new_bias
        peak = jnp.maximum(
            jnp.max(old_s, axis=1, keepdims=True), jnp.max(new_s, axis=1, keepdims=True)
        )
        old_e, new_e = jnp.exp(old_s - peak), jnp.exp(new_s - peak)
        whole = jnp.sum(old_e, axis=1, keepdims=True) + jnp.sum(new_e, axis=1, keepdims=True)
        old_w, new_w = (old_e / whole).astype(bf16), (new_e / whole).astype(bf16)
        mixed = jnp.dot(old_w, old_v, preferred_element_type=f32)
        mixed = mixed + jnp.dot(new_w, new_v, preferred_element_type=f32)
        for h in range(GROUP):
            to = (k * GROUP + h) * HEAD_SIZE
            mixed_ref[:, to : to + HEAD_SIZE] = mixed[8 * h : 8 * h + 8].astype(bf16)


def logits_kernel(me_ref, own_ref, other_ref, gain_ref, spot_ref, head_ref, out_ref, pairs_ref):
    me = me_ref[0]
    lane = lax.broadcasted_iota(i32, (256, 256), 1)
    for pair in range(GEN // 2):
        where = jnp.bitwise_xor(pair, me // 2)
        place = lax.rem(where, 4) * 4 + where // 4
        rows = jnp.concatenate([own_ref[place], other_ref[place]], axis=0)
        pick = (spot_ref[:, pair : pair + 1] == lane).astype(f32).astype(bf16)
        taken = jnp.dot(pick, rows, preferred_element_type=f32)
        for b in range(2 * TP):
            pairs_ref[b, 8 * pair : 8 * pair + 8, :] = taken[8 * b : 8 * b + 8]
    gain = gain_ref[...].astype(f32)
    column = lax.broadcasted_iota(i32, (128, 128), 1)
    squares = jnp.zeros((128, 128), f32)
    for t in range(TP):
        for j in range(2):
            raw = pairs_ref[2 * t + j]
            squares = jnp.where(
                column == 2 * t + j, jnp.sum(raw * raw, axis=1, keepdims=True), squares
            )
            part = jnp.dot(
                (raw * gain).astype(bf16),
                head_ref[t, :, j * BLOCK : (j + 1) * BLOCK],
                preferred_element_type=f32,
            )
            out_ref[t, j * 128 : (j + 1) * 128, :] = part.astype(bf16)
    squares = squares.T
    high = squares.astype(bf16).astype(f32)
    low = squares - high
    line = lax.broadcasted_iota(i32, (16, 128), 0)
    for t in range(TP):
        extra = jnp.zeros((16, 128), f32)
        for j in range(2):
            b = 2 * t + j
            extra = jnp.where(line == 2 * j, high[b : b + 1], extra)
            extra = jnp.where(line == 2 * j + 1, low[b : b + 1], extra)
        out_ref[t, 256:272, :] = extra.astype(bf16)


def stats_kernel(parts_ref, offset_ref, out_ref):
    total = parts_ref[0].astype(f32)
    for t in range(1, TP):
        total = total + parts_ref[t].astype(f32)
    token = lax.broadcasted_iota(i32, (BLOCK, 128), 0)
    line = lax.broadcasted_iota(i32, (8, 128), 0)
    out = jnp.zeros((8, 128), f32)
    for j in range(2):
        squares = total[256 + 2 * j : 257 + 2 * j] + total[257 + 2 * j : 258 + 2 * j]
        logits = total[j * 128 : (j + 1) * 128].T * lax.rsqrt(squares / D + epsilon)
        peak = jnp.max(logits, axis=0, keepdims=True)
        mass = jnp.sum(jnp.exp(logits - peak), axis=0, keepdims=True)
        hit = jnp.where(token == offset_ref[j : j + 1] - 1, logits, 0.0)
        picked = jnp.sum(hit, axis=0, keepdims=True)
        for at, value in enumerate((peak, mass, picked)):
            out = jnp.where(line == 3 * j + at, value, out)
    out_ref[...] = out


def rows_kernel(stats_ref, row_ref, out_ref):
    mine = lax.broadcasted_iota(i32, (ROWS, GEN), 0)
    lane = lax.broadcasted_iota(i32, (ROWS, 128), 1)
    out = jnp.zeros((ROWS, 128), f32)
    for s in range(STEPS):
        best = jnp.full((ROWS, 1), -jnp.inf, f32)
        combos = [(j, slot) for j in range(2) for slot in range(2)]
        masks = [row_ref[2 * j + slot : 2 * j + slot + 1, :] == mine for j, slot in combos]

        def stat(which, j, slot):
            at = (3 * j + which) * 4 + slot * 2 + s
            return stats_ref[at : at + 1, :]

        for mask, (j, slot) in zip(masks, combos):
            peak = jnp.where(mask, stat(0, j, slot), -jnp.inf)
            best = jnp.maximum(best, jnp.max(peak, axis=1, keepdims=True))
        mass = jnp.zeros((ROWS, 1), f32)
        picked = jnp.zeros((ROWS, 1), f32)
        for mask, (j, slot) in zip(masks, combos):
            grown = stat(1, j, slot) * jnp.exp(jnp.where(mask, stat(0, j, slot), best) - best)
            mass = mass + jnp.sum(jnp.where(mask, grown, 0.0), axis=1, keepdims=True)
            picked = picked + jnp.sum(
                jnp.where(mask, stat(2, j, slot), 0.0), axis=1, keepdims=True
            )
        for at, value in enumerate((best, mass, picked)):
            out = jnp.where(lane == 3 * s + at, value, out)
    out_ref[...] = out


def gen_index(z, x, core):
    return (z * 4 + x) * 2 + core


def exchange(value, axis, k):
    pairs = []
    for g in range(GEN):
        z, x, core = g // 8, g // 2 % 4, g % 2
        if axis == "z":
            z ^= k
        elif axis == "x":
            x ^= k
        else:
            core ^= k
        pairs.append((g, gen_index(z, x, core)))
    return lax.ppermute(value, "gen", pairs)


def gather_gen(piece):
    along_z = jnp.stack([piece] + [exchange(piece, "z", k) for k in range(1, 4)])
    along_x = jnp.stack([along_z] + [exchange(along_z, "x", k) for k in range(1, 4)])
    own = along_x.reshape((16,) + piece.shape)
    return own, exchange(own, "core", 1)


def all_to_all(value, axis):
    return lax.all_to_all(value, axis, split_axis=0, concat_axis=0, tiled=True)


def spread(value, axis, count):
    return all_to_all(jnp.broadcast_to(value[None], (count,) + value.shape), axis)


def rotary_tables(lengths):
    half = HEAD_SIZE // 2
    exponent = jnp.arange(half, dtype=f32) * (2.0 / HEAD_SIZE)
    inverse = jnp.power(f32(rope_base), -exponent)
    positions = (jnp.arange(STEPS, dtype=i32)[:, None] + lengths[None, :]).reshape(-1)
    angles = positions.astype(f32)[:, None] * inverse[None, :]
    cosine, sine = jnp.cos(angles), jnp.sin(angles)
    return (
        jnp.concatenate([cosine, cosine], axis=1),
        jnp.concatenate([-sine, sine], axis=1),
    )


def routing(kept, chosen, rank):
    row = jnp.arange(ROWS, dtype=i32)
    named = kept[:, :, None] == jnp.arange(ROWS, dtype=i32)
    match = jnp.any(named, axis=1)
    first = jnp.min(jnp.where(match, row[:, None], ROWS - 1), axis=0)
    last = jnp.max(jnp.where(match, row[:, None], 0), axis=0)
    entry = jnp.arange(KPS, dtype=i32)
    codes = chosen[:, :, None]
    here = (codes // (KPS * BLOCK) == rank) & (codes // BLOCK % KPS == entry)
    offset = jnp.where(here, codes % BLOCK + 1, 0)
    both = jnp.array([1, 256], i32)
    packed = jnp.sum(offset * both[:, None, None], axis=0)
    packed = jnp.sum(jnp.where(named, packed[:, :, None], 0), axis=1)
    rows_of = jnp.stack([first, last], axis=1)
    taken = jnp.where(row[:, None, None] == rows_of[None], packed[:, :, None], 0)
    return rows_of, rows_of + ROWS * jnp.sum(taken, axis=0)


def body(embeddings, cache, lengths, attn_gain, wqkv, wout, final_gain, head, kept, chosen):
    rank = lax.axis_index("tp")
    me = lax.axis_index("gen").astype(i32)
    me_ref = me.reshape(1)
    features = D // TP

    head_part = all_to_all(head.reshape(TP, features, 2 * BLOCK), "tp")
    own_w, other_w = gather_gen(wqkv.T)
    out_whole = lax.all_gather(wout, "gen", axis=0, tiled=True)

    rows_of, packed = routing(kept[0], chosen, rank)
    mine = all_to_all(packed.reshape(GEN, 1, 4), "gen").reshape(GEN, 4)
    routes = spread(mine.reshape(1, GEN * 4), "tp", TP).reshape(TP, GEN // 2, 2, 2, 2)
    row = jnp.bitwise_and(routes, ROWS - 1).transpose(0, 3, 2, 4, 1)
    side = jnp.bitwise_xor(jnp.arange(2, dtype=i32), jnp.bitwise_and(me, 1))
    spot = side[:, None, None] * 128 + row // OWN * 8 + row % OWN
    spot = spot[:, :, :, :, None, :] + jnp.arange(STEPS, dtype=i32)[:, None] * OWN
    spot = spot.reshape(256, GEN // 2)
    sampled = jnp.stack([mine // ROWS % 256, mine // (ROWS * 256)], axis=-1)
    offset = sampled.reshape(GEN, 2, 4).transpose(1, 0, 2).reshape(2, 128)

    x = embeddings.reshape(STEPS, TP, OWN, features).transpose(1, 0, 2, 3).reshape(128, features)
    parts = call(
        project_kernel,
        shape((128, QKV + 128), bf16),
        me_ref,
        x,
        attn_gain.reshape(1, features),
        own_w,
        other_w,
        scalars=1,
    )
    parts = all_to_all(parts.reshape(TP, 8, QKV + 128), "tp")
    cosine, sine = rotary_tables(lengths)
    wide_lengths = jnp.broadcast_to(jnp.tile(lengths, STEPS)[:, None], (8, 128))
    mixed, entries = call(
        attend_kernel,
        (shape((8, QUERY_HEADS * HEAD_SIZE), bf16), shape((8, 1024), bf16)),
        parts,
        cache,
        wide_lengths,
        cosine,
        sine,
    )
    mixed = spread(mixed, "tp", TP).reshape(128, QUERY_HEADS * HEAD_SIZE)
    layer_out = (
        x.astype(f32) + jnp.dot(mixed, out_whole, preferred_element_type=f32)
    ).astype(bf16)
    last_hidden = layer_out.reshape(TP, STEPS, OWN, features)[:, -1].reshape(ROWS, features)

    own_rows, other_rows = gather_gen(layer_out)
    gain = lax.dynamic_slice_in_dim(final_gain, rank * features, features, 0)
    logits = call(
        logits_kernel,
        shape((TP, 272, 128), bf16),
        me_ref,
        own_rows,
        other_rows,
        gain.reshape(1, features),
        spot,
        head_part,
        scalars=1,
        scratch=[pltpu.VMEM((2 * TP, 128, features), f32)],
    )
    logits = all_to_all(logits, "tp")
    stats = call(stats_kernel, shape((8, 128), f32), logits, offset)
    stats = stats.reshape(8, GEN, 4).transpose(1, 0, 2).reshape(GEN, 1, 32)
    stats = all_to_all(stats, "gen").reshape(GEN, 32).T
    row_stats = call(
        rows_kernel, shape((ROWS, 128), f32), stats, rows_of.reshape(GEN, 4).T
    )
    row_stats = all_to_all(row_stats.reshape(TP, OWN, 128)[:, :, :8], "tp")
    peak, mass, picked = (row_stats[:, :, i : 3 * STEPS : 3] for i in range(3))
    best = jnp.max(peak, axis=0)
    mass = jnp.sum(mass * jnp.exp(peak - best), axis=0)
    logprobs = jnp.sum(picked, axis=0) - best - jnp.log(mass)
    return logprobs.T, last_hidden, entries.reshape(STEPS, OWN, 1024)


def solution(mesh):
    return jax.shard_map(
        body,
        mesh=mesh,
        in_specs=(
            P(None, "gen", "tp"),
            P(("gen", "tp"), None, None),
            P(("gen", "tp")),
            P("tp"),
            P("tp", "gen"),
            P("gen", "tp"),
            P(),
            P(None, ("gen", "tp")),
            P("tp", "gen", None),
            P(None, "gen"),
        ),
        out_specs=(P(None, ("gen", "tp")), P("gen", "tp"), P(None, ("gen", "tp"), None)),
        check_vma=False,
    )
```

time: 911 us -> 405 us (0.44); the launches traced: 896 us -> 404 us
  blocking collectives: 256 us -> 21 us
  waiting for transfers between devices: 454 us -> 227 us
  local copies, waits for them, and re-layouts: 51.1 us -> 14.9 us
  starting transfers between devices: 85 us -> 111 us
  matrix products: 18.3 us -> 2.27 us
  other arithmetic: 16.9 us -> 3.81 us
    all_gather x4 -> x0, blocking collectives: 153 us -> none  [the longest x2 80.3 us: body(): lax.all_gather(layer_out, 'tp', axis=1, tiled=True).astype(jnp.float32)]
    unnamed x4 -> x1, waiting for transfers between devices: 118 us -> 0.68 us
    all_to_all x11 -> x7, waiting for transfers between devices: 200 us -> 84.6 us  [all_to_all(): return lax.all_to_all(value, axis, split_axis=0, concat_axis=0, tiled=True)]
    psum x2 -> x0, blocking collectives: 66.4 us -> none  [the longest x1 35.1 us: body(): row_squares = lax.psum(square_sum, 'tp')]
    ppermute x0 -> x14, starting transfers between devices: none -> 64.4 us  [exchange(): return lax.ppermute(value, 'gen', pairs)]
    ppermute x0 -> x14, waiting for transfers between devices: none -> 51.2 us  [exchange(): return lax.ppermute(value, 'gen', pairs)]
    all_gather x2 -> x1, waiting for transfers between devices: 136 us -> 90.9 us  [body(): out_whole = lax.all_gather(wout, 'gen', axis=0, tiled=True)]
    all_to_all x11 -> x7, starting transfers between devices: 84.9 us -> 46.8 us  [all_to_all(): return lax.all_to_all(value, axis, split_axis=0, concat_axis=0, tiled=True)]
  transfers between devices with their start and end apart: 14 -> 22, of which waited for: 13 -> 18; matrix products, arithmetic and copies ran while one was open for 7% -> 4% of each run, Pallas kernels for 0% -> 1%
where the time goes in v1:
time: 405 us; the launch traced here: 404 us
  waiting for transfers between devices  227 us (56%)
  starting transfers between devices  111 us (27%)
  blocking collectives  21 us (5%)
  local copies, waits for them, and re-layouts  14.9 us (4%)
  between operations  14.6 us (4%)
  Pallas kernels  8.58 us (2%)
    all_gather x1, waiting for transfers between devices, body(): out_whole = lax.all_gather(wout, 'gen', axis=0, tiled=True)  90.9 us
    all_to_all x7, waiting for transfers between devices, all_to_all(): return lax.all_to_all(value, axis, split_axis=0, concat_axis=0, tiled=True)  84.6 us
    ppermute x14, starting transfers between devices, exchange(): return lax.ppermute(value, 'gen', pairs)  64.4 us
    ppermute x14, waiting for transfers between devices, exchange(): return lax.ppermute(value, 'gen', pairs)  51.2 us
    all_to_all x7, starting transfers between devices, all_to_all(): return lax.all_to_all(value, axis, split_axis=0, concat_axis=0, tiled=True)  46.8 us
    all_to_all x1, blocking collectives, all_to_all(): return lax.all_to_all(value, axis, split_axis=0, concat_axis=0, tiled=True)  21 us
    pallas_call x5, Pallas kernels, call(): pl.pallas_call(kernel, out_shape=out_shape, in_specs=specs, out_specs=jax...  8.58 us
  transfers between devices with their start and end apart: 22, of which 18 were waited for; matrix products, arithmetic and copies ran while one was open for 4% of the time, Pallas kernels for 1%

profile of v1, /device:TPU:1, one launch (start us, length us, event | category | flops | bytes accessed | tf_op | source)
XLA Modules:
  0.0 403.8 jit_solution(5013728737543910736)
XLA Ops:
  7.2 9.6 %collective-permute-start = (bf16[112,320]{0,1:T(8,128)(2,1)}, bf16[112,320]{0,1:T(8,128)(2,1)S(1)}, u32[]{:S(2)}, u32[]{:S(2)}) collective-permute-start(bf16[112,320]{0,1:T(8,128)(2,1)} %bitcast.112), channel_id=1, source_target_pairs={{0,128},{16,144},{32,160},{48,176},{64,192},{80,208},{96,224},{112... | collective-permute-start | bytes 215048 | tf_op jit(solution)/shard_map/ppermute | solution.py:230
  16.8 10.6 %collective-permute-start.1 = (bf16[112,320]{0,1:T(8,128)(2,1)}, bf16[112,320]{0,1:T(8,128)(2,1)S(1)}, u32[]{:S(2)}, u32[]{:S(2)}) collective-permute-start(bf16[112,320]{0,1:T(8,128)(2,1)} %bitcast.113), channel_id=1, source_target_pairs={{0,256},{16,272},{32,288},{48,304},{64,320},{80,336},{96,352},{112... | collective-permute-start | bytes 215048 | tf_op jit(solution)/shard_map/ppermute | solution.py:230
  31.1 11.6 %collective-permute-done.2 = bf16[112,320]{0,1:T(8,128)(2,1)S(1)} collective-permute-done((bf16[112,320]{0,1:T(8,128)(2,1)}, bf16[112,320]{0,1:T(8,128)(2,1)S(1)}, u32[]{:S(2)}, u32[]{:S(2)}) %collective-permute-start.2) | collective-permute-done | bytes 71712 | tf_op jit(solution)/shard_map/ppermute | solution.py:230
  43.7 4.4 %collective-permute-start.5 = (bf16[4,112,320]{1,2,0:T(8,128)(2,1)S(1)}, bf16[4,112,320]{1,2,0:T(8,128)(2,1)S(1)}, u32[]{:S(2)}, u32[]{:S(2)}) collective-permute-start(bf16[4,112,320]{1,2,0:T(8,128)(2,1)S(1)} %get-tuple-element.24), channel_id=1, source_target_pairs={{0,96},{16,112},{32,64},{48,80},{64,32},{80,48},{96,0},{112,16},{1... | collective-permute-start | bytes 860168 | tf_op jit(solution)/shard_map/ppermute | solution.py:230
  50.0 3.3 collective-permute-start.4
  55.6 2.9 collective-permute-done.3
  58.4 6.9 %collective-permute-done.4 = bf16[4,112,320]{1,2,0:T(8,128)(2,1)S(1)} collective-permute-done((bf16[4,112,320]{1,2,0:T(8,128)(2,1)S(1)}, bf16[4,112,320]{1,2,0:T(8,128)(2,1)S(1)}, u32[]{:S(2)}, u32[]{:S(2)}) %collective-permute-start.4) | collective-permute-done | bytes 286752 | tf_op jit(solution)/shard_map/ppermute | solution.py:230
  65.7 3.6 collective-permute-start.6
  70.4 10.0 %all-to-all-start.2 = ((s32[32,1,4]{2,1,0:T(1,128)}), s32[32,1,4]{2,1,0:T(1,128)S(1)}, u32[]{:S(2)}, u32[]{:S(2)}) async-start(s32[32,1,4]{2,1,0:T(1,128)} %bitcast.28), calls=%async_computation.2 | async-start | bytes 32768 | tf_op jit(solution)/shard_map/all_to_all | solution.py:241
  85.3 9.3 %all-to-all-done.2 = s32[32,1,4]{2,1,0:T(1,128)S(1)} async-done(((s32[32,1,4]{2,1,0:T(1,128)}), s32[32,1,4]{2,1,0:T(1,128)S(1)}, u32[]{:S(2)}, u32[]{:S(2)}) %all-to-all-start.2) | async-done | bytes 544 | tf_op jit(solution)/shard_map/all_to_all | solution.py:241
  94.6 8.6 %all-to-all-start = ((bf16[16,8,3712]{2,1,0:T(8,128)(2,1)}), bf16[16,8,3712]{2,1,0:T(8,128)(2,1)S(1)}, u32[]{:S(2)}, u32[]{:S(2)}) async-start(bf16[16,8,3712]{2,1,0:T(8,128)(2,1)} %bitcast.95), calls=%async_computation | async-start | bytes 1900544 | tf_op jit(solution)/shard_map/all_to_all | solution.py:241
  104.9 23.3 %all-to-all-done.parts_ref = bf16[16,8,3712]{2,1,0:T(8,128)(2,1)S(1)} async-done(((bf16[16,8,3712]{2,1,0:T(8,128)(2,1)}), bf16[16,8,3712]{2,1,0:T(8,128)(2,1)S(1)}, u32[]{:S(2)}, u32[]{:S(2)}) %all-to-all-start) | async-done | bytes 950304 | tf_op jit(solution)/shard_map/all_to_all | solution.py:241
  128.7 4.3 %all-to-all-start.3 = ((s32[16,1,128]{2,1,0:T(1,128)}), s32[16,1,128]{2,1,0:T(1,128)S(1)}, u32[]{:S(2)}, u32[]{:S(2)}) async-start(s32[16,1,128]{2,1,0:T(1,128)} %broadcast_in_dim.110), calls=%async_computation.3 | async-start | bytes 16384 | tf_op jit(solution)/shard_map/all_to_all | solution.py:241
  135.0 4.7 %all-to-all-done.3 = s32[16,1,128]{2,1,0:T(1,128)S(1)} async-done(((s32[16,1,128]{2,1,0:T(1,128)}), s32[16,1,128]{2,1,0:T(1,128)S(1)}, u32[]{:S(2)}, u32[]{:S(2)}) %all-to-all-start.3) | async-done | bytes 8224 | tf_op jit(solution)/shard_map/all_to_all | solution.py:241
  139.7 21.0 %all_to_all.40 = bf16[16,8,2560]{2,1,0:T(8,128)(2,1)S(1)} all-to-all(bf16[16,8,2560]{2,1,0:T(8,128)(2,1)S(1)} %broadcast_in_dim.98), channel_id=1, replica_groups=mesh['gen'=32,'tp'=16] {'tp'}, dimensions={0} | all-to-all | bytes 1310720 | tf_op jit(solution)/shard_map/all_to_all | solution.py:241
  160.7 4.5 %all-to-all-start.4 = ((bf16[16,320,256]{2,1,0:T(8,128)(2,1)}), bf16[16,320,256]{2,1,0:T(8,128)(2,1)}, u32[]{:S(2)}, u32[]{:S(2)}) async-start(bf16[16,320,256]{2,1,0:T(8,128)(2,1)} %bitcast.100), calls=%async_computation.4 | async-start | bytes 5242880 | tf_op jit(solution)/shard_map/all_to_all | solution.py:241
  166.1 90.9 %all-gather.2.cloned.1.call-done = bf16[2560,320]{1,0:T(8,128)(2,1)} async-done(((bf16[80,320]{1,0:T(8,128)(2,1)}), bf16[2560,320]{1,0:T(8,128)(2,1)}) %all-gather.2.cloned.1.call-update) | async-done | bytes 1638416 | tf_op jit(solution)/shard_map/all_gather | solution.py:287
  259.2 5.8 %collective-permute-start.7 = (bf16[128,320]{0,1:T(8,128)(2,1)S(1)}, bf16[128,320]{0,1:T(8,128)(2,1)S(1)}, u32[]{:S(2)}, u32[]{:S(2)}) collective-permute-start(bf16[128,320]{0,1:T(8,128)(2,1)S(1)} %fusion), channel_id=1, source_target_pairs={{0,128},{16,144},{32,160},{48,176},{64,192},{80,208},{96,224},{112... | collective-permute-start | bytes 245768 | tf_op jit(solution)/shard_map/ppermute | solution.py:230
  265.0 6.5 %collective-permute-start.8 = (bf16[128,320]{0,1:T(8,128)(2,1)S(1)}, bf16[128,320]{0,1:T(8,128)(2,1)S(1)}, u32[]{:S(2)}, u32[]{:S(2)}) collective-permute-start(bf16[128,320]{0,1:T(8,128)(2,1)S(1)} %fusion), channel_id=1, source_target_pairs={{0,256},{16,272},{32,288},{48,304},{64,320},{80,336},{96,352},{112... | collective-permute-start | bytes 245768 | tf_op jit(solution)/shard_map/ppermute | solution.py:230
  271.5 3.9 collective-permute-start.9
  276.2 9.5 %collective-permute-done.8 = bf16[128,320]{0,1:T(8,128)(2,1)S(1)} collective-permute-done((bf16[128,320]{0,1:T(8,128)(2,1)S(1)}, bf16[128,320]{0,1:T(8,128)(2,1)S(1)}, u32[]{:S(2)}, u32[]{:S(2)}) %collective-permute-start.8) | collective-permute-done | bytes 81952 | tf_op jit(solution)/shard_map/ppermute | solution.py:230
  288.4 4.3 %collective-permute-start.11 = (bf16[4,128,320]{1,2,0:T(8,128)(2,1)S(1)}, bf16[4,128,320]{1,2,0:T(8,128)(2,1)S(1)}, u32[]{:S(2)}, u32[]{:S(2)}) collective-permute-start(bf16[4,128,320]{1,2,0:T(8,128)(2,1)S(1)} %get-tuple-element.22), channel_id=1, source_target_pairs={{0,64},{16,80},{32,96},{48,112},{64,0},{80,16},{96,32},{112,48},{1... | collective-permute-start | bytes 983048 | tf_op jit(solution)/shard_map/ppermute | solution.py:230
  296.1 8.7 %collective-permute-done.11 = bf16[4,128,320]{1,2,0:T(8,128)(2,1)S(1)} collective-permute-done((bf16[4,128,320]{1,2,0:T(8,128)(2,1)S(1)}, bf16[4,128,320]{1,2,0:T(8,128)(2,1)S(1)}, u32[]{:S(2)}, u32[]{:S(2)}) %collective-permute-start.11) | collective-permute-done | bytes 327712 | tf_op jit(solution)/shard_map/ppermute | solution.py:230
  304.8 6.4 %collective-permute-done.12 = bf16[4,128,320]{1,2,0:T(8,128)(2,1)S(1)} collective-permute-done((bf16[4,128,320]{1,2,0:T(8,128)(2,1)S(1)}, bf16[4,128,320]{1,2,0:T(8,128)(2,1)S(1)}, u32[]{:S(2)}, u32[]{:S(2)}) %collective-permute-start.12) | collective-permute-done | bytes 327712 | tf_op jit(solution)/shard_map/ppermute | solution.py:230
  311.4 3.3 collective-permute-start.13
  319.3 4.5 %shard_map.132 = bf16[16,272,128]{2,1,0:T(8,128)(2,1)S(1)} custom-call(s32[1]{0:T(128)} %bitcast.me_ref, bf16[16,128,320]{2,1,0:T(8,128)(2,1)S(1)} %bitcast.93, bf16[16,128,320]{2,1,0:T(8,128)(2,1)S(1)} %copy.125.other_ref, bf16[1,320]{1,0:T(2,128)(2,1)S(1)} %reshape.347.gain_ref, s32[256,16]{1,0:T(8,128)S(1)} %broadcast_add_fusion.spot_ref, ...), custom_call_target="tpu_custom_call" | custom-call | tf_op jit(solution)/shard_map/pallas_call | solution.py:35
  324.8 8.9 %all-to-all-start.5 = ((bf16[16,272,128]{2,1,0:T(8,128)(2,1)}), bf16[16,272,128]{2,1,0:T(8,128)(2,1)S(1)}, u32[]{:S(2)}, u32[]{:S(2)}) async-start(bf16[16,272,128]{2,1,0:T(8,128)(2,1)} %copy-done), calls=%async_computation.5 | async-start | bytes 2228224 | tf_op jit(solution)/shard_map/all_to_all | solution.py:241
  334.1 28.1 %all-to-all-done.5.parts_ref = bf16[16,272,128]{2,1,0:T(8,128)(2,1)S(1)} async-done(((bf16[16,272,128]{2,1,0:T(8,128)(2,1)}), bf16[16,272,128]{2,1,0:T(8,128)(2,1)S(1)}, u32[]{:S(2)}, u32[]{:S(2)}) %all-to-all-start.5) | async-done | bytes 1114144 | tf_op jit(solution)/shard_map/all_to_all | solution.py:241
  363.3 7.0 %all-to-all-start.6 = ((f32[32,1,32]{2,1,0:T(1,128)}), f32[32,1,32]{2,1,0:T(1,128)S(1)}, u32[]{:S(2)}, u32[]{:S(2)}) async-start(f32[32,1,32]{2,1,0:T(1,128)} %copy.131), calls=%async_computation.6 | async-start | bytes 32768 | tf_op jit(solution)/shard_map/all_to_all | solution.py:241
  370.6 13.9 %all-to-all-done.6 = f32[32,1,32]{2,1,0:T(1,128)S(1)} async-done(((f32[32,1,32]{2,1,0:T(1,128)}), f32[32,1,32]{2,1,0:T(1,128)S(1)}, u32[]{:S(2)}, u32[]{:S(2)}) %all-to-all-start.6) | async-done | bytes 4128 | tf_op jit(solution)/shard_map/all_to_all | solution.py:241
  385.5 3.5 all-to-all-start.7
  390.5 5.3 %all-to-all-done.7 = f32[16,4,8]{2,1,0:T(4,128)S(1)} async-done(((f32[16,4,8]{2,1,0:T(4,128)}), f32[16,4,8]{2,1,0:T(4,128)S(1)}, u32[]{:S(2)}, u32[]{:S(2)}) %all-to-all-start.7) | async-done | bytes 2080 | tf_op jit(solution)/shard_map/all_to_all | solution.py:241
  (115 shorter events, 40.1 us)
Async XLA Ops:
  7.2 22.2 %collective-permute-start = (bf16[112,320]{0,1:T(8,128)(2,1)}, bf16[112,320]{0,1:T(8,128)(2,1)S(1)}, u32[]{:S(2)}, u32[]{:S(2)}) collective-permute-start(bf16[112,320]{0,1:T(8,128)(2,1)} %bitcast.112), channel_id=1, source_target_pairs={{0,128},{16,144},{32,160},{48,176},{64,192},{80,208},{96,224},{112... | collective-permute-start | bytes 215048 | tf_op jit(solution)/shard_map/ppermute | solution.py:230
  16.8 14.2 %collective-permute-start.1 = (bf16[112,320]{0,1:T(8,128)(2,1)}, bf16[112,320]{0,1:T(8,128)(2,1)S(1)}, u32[]{:S(2)}, u32[]{:S(2)}) collective-permute-start(bf16[112,320]{0,1:T(8,128)(2,1)} %bitcast.113), channel_id=1, source_target_pairs={{0,256},{16,272},{32,288},{48,304},{64,320},{80,336},{96,352},{112... | collective-permute-start | bytes 215048 | tf_op jit(solution)/shard_map/ppermute | solution.py:230
  27.5 15.2 %collective-permute-start.2 = (bf16[112,320]{0,1:T(8,128)(2,1)}, bf16[112,320]{0,1:T(8,128)(2,1)S(1)}, u32[]{:S(2)}, u32[]{:S(2)}) collective-permute-start(bf16[112,320]{0,1:T(8,128)(2,1)} %bitcast.114), channel_id=1, source_target_pairs={{0,384},{16,400},{32,416},{48,432},{64,448},{80,464},{96,480},{112... | collective-permute-start | bytes 215048 | tf_op jit(solution)/shard_map/ppermute | solution.py:230
  43.7 11.9 %collective-permute-start.5 = (bf16[4,112,320]{1,2,0:T(8,128)(2,1)S(1)}, bf16[4,112,320]{1,2,0:T(8,128)(2,1)S(1)}, u32[]{:S(2)}, u32[]{:S(2)}) collective-permute-start(bf16[4,112,320]{1,2,0:T(8,128)(2,1)S(1)} %get-tuple-element.24), channel_id=1, source_target_pairs={{0,96},{16,112},{32,64},{48,80},{64,32},{80,48},{96,0},{112,16},{1... | collective-permute-start | bytes 860168 | tf_op jit(solution)/shard_map/ppermute | solution.py:230
  48.1 10.4 %collective-permute-start.3 = (bf16[4,112,320]{1,2,0:T(8,128)(2,1)S(1)}, bf16[4,112,320]{1,2,0:T(8,128)(2,1)S(1)}, u32[]{:S(2)}, u32[]{:S(2)}) collective-permute-start(bf16[4,112,320]{1,2,0:T(8,128)(2,1)S(1)} %get-tuple-element.24), channel_id=1, source_target_pairs={{0,32},{16,48},{32,0},{48,16},{64,96},{80,112},{96,64},{112,80},{1... | collective-permute-start | bytes 860168 | tf_op jit(solution)/shard_map/ppermute | solution.py:230
  50.0 15.4 %collective-permute-start.4 = (bf16[4,112,320]{1,2,0:T(8,128)(2,1)S(1)}, bf16[4,112,320]{1,2,0:T(8,128)(2,1)S(1)}, u32[]{:S(2)}, u32[]{:S(2)}) collective-permute-start(bf16[4,112,320]{1,2,0:T(8,128)(2,1)S(1)} %get-tuple-element.24), channel_id=1, source_target_pairs={{0,64},{16,80},{32,96},{48,112},{64,0},{80,16},{96,32},{112,48},{1... | collective-permute-start | bytes 860168 | tf_op jit(solution)/shard_map/ppermute | solution.py:230
  65.4 4.0 copy-start.5
  65.4 4.1 %copy-start.7 = (s32[2]{0:T(128)S(1)}, s32[2]{0:T(128)}, u32[]{:S(2)}) copy-start(s32[2]{0:T(128)} %constant.148.clone) | copy-start | bytes 28
  65.4 4.1 %copy-start.4 = (s32[1,64,2]{1,2,0:T(2,128)S(1)}, s32[1,64,2]{1,2,0:T(2,128)}, u32[]{:S(2)}) copy-start(s32[1,64,2]{1,2,0:T(2,128)} %param.19) | copy-start | bytes 1540
  65.4 15.1 %copy-start.3 = (bf16[2,64,320]{2,1,0:T(8,128)(2,1)S(1)}, bf16[2,64,320]{2,1,0:T(8,128)(2,1)}, u32[]{:S(2)}) copy-start(bf16[2,64,320]{2,1,0:T(8,128)(2,1)} %param.11) | copy-start | bytes 245764
  65.4 15.3 %copy-start.6 = (bf16[320]{0:T(512)(128)(2,1)S(1)}, bf16[320]{0:T(512)(128)(2,1)}, u32[]{:S(2)}) copy-start(bf16[320]{0:T(512)(128)(2,1)} %param.14) | copy-start | bytes 1924
  65.7 15.7 %collective-permute-start.6 = (bf16[16,112,320]{1,2,0:T(8,128)(2,1)S(1)}, bf16[16,112,320]{1,2,0:T(8,128)(2,1)}, u32[]{:S(2)}, u32[]{:S(2)}) collective-permute-start(bf16[16,112,320]{1,2,0:T(8,128)(2,1)S(1)} %bitcast.98), channel_id=1, source_target_pairs={{0,16},{16,0},{32,48},{48,32},{64,80},{80,64},{96,112},{112,96},{1... | collective-permute-start | bytes 3440648 | tf_op jit(solution)/shard_map/ppermute | solution.py:230
  70.4 24.1 %all-to-all-start.2 = ((s32[32,1,4]{2,1,0:T(1,128)}), s32[32,1,4]{2,1,0:T(1,128)S(1)}, u32[]{:S(2)}, u32[]{:S(2)}) async-start(s32[32,1,4]{2,1,0:T(1,128)} %bitcast.28), calls=%async_computation.2 | async-start | bytes 32768 | tf_op jit(solution)/shard_map/all_to_all | solution.py:241
  84.3 0.9 copy-start.1
  85.3 18.0 %copy-start.8 = (s32[4]{0:T(128)S(1)}, s32[4]{0:T(128)}, u32[]{:S(2)}) copy-start(s32[4]{0:T(128)} %param.13) | copy-start | bytes 52
  85.3 47.9 %copy-start.2 = (bf16[4,128,1024]{2,1,0:T(8,128)(2,1)S(1)}, bf16[4,128,1024]{2,1,0:T(8,128)(2,1)}, u32[]{:S(2)}) copy-start(bf16[4,128,1024]{2,1,0:T(8,128)(2,1)} %cache_ref.1) | copy-start | bytes 3145732
  94.6 33.5 %all-to-all-start = ((bf16[16,8,3712]{2,1,0:T(8,128)(2,1)}), bf16[16,8,3712]{2,1,0:T(8,128)(2,1)S(1)}, u32[]{:S(2)}, u32[]{:S(2)}) async-start(bf16[16,8,3712]{2,1,0:T(8,128)(2,1)} %bitcast.95), calls=%async_computation | async-start | bytes 1900544 | tf_op jit(solution)/shard_map/all_to_all | solution.py:241
  128.7 10.9 %all-to-all-start.3 = ((s32[16,1,128]{2,1,0:T(1,128)}), s32[16,1,128]{2,1,0:T(1,128)S(1)}, u32[]{:S(2)}, u32[]{:S(2)}) async-start(s32[16,1,128]{2,1,0:T(1,128)} %broadcast_in_dim.110), calls=%async_computation.3 | async-start | bytes 16384 | tf_op jit(solution)/shard_map/all_to_all | solution.py:241
  160.7 158.6 %all-to-all-start.4 = ((bf16[16,320,256]{2,1,0:T(8,128)(2,1)}), bf16[16,320,256]{2,1,0:T(8,128)(2,1)}, u32[]{:S(2)}, u32[]{:S(2)}) async-start(bf16[16,320,256]{2,1,0:T(8,128)(2,1)} %bitcast.100), calls=%async_computation.4 | async-start | bytes 5242880 | tf_op jit(solution)/shard_map/all_to_all | solution.py:241
  165.2 91.8 %all-gather.2.cloned.1.call-start = ((), (), s32[]{:S(2)}) async-start(), calls=%async_computation.8 | async-start | bytes 2027520 | tf_op jit(solution)/shard_map/all_gather | solution.py:287
  259.2 17.0 %collective-permute-start.7 = (bf16[128,320]{0,1:T(8,128)(2,1)S(1)}, bf16[128,320]{0,1:T(8,128)(2,1)S(1)}, u32[]{:S(2)}, u32[]{:S(2)}) collective-permute-start(bf16[128,320]{0,1:T(8,128)(2,1)S(1)} %fusion), channel_id=1, source_target_pairs={{0,128},{16,144},{32,160},{48,176},{64,192},{80,208},{96,224},{112... | collective-permute-start | bytes 245768 | tf_op jit(solution)/shard_map/ppermute | solution.py:230
  265.0 20.7 %collective-permute-start.8 = (bf16[128,320]{0,1:T(8,128)(2,1)S(1)}, bf16[128,320]{0,1:T(8,128)(2,1)S(1)}, u32[]{:S(2)}, u32[]{:S(2)}) collective-permute-start(bf16[128,320]{0,1:T(8,128)(2,1)S(1)} %fusion), channel_id=1, source_target_pairs={{0,256},{16,272},{32,288},{48,304},{64,320},{80,336},{96,352},{112... | collective-permute-start | bytes 245768 | tf_op jit(solution)/shard_map/ppermute | solution.py:230
  271.5 14.2 %collective-permute-start.9 = (bf16[128,320]{0,1:T(8,128)(2,1)S(1)}, bf16[128,320]{0,1:T(8,128)(2,1)S(1)}, u32[]{:S(2)}, u32[]{:S(2)}) collective-permute-start(bf16[128,320]{0,1:T(8,128)(2,1)S(1)} %fusion), channel_id=1, source_target_pairs={{0,384},{16,400},{32,416},{48,432},{64,448},{80,464},{96,480},{112... | collective-permute-start | bytes 245768 | tf_op jit(solution)/shard_map/ppermute | solution.py:230
  285.7 10.4 %collective-permute-start.10 = (bf16[4,128,320]{1,2,0:T(8,128)(2,1)S(1)}, bf16[4,128,320]{1,2,0:T(8,128)(2,1)S(1)}, u32[]{:S(2)}, u32[]{:S(2)}) collective-permute-start(bf16[4,128,320]{1,2,0:T(8,128)(2,1)S(1)} %get-tuple-element.22), channel_id=1, source_target_pairs={{0,32},{16,48},{32,0},{48,16},{64,96},{80,112},{96,64},{112,80},{1... | collective-permute-start | bytes 983048 | tf_op jit(solution)/shard_map/ppermute | solution.py:230
  288.4 16.4 %collective-permute-start.11 = (bf16[4,128,320]{1,2,0:T(8,128)(2,1)S(1)}, bf16[4,128,320]{1,2,0:T(8,128)(2,1)S(1)}, u32[]{:S(2)}, u32[]{:S(2)}) collective-permute-start(bf16[4,128,320]{1,2,0:T(8,128)(2,1)S(1)} %get-tuple-element.22), channel_id=1, source_target_pairs={{0,64},{16,80},{32,96},{48,112},{64,0},{80,16},{96,32},{112,48},{1... | collective-permute-start | bytes 983048 | tf_op jit(solution)/shard_map/ppermute | solution.py:230
  292.7 18.5 %collective-permute-start.12 = (bf16[4,128,320]{1,2,0:T(8,128)(2,1)S(1)}, bf16[4,128,320]{1,2,0:T(8,128)(2,1)S(1)}, u32[]{:S(2)}, u32[]{:S(2)}) collective-permute-start(bf16[4,128,320]{1,2,0:T(8,128)(2,1)S(1)} %get-tuple-element.22), channel_id=1, source_target_pairs={{0,96},{16,112},{32,64},{48,80},{64,32},{80,48},{96,0},{112,16},{1... | collective-permute-start | bytes 983048 | tf_op jit(solution)/shard_map/ppermute | solution.py:230
  311.4 6.1 %collective-permute-start.13 = (bf16[16,128,320]{1,2,0:T(8,128)(2,1)S(1)}, bf16[16,128,320]{1,2,0:T(8,128)(2,1)}, u32[]{:S(2)}, u32[]{:S(2)}) collective-permute-start(bf16[16,128,320]{1,2,0:T(8,128)(2,1)S(1)} %bitcast.99), channel_id=1, source_target_pairs={{0,16},{16,0},{32,48},{48,32},{64,80},{80,64},{96,112},{112,96},{1... | collective-permute-start | bytes 3932168 | tf_op jit(solution)/shard_map/ppermute | solution.py:230
  323.8 1.0 copy-start
  324.8 37.4 %all-to-all-start.5 = ((bf16[16,272,128]{2,1,0:T(8,128)(2,1)}), bf16[16,272,128]{2,1,0:T(8,128)(2,1)S(1)}, u32[]{:S(2)}, u32[]{:S(2)}) async-start(bf16[16,272,128]{2,1,0:T(8,128)(2,1)} %copy-done), calls=%async_computation.5 | async-start | bytes 2228224 | tf_op jit(solution)/shard_map/all_to_all | solution.py:241
  363.3 21.1 %all-to-all-start.6 = ((f32[32,1,32]{2,1,0:T(1,128)}), f32[32,1,32]{2,1,0:T(1,128)S(1)}, u32[]{:S(2)}, u32[]{:S(2)}) async-start(f32[32,1,32]{2,1,0:T(1,128)} %copy.131), calls=%async_computation.6 | async-start | bytes 32768 | tf_op jit(solution)/shard_map/all_to_all | solution.py:241
  385.5 10.3 %all-to-all-start.7 = ((f32[16,4,8]{2,1,0:T(4,128)}), f32[16,4,8]{2,1,0:T(4,128)S(1)}, u32[]{:S(2)}, u32[]{:S(2)}) async-start(f32[16,4,8]{2,1,0:T(4,128)} %bitcast.92), calls=%async_computation.7 | async-start | bytes 65536 | tf_op jit(solution)/shard_map/all_to_all | solution.py:241
Sparse Core Ops, SparseCore 0:
  169.2 87.6 all-gather.1

commit v2 on v1

--- a/solution.py
+++ b/solution.py
@@ -50,28 +50,97 @@
     return lax.dot_general(a, b, (((1,), (1,)), ((), ())), preferred_element_type=f32)
 
 
-def project_kernel(me_ref, x_ref, gain_ref, own_ref, other_ref, out_ref):
+def swap_halves(value):
+    return jnp.concatenate([value[:, 64:], value[:, :64]], axis=1)
+
+
+def unpack(piece, rows):
+    tail = piece[2 * rows :]
+    other = swap_halves(tail.astype(f32)).astype(bf16)
+    tail = jnp.concatenate([tail, other[: rows - 64]], axis=0)
+    return jnp.concatenate([piece[:rows], piece[rows : 2 * rows], tail], axis=1)
+
+
+def pack_kernel(rank_ref, weights_ref, table_ref, out_ref):
+    turned = weights_ref[...].astype(f32).T
+    out_ref[0:112, :] = turned[:, 0:128].astype(bf16)
+    out_ref[112:224, :] = turned[:, 128:256].astype(bf16)
+    block = lax.broadcasted_iota(i32, (ROWS, ROWS), 1)
+    row = lax.broadcasted_iota(i32, (ROWS, ROWS), 0)
+    named = [table_ref[:, k : k + 1] == block for k in range(KPS)]
+    match = jnp.logical_or(named[0], named[1])
+    first = jnp.min(jnp.where(match, row, ROWS - 1), axis=0, keepdims=True)
+    last = jnp.max(jnp.where(match, row, 0), axis=0, keepdims=True)
+    line = lax.broadcasted_iota(i32, (16, ROWS), 0)
+    meta = jnp.where(line == 0, first, jnp.where(line == 1, last, 0))
+    for s in range(STEPS):
+        code = table_ref[:, KPS + s : KPS + s + 1]
+        offset = jnp.zeros((ROWS, ROWS), i32)
+        for k in range(KPS):
+            here = jnp.logical_and(code // BLOCK == rank_ref[0] * KPS + k, named[k])
+            offset = jnp.where(here, lax.rem(code, BLOCK) + 1, offset)
+        for slot, target in enumerate((first, last)):
+            value = jnp.sum(jnp.where(row == target, offset, 0), axis=0, keepdims=True)
+            meta = jnp.where(line == 2 + 2 * s + slot, value, meta)
+    side = jnp.concatenate([turned[64:112, 256:320], meta.astype(f32)], axis=0)
+    out_ref[224:288, :] = jnp.concatenate([turned[0:64, 256:320], side], axis=1).astype(bf16)
+
+
+def project_kernel(me_ref, x_ref, gain_ref, pieces_ref, out_ref, meta_ref):
     me = me_ref[0]
-    core = lax.rem(me, 2)
     wide = x_ref[...].astype(f32)
     scaled = (wide * gain_ref[...].astype(f32)).astype(bf16)
+    scaled = jnp.concatenate([scaled, jnp.zeros((128, 64), bf16)], axis=1)
+    lane = lax.broadcasted_iota(i32, (16, 128), 1)
+    metas = [jnp.zeros((16, 128), f32), jnp.zeros((16, 128), f32)]
+    for z in range(4):
+        pieces = []
+        for g in range(8 * z, 8 * z + 8):
+            piece = pieces_ref[g]
+            pieces.append(unpack(piece, 112))
+            table = piece[272:288].astype(f32)
+            for j in range(2):
+                mine = jnp.where(lane == 64 + 2 * me + j, table, 0.0)
+                column = jnp.sum(mine, axis=1, keepdims=True)
+                metas[j] = jnp.where(lane == 32 + g, column, metas[j])
+        part = nt_dot(scaled, jnp.concatenate(pieces, axis=0))
+        out_ref[:, z * 896 : (z + 1) * 896] = part.astype(bf16)
+    for j in range(2):
+        meta_ref[16 * j : 16 * j + 16, :] = metas[j]
+    squares = jnp.sum(wide * wide, axis=1, keepdims=True)
+    high = squares.astype(bf16).astype(f32)
+    low = squares - high
+    line = lax.rem(lax.broadcasted_iota(i32, (TP * 8, 128), 0), 8)
+    lane = lax.broadcasted_iota(i32, (TP * 8, 128), 1)
+    extra = jnp.zeros((TP * 8, 128), f32)
+    for j in range(2):
+        for slot in range(2):
+            extra = jnp.where(line == 2 * j + slot, metas[j][slot : slot + 1], extra)
+    extra = jnp.where(lane == 0, high, jnp.where(lane == 1, low, extra))
+    out_ref[:, QKV:] = extra.astype(bf16)
+
+
+def output_kernel(me_ref, mixed_ref, own_ref, other_ref, x_ref, rows_ref, packed_ref):
+    core = lax.rem(me_ref[0], 2)
+    total = x_ref[...].astype(f32)
     for z in range(4):
         pieces = []
         for x in range(4):
-            spot = jnp.bitwise_xor(z * 4 + x, me // 2)
-            place = lax.rem(spot, 4) * 4 + spot // 4
-            a = own_ref[place]
-            b = other_ref[place]
-            pieces.append(jnp.where(core == 0, a, b))
-            pieces.append(jnp.where(core == 0, b, a))
-        part = nt_dot(scaled, jnp.concatenate(pieces, axis=0))
-        out_ref[:, z * 896 : (z + 1) * 896] = part.astype(bf16)
-    squares = jnp.sum(wide * wide, axis=1, keepdims=True)
-    high = squares.astype(bf16)
-    low = (squares - high.astype(f32)).astype(bf16)
-    lane = lax.broadcasted_iota(i32, (TP * 8, 128), 1)
-    extra = jnp.where(lane == 0, high.astype(f32), jnp.where(lane == 1, low.astype(f32), 0.0))
-    out_ref[:, QKV:] = extra.astype(bf16)
+            a = own_ref[x * 4 + z]
+            b = other_ref[x * 4 + z]
+            pieces += [jnp.where(core == 0, a, b), jnp.where(core == 0, b, a)]
+        depth = 8 * pieces[0].shape[0]
+        total = total + jnp.dot(
+            mixed_ref[:, z * depth : (z + 1) * depth],
+            jnp.concatenate(pieces, axis=0),
+            preferred_element_type=f32,
+        )
+    rows = total.astype(bf16)
+    rows_ref[...] = rows
+    packed_ref[0:128, :] = rows[:, 0:128]
+    packed_ref[128:256, :] = rows[:, 128:256]
+    tail = rows[:, 256:320].astype(f32)
+    packed_ref[256:320, :] = jnp.concatenate([tail[0:64], tail[64:128]], axis=1).astype(bf16)
 
 
 def attend_kernel(parts_ref, cache_ref, lengths_ref, cos_ref, sin_ref, mixed_ref, entry_ref):
@@ -125,17 +194,16 @@
             mixed_ref[:, to : to + HEAD_SIZE] = mixed[8 * h : 8 * h + 8].astype(bf16)
 
 
-def logits_kernel(me_ref, own_ref, other_ref, gain_ref, spot_ref, head_ref, out_ref, pairs_ref):
-    me = me_ref[0]
+def logits_kernel(own_ref, other_ref, gain_ref, spot_ref, head_ref, out_ref, pairs_ref):
     lane = lax.broadcasted_iota(i32, (256, 256), 1)
+    features = gain_ref.shape[1]
     for pair in range(GEN // 2):
-        where = jnp.bitwise_xor(pair, me // 2)
-        place = lax.rem(where, 4) * 4 + where // 4
-        rows = jnp.concatenate([own_ref[place], other_ref[place]], axis=0)
+        place = pair % 4 * 4 + pair // 4
+        rows = [unpack(ref[place], 128) for ref in (own_ref, other_ref)]
         pick = (spot_ref[:, pair : pair + 1] == lane).astype(f32).astype(bf16)
-        taken = jnp.dot(pick, rows, preferred_element_type=f32)
+        taken = jnp.dot(pick, jnp.concatenate(rows, axis=0), preferred_element_type=f32)
         for b in range(2 * TP):
-            pairs_ref[b, 8 * pair : 8 * pair + 8, :] = taken[8 * b : 8 * b + 8]
+            pairs_ref[b, 8 * pair : 8 * pair + 8, :] = taken[8 * b : 8 * b + 8, :features]
     gain = gain_ref[...].astype(f32)
     column = lax.broadcasted_iota(i32, (128, 128), 1)
     squares = jnp.zeros((128, 128), f32)
@@ -216,33 +284,25 @@
     return (z * 4 + x) * 2 + core
 
 
-def exchange(value, axis, k):
-    pairs = []
-    for g in range(GEN):
-        z, x, core = g // 8, g // 2 % 4, g % 2
-        if axis == "z":
-            z ^= k
-        elif axis == "x":
-            x ^= k
-        else:
-            core ^= k
-        pairs.append((g, gen_index(z, x, core)))
-    return lax.ppermute(value, "gen", pairs)
+Z_GROUPS = [[gen_index(z, x, c) for z in range(4)] for x in range(4) for c in range(2)]
+X_GROUPS = [[gen_index(z, x, c) for x in range(4)] for z in range(4) for c in range(2)]
 
 
 def gather_gen(piece):
-    along_z = jnp.stack([piece] + [exchange(piece, "z", k) for k in range(1, 4)])
-    along_x = jnp.stack([along_z] + [exchange(along_z, "x", k) for k in range(1, 4)])
+    along_z = spread(piece, "gen", 4, Z_GROUPS)
+    along_x = spread(along_z, "gen", 4, X_GROUPS)
     own = along_x.reshape((16,) + piece.shape)
-    return own, exchange(own, "core", 1)
-
-
-def all_to_all(value, axis):
-    return lax.all_to_all(value, axis, split_axis=0, concat_axis=0, tiled=True)
-
-
-def spread(value, axis, count):
-    return all_to_all(jnp.broadcast_to(value[None], (count,) + value.shape), axis)
+    return own, lax.ppermute(own, "gen", [(g, g ^ 1) for g in range(GEN)])
+
+
+def all_to_all(value, axis, groups=None):
+    return lax.all_to_all(
+        value, axis, split_axis=0, concat_axis=0, tiled=True, axis_index_groups=groups
+    )
+
+
+def spread(value, axis, count, groups=None):
+    return all_to_all(jnp.broadcast_to(value[None], (count,) + value.shape), axis, groups)
 
 
 def rotary_tables(lengths):
@@ -258,57 +318,50 @@
     )
 
 
-def routing(kept, chosen, rank):
-    row = jnp.arange(ROWS, dtype=i32)
-    named = kept[:, :, None] == jnp.arange(ROWS, dtype=i32)
-    match = jnp.any(named, axis=1)
-    first = jnp.min(jnp.where(match, row[:, None], ROWS - 1), axis=0)
-    last = jnp.max(jnp.where(match, row[:, None], 0), axis=0)
-    entry = jnp.arange(KPS, dtype=i32)
-    codes = chosen[:, :, None]
-    here = (codes // (KPS * BLOCK) == rank) & (codes // BLOCK % KPS == entry)
-    offset = jnp.where(here, codes % BLOCK + 1, 0)
-    both = jnp.array([1, 256], i32)
-    packed = jnp.sum(offset * both[:, None, None], axis=0)
-    packed = jnp.sum(jnp.where(named, packed[:, :, None], 0), axis=1)
-    rows_of = jnp.stack([first, last], axis=1)
-    taken = jnp.where(row[:, None, None] == rows_of[None], packed[:, :, None], 0)
-    return rows_of, rows_of + ROWS * jnp.sum(taken, axis=0)
+def row_table(kept):
+    row = jnp.arange(ROWS, dtype=i32)[:, None]
+    match = jnp.any(kept[:, :, None] == jnp.arange(ROWS, dtype=i32), axis=1)
+    first = jnp.min(jnp.where(match, row, ROWS - 1), axis=0)
+    last = jnp.max(jnp.where(match, row, 0), axis=0)
+    return jnp.stack([first, last], axis=1)
 
 
 def body(embeddings, cache, lengths, attn_gain, wqkv, wout, final_gain, head, kept, chosen):
-    rank = lax.axis_index("tp")
+    rank = lax.axis_index("tp").astype(i32)
     me = lax.axis_index("gen").astype(i32)
-    me_ref = me.reshape(1)
     features = D // TP
 
+    table = jnp.concatenate([kept[0], chosen.T], axis=1)
+    piece = call(
+        pack_kernel, shape((288, 128), bf16), rank.reshape(1), wqkv, table, scalars=1
+    )
+    pieces = lax.all_gather(piece, "gen")
     head_part = all_to_all(head.reshape(TP, features, 2 * BLOCK), "tp")
-    own_w, other_w = gather_gen(wqkv.T)
-    out_whole = lax.all_gather(wout, "gen", axis=0, tiled=True)
-
-    rows_of, packed = routing(kept[0], chosen, rank)
-    mine = all_to_all(packed.reshape(GEN, 1, 4), "gen").reshape(GEN, 4)
-    routes = spread(mine.reshape(1, GEN * 4), "tp", TP).reshape(TP, GEN // 2, 2, 2, 2)
-    row = jnp.bitwise_and(routes, ROWS - 1).transpose(0, 3, 2, 4, 1)
+    wout, head_part = lax.optimization_barrier((wout, head_part))
+    own_out, other_out = gather_gen(wout)
+
+    x = embeddings.reshape(STEPS, TP, OWN, features).transpose(1, 0, 2, 3).reshape(128, features)
+    parts, meta = call(
+        project_kernel,
+        (shape((128, QKV + 128), bf16), shape((32, 128), f32)),
+        me.reshape(1),
+        x,
+        attn_gain.reshape(1, features),
+        pieces,
+        scalars=1,
+    )
+    parts, own_out, other_out = lax.optimization_barrier((parts, own_out, other_out))
+    parts = all_to_all(parts.reshape(TP, 8, QKV + 128), "tp")
+
+    meta = meta.reshape(2, 16, 128)[:, :6, 32:64].astype(i32).reshape(2, 3, 2, GEN)
+    offset = meta[:, 1:].transpose(0, 3, 2, 1).reshape(2, 128)
+    routes = parts[:, :4, QKV + 32 : QKV + 64].astype(f32).astype(i32)
+    row = routes.reshape(TP, 2, 2, GEN // 2, 2).transpose(0, 1, 4, 2, 3)
     side = jnp.bitwise_xor(jnp.arange(2, dtype=i32), jnp.bitwise_and(me, 1))
     spot = side[:, None, None] * 128 + row // OWN * 8 + row % OWN
     spot = spot[:, :, :, :, None, :] + jnp.arange(STEPS, dtype=i32)[:, None] * OWN
     spot = spot.reshape(256, GEN // 2)
-    sampled = jnp.stack([mine // ROWS % 256, mine // (ROWS * 256)], axis=-1)
-    offset = sampled.reshape(GEN, 2, 4).transpose(1, 0, 2).reshape(2, 128)
-
-    x = embeddings.reshape(STEPS, TP, OWN, features).transpose(1, 0, 2, 3).reshape(128, features)
-    parts = call(
-        project_kernel,
-        shape((128, QKV + 128), bf16),
-        me_ref,
-        x,
-        attn_gain.reshape(1, features),
-        own_w,
-        other_w,
-        scalars=1,
-    )
-    parts = all_to_all(parts.reshape(TP, 8, QKV + 128), "tp")
+
     cosine, sine = rotary_tables(lengths)
     wide_lengths = jnp.broadcast_to(jnp.tile(lengths, STEPS)[:, None], (8, 128))
     mixed, entries = call(
@@ -321,32 +374,36 @@
         sine,
     )
     mixed = spread(mixed, "tp", TP).reshape(128, QUERY_HEADS * HEAD_SIZE)
-    layer_out = (
-        x.astype(f32) + jnp.dot(mixed, out_whole, preferred_element_type=f32)
-    ).astype(bf16)
+    layer_out, packed = call(
+        output_kernel,
+        (shape((128, features), bf16), shape((320, 128), bf16)),
+        me.reshape(1),
+        mixed,
+        own_out,
+        other_out,
+        x,
+        scalars=1,
+    )
     last_hidden = layer_out.reshape(TP, STEPS, OWN, features)[:, -1].reshape(ROWS, features)
 
-    own_rows, other_rows = gather_gen(layer_out)
+    own_rows, other_rows = gather_gen(packed)
     gain = lax.dynamic_slice_in_dim(final_gain, rank * features, features, 0)
     logits = call(
         logits_kernel,
         shape((TP, 272, 128), bf16),
-        me_ref,
         own_rows,
         other_rows,
         gain.reshape(1, features),
         spot,
         head_part,
-        scalars=1,
         scratch=[pltpu.VMEM((2 * TP, 128, features), f32)],
     )
     logits = all_to_all(logits, "tp")
     stats = call(stats_kernel, shape((8, 128), f32), logits, offset)
     stats = stats.reshape(8, GEN, 4).transpose(1, 0, 2).reshape(GEN, 1, 32)
     stats = all_to_all(stats, "gen").reshape(GEN, 32).T
-    row_stats = call(
-        rows_kernel, shape((ROWS, 128), f32), stats, rows_of.reshape(GEN, 4).T
-    )
+    rows_of = row_table(kept[0]).reshape(GEN, 4).T
+    row_stats = call(rows_kernel, shape((ROWS, 128), f32), stats, rows_of)
     row_stats = all_to_all(row_stats.reshape(TP, OWN, 128)[:, :, :8], "tp")
     peak, mass, picked = (row_stats[:, :, i : 3 * STEPS : 3] for i in range(3))
     best = jnp.max(peak, axis=0)

time: 405 us -> 339 us (0.84)
  blocking collectives: 21 us -> 123 us
  waiting for transfers between devices: 227 us -> 139 us
  starting transfers between devices: 111 us -> 40.9 us
  local copies, waits for them, and re-layouts: 14.9 us -> 8.8 us
    all_to_all x1 -> x5, blocking collectives: 21 us -> 123 us  [all_to_all(): lax.all_to_all(value, axis, split_axis=0, concat_axis=0, tiled=True, axis...]
    all_gather x1, waiting for transfers between devices: 90.9 us -> 0.02 us  [body(): pieces = lax.all_gather(piece, 'gen')]
    ppermute x14 -> x2, starting transfers between devices: 64.4 us -> 10.1 us  [gather_gen(): return (own, lax.ppermute(own, 'gen', [(g, g ^ 1) for g in range(GEN)]))]
    all_to_all x7 -> x5, waiting for transfers between devices: 84.6 us -> 137 us  [all_to_all(): lax.all_to_all(value, axis, split_axis=0, concat_axis=0, tiled=True, axis...]
    ppermute x14 -> x2, waiting for transfers between devices: 51.2 us -> 1.26 us  [gather_gen(): return (own, lax.ppermute(own, 'gen', [(g, g ^ 1) for g in range(GEN)]))]
    all_to_all x7 -> x5, starting transfers between devices: 46.8 us -> 30.8 us  [all_to_all(): lax.all_to_all(value, axis, split_axis=0, concat_axis=0, tiled=True, axis...]
    pallas_call x5 -> x7, Pallas kernels: 8.58 us -> 11.3 us  [call(): pl.pallas_call(kernel, out_shape=out_shape, in_specs=specs, out_specs=jax...]
  transfers between devices with their start and end apart: 22 -> 8, of which waited for: 18 -> 6; matrix products, arithmetic and copies ran while one was open for 4% -> 1% of each run, Pallas kernels for 1% -> 1%
where the time goes in v2:
time: 339 us; the launch traced here: 338 us
  waiting for transfers between devices  139 us (41%)
  blocking collectives  123 us (36%)
  starting transfers between devices  40.9 us (12%)
  between operations  14.4 us (4%)
  Pallas kernels  11.3 us (3%)
  local copies, waits for them, and re-layouts  8.8 us (3%)
    all_to_all x5, waiting for transfers between devices, all_to_all(): lax.all_to_all(value, axis, split_axis=0, concat_axis=0, tiled=True, axis...  137 us
    all_to_all x5, blocking collectives, all_to_all(): lax.all_to_all(value, axis, split_axis=0, concat_axis=0, tiled=True, axis...  123 us
    all_to_all x5, starting transfers between devices, all_to_all(): lax.all_to_all(value, axis, split_axis=0, concat_axis=0, tiled=True, axis...  30.8 us
    pallas_call x7, Pallas kernels, call(): pl.pallas_call(kernel, out_shape=out_shape, in_specs=specs, out_specs=jax...  11.3 us
    ppermute x2, starting transfers between devices, gather_gen(): return (own, lax.ppermute(own, 'gen', [(g, g ^ 1) for g in range(GEN)]))  10.1 us
  transfers between devices with their start and end apart: 8, of which 6 were waited for; matrix products, arithmetic and copies ran while one was open for 1% of the time, Pallas kernels for 1%

profile of v2, /device:TPU:1, one launch (start us, length us, event | category | flops | bytes accessed | tf_op | source)
XLA Modules:
  0.0 338.1 jit_solution(11581712826370444914)
XLA Ops:
  7.2 9.3 %all-to-all-start = ((bf16[16,320,256]{2,1,0:T(8,128)(2,1)}), bf16[16,320,256]{2,1,0:T(8,128)(2,1)S(1)}, u32[]{:S(2)}, u32[]{:S(2)}) async-start(bf16[16,320,256]{2,1,0:T(8,128)(2,1)} %bitcast.63), calls=%async_computation | async-start | bytes 5242880 | tf_op jit(solution)/shard_map/all_to_all | solution.py:299
  16.7 0.9 shard_map.121
  17.7 64.6 %all-to-all-done.head_ref = bf16[16,320,256]{2,1,0:T(8,128)(2,1)S(1)} async-done(((bf16[16,320,256]{2,1,0:T(8,128)(2,1)}), bf16[16,320,256]{2,1,0:T(8,128)(2,1)S(1)}, u32[]{:S(2)}, u32[]{:S(2)}) %all-to-all-start) | async-done | bytes 2621472 | tf_op jit(solution)/shard_map/all_to_all | solution.py:299
  82.3 44.3 %all_to_all.50 = bf16[4,80,320]{2,1,0:T(8,128)(2,1)S(1)} all-to-all(bf16[4,80,320]{2,1,0:T(8,128)(2,1)S(1)} %broadcast_in_dim.30), channel_id=1, replica_groups={{0,128,256,384},{16,144,272,400},{32,160,288,416},{48,176,304,432},{64,..., dimensions={0} | all-to-all | bytes 409600 | tf_op jit(solution)/shard_map/all_to_all | solution.py:299
  126.7 17.9 %all_to_all.51 = bf16[4,4,80,320]{3,2,1,0:T(8,128)(2,1)S(1)} all-to-all(bf16[4,4,80,320]{3,2,1,0:T(8,128)(2,1)S(1)} %broadcast_in_dim.31), channel_id=1, replica_groups={{0,32,64,96},{16,48,80,112},{128,160,192,224},{144,176,208,240},{256,28..., dimensions={0} | all-to-all | bytes 1638400 | tf_op jit(solution)/shard_map/all_to_all | solution.py:299
  144.5 3.5 %collective-permute-start = (bf16[16,80,320]{2,1,0:T(8,128)(2,1)S(1)}, bf16[16,80,320]{2,1,0:T(8,128)(2,1)S(1)}, u32[]{:S(2)}, u32[]{:S(2)}) collective-permute-start(bf16[16,80,320]{2,1,0:T(8,128)(2,1)S(1)} %bitcast.55), channel_id=1, source_target_pairs={{0,16},{16,0},{32,48},{48,32},{64,80},{80,64},{96,112},{112,96},{1... | collective-permute-start | bytes 2457608 | tf_op jit(solution)/shard_map/ppermute | solution.py:295
  148.2 1.7 copy-done
  149.9 1.0 shard_map.122
  150.9 0.9 copy-done.2
  151.9 0.3 copy-done.4
  152.1 3.6 %all-to-all-start.3 = ((bf16[16,8,3712]{2,1,0:T(8,128)(2,1)}), bf16[16,8,3712]{2,1,0:T(8,128)(2,1)S(1)}, u32[]{:S(2)}, u32[]{:S(2)}) async-start(bf16[16,8,3712]{2,1,0:T(8,128)(2,1)} %bitcast.59), calls=%async_computation.3 | async-start | bytes 1900544 | tf_op jit(solution)/shard_map/all_to_all | solution.py:299
  156.2 25.4 %all-to-all-done.3.parts_ref = bf16[16,8,3712]{2,1,0:T(8,128)(2,1)S(1)} async-done(((bf16[16,8,3712]{2,1,0:T(8,128)(2,1)}), bf16[16,8,3712]{2,1,0:T(8,128)(2,1)S(1)}, u32[]{:S(2)}, u32[]{:S(2)}) %all-to-all-start.3) | async-done | bytes 950304 | tf_op jit(solution)/shard_map/all_to_all | solution.py:299
  181.6 1.8 shard_map.123
  183.5 22.2 %all_to_all.52 = bf16[16,8,2560]{2,1,0:T(8,128)(2,1)S(1)} all-to-all(bf16[16,8,2560]{2,1,0:T(8,128)(2,1)S(1)} %broadcast_in_dim.34), channel_id=1, replica_groups=mesh['gen'=32,'tp'=16] {'tp'}, dimensions={0} | all-to-all | bytes 1310720 | tf_op jit(solution)/shard_map/all_to_all | solution.py:299
  205.7 0.7 shard_map.124
  206.4 22.3 %all_to_all.53 = bf16[4,320,128]{2,1,0:T(8,128)(2,1)S(1)} all-to-all(bf16[4,320,128]{2,1,0:T(8,128)(2,1)S(1)} %broadcast_in_dim.35), channel_id=1, replica_groups={{0,128,256,384},{16,144,272,400},{32,160,288,416},{48,176,304,432},{64,..., dimensions={0} | all-to-all | bytes 655360 | tf_op jit(solution)/shard_map/all_to_all | solution.py:299
  229.0 16.6 %all_to_all.54 = bf16[4,4,320,128]{3,2,1,0:T(8,128)(2,1)S(1)} all-to-all(bf16[4,4,320,128]{3,2,1,0:T(8,128)(2,1)S(1)} %broadcast_in_dim.36), channel_id=1, replica_groups={{0,32,64,96},{16,48,80,112},{128,160,192,224},{144,176,208,240},{256,28..., dimensions={0} | all-to-all | bytes 2621440 | tf_op jit(solution)/shard_map/all_to_all | solution.py:299
  245.6 6.6 %collective-permute-start.1 = (bf16[16,320,128]{2,1,0:T(8,128)(2,1)S(1)}, bf16[16,320,128]{2,1,0:T(8,128)(2,1)}, u32[]{:S(2)}, u32[]{:S(2)}) collective-permute-start(bf16[16,320,128]{2,1,0:T(8,128)(2,1)S(1)} %bitcast.53), channel_id=1, source_target_pairs={{0,16},{16,0},{32,48},{48,32},{64,80},{80,64},{96,112},{112,96},{1... | collective-permute-start | bytes 3932168 | tf_op jit(solution)/shard_map/ppermute | solution.py:295
  252.2 0.8 dynamic_slice.3
  253.7 1.3 collective-permute-done.1.other_ref
  255.0 5.7 %shard_map.125 = bf16[16,272,128]{2,1,0:T(8,128)(2,1)} custom-call(bf16[16,320,128]{2,1,0:T(8,128)(2,1)S(1)} %bitcast.54, bf16[16,320,128]{2,1,0:T(8,128)(2,1)} %collective-permute-done.1.other_ref, bf16[1,320]{1,0:T(2,128)(2,1)S(1)} %reshape.128.gain_ref, s32[256,16]{1,0:T(8,128)S(1)} %broadcast_add_fusion.spot_ref, bf16[16,320,256]{2,1,0:T(8,128)(2,1)} %copy-done.6), custom_call_target="tpu_custom_call" | custom-call | tf_op jit(solution)/shard_map/pallas_call | solution.py:35
  260.6 9.2 %all-to-all-start.7 = ((bf16[16,272,128]{2,1,0:T(8,128)(2,1)}), bf16[16,272,128]{2,1,0:T(8,128)(2,1)S(1)}, u32[]{:S(2)}, u32[]{:S(2)}) async-start(bf16[16,272,128]{2,1,0:T(8,128)(2,1)} %shard_map.125), calls=%async_computation.7 | async-start | bytes 2228224 | tf_op jit(solution)/shard_map/all_to_all | solution.py:299
  270.3 28.0 %all-to-all-done.7.parts_ref = bf16[16,272,128]{2,1,0:T(8,128)(2,1)S(1)} async-done(((bf16[16,272,128]{2,1,0:T(8,128)(2,1)}), bf16[16,272,128]{2,1,0:T(8,128)(2,1)S(1)}, u32[]{:S(2)}, u32[]{:S(2)}) %all-to-all-start.7) | async-done | bytes 1114144 | tf_op jit(solution)/shard_map/all_to_all | solution.py:299
  298.7 0.7 copy.83
  299.4 5.2 %all-to-all-start.8 = ((f32[32,1,32]{2,1,0:T(1,128)}), f32[32,1,32]{2,1,0:T(1,128)S(1)}, u32[]{:S(2)}, u32[]{:S(2)}) async-start(f32[32,1,32]{2,1,0:T(1,128)} %copy.83), calls=%async_computation.8 | async-start | bytes 32768 | tf_op jit(solution)/shard_map/all_to_all | solution.py:299
  304.9 14.0 %all-to-all-done.8 = f32[32,1,32]{2,1,0:T(1,128)S(1)} async-done(((f32[32,1,32]{2,1,0:T(1,128)}), f32[32,1,32]{2,1,0:T(1,128)S(1)}, u32[]{:S(2)}, u32[]{:S(2)}) %all-to-all-start.8) | async-done | bytes 4128 | tf_op jit(solution)/shard_map/all_to_all | solution.py:299
  318.9 1.0 shard_map.127
  319.9 3.5 %all-to-all-start.9 = ((f32[16,4,8]{2,1,0:T(4,128)}), f32[16,4,8]{2,1,0:T(4,128)S(1)}, u32[]{:S(2)}, u32[]{:S(2)}) async-start(f32[16,4,8]{2,1,0:T(4,128)} %bitcast.52), calls=%async_computation.9 | async-start | bytes 65536 | tf_op jit(solution)/shard_map/all_to_all | solution.py:299
  323.4 0.6 reshape.139
  324.1 0.6 reshape_squeeze.3
  324.7 5.5 %all-to-all-done.9 = f32[16,4,8]{2,1,0:T(4,128)S(1)} async-done(((f32[16,4,8]{2,1,0:T(4,128)}), f32[16,4,8]{2,1,0:T(4,128)S(1)}, u32[]{:S(2)}, u32[]{:S(2)}) %all-to-all-start.9) | async-done | bytes 2080 | tf_op jit(solution)/shard_map/all_to_all | solution.py:299
  330.6 0.7 copy.87
  (83 shorter events, 3.7 us)
Async XLA Ops:
  7.2 9.4 %copy-start.9 = (s32[1,64,2]{1,2,0:T(2,128)S(1)}, s32[1,64,2]{1,2,0:T(2,128)}, u32[]{:S(2)}) copy-start(s32[1,64,2]{1,2,0:T(2,128)} %param.18) | copy-start | bytes 1540
  7.2 9.4 %copy-start.11 = (s32[2,64]{1,0:T(2,128)S(1)}, s32[2,64]{1,0:T(2,128)}, u32[]{:S(2)}) copy-start(s32[2,64]{1,0:T(2,128)} %param.19) | copy-start | bytes 1540
  7.2 9.5 %copy-start.5 = (bf16[320,112]{1,0:T(8,128)(2,1)S(1)}, bf16[320,112]{1,0:T(8,128)(2,1)}, u32[]{:S(2)}) copy-start(bf16[320,112]{1,0:T(8,128)(2,1)} %weights_ref.1) | copy-start | bytes 215044
  7.2 75.1 %copy-start.8 = (bf16[80,320]{1,0:T(8,128)(2,1)S(1)}, bf16[80,320]{1,0:T(8,128)(2,1)}, u32[]{:S(2)}) copy-start(bf16[80,320]{1,0:T(8,128)(2,1)} %param.15) | copy-start | bytes 153604
  7.2 75.1 %all-to-all-start = ((bf16[16,320,256]{2,1,0:T(8,128)(2,1)}), bf16[16,320,256]{2,1,0:T(8,128)(2,1)S(1)}, u32[]{:S(2)}, u32[]{:S(2)}) async-start(bf16[16,320,256]{2,1,0:T(8,128)(2,1)} %bitcast.63), calls=%async_computation | async-start | bytes 5242880 | tf_op jit(solution)/shard_map/all_to_all | solution.py:299
  16.5 131.7 %all-gather.3.cloned.1.call-start = ((), (), s32[]{:S(2)}) async-start(), calls=%async_computation.10 | async-start | bytes 2433024 | tf_op jit(solution)/shard_map/all_gather | solution.py:338
  82.3 44.3 %copy-start.6 = (bf16[16,320,256]{2,1,0:T(8,128)(2,1)}, bf16[16,320,256]{2,1,0:T(8,128)(2,1)S(1)}, u32[]{:S(2)}) copy-start(bf16[16,320,256]{2,1,0:T(8,128)(2,1)S(1)} %all-to-all-done.head_ref) | copy-start | bytes 7864324
  126.6 21.4 %copy-start.10 = (bf16[320]{0:T(512)(128)(2,1)S(1)}, bf16[320]{0:T(512)(128)(2,1)}, u32[]{:S(2)}) copy-start(bf16[320]{0:T(512)(128)(2,1)} %param.13) | copy-start | bytes 1924
  126.6 21.5 %copy-start.7 = (bf16[2,64,320]{2,1,0:T(8,128)(2,1)S(1)}, bf16[2,64,320]{2,1,0:T(8,128)(2,1)}, u32[]{:S(2)}) copy-start(bf16[2,64,320]{2,1,0:T(8,128)(2,1)} %param.10) | copy-start | bytes 245764
  144.5 6.4 %collective-permute-start = (bf16[16,80,320]{2,1,0:T(8,128)(2,1)S(1)}, bf16[16,80,320]{2,1,0:T(8,128)(2,1)S(1)}, u32[]{:S(2)}, u32[]{:S(2)}) collective-permute-start(bf16[16,80,320]{2,1,0:T(8,128)(2,1)S(1)} %bitcast.55), channel_id=1, source_target_pairs={{0,16},{16,0},{32,48},{48,32},{64,80},{80,64},{96,112},{112,96},{1... | collective-permute-start | bytes 2457608 | tf_op jit(solution)/shard_map/ppermute | solution.py:295
  148.2 1.7 copy-start
  150.9 1.3 copy-start.4
  150.9 4.9 %copy-start.12 = (s32[4]{0:T(128)S(1)}, s32[4]{0:T(128)}, u32[]{:S(2)}) copy-start(s32[4]{0:T(128)} %param.12) | copy-start | bytes 52
  150.9 30.8 %copy-start.1 = (bf16[4,128,1024]{2,1,0:T(8,128)(2,1)S(1)}, bf16[4,128,1024]{2,1,0:T(8,128)(2,1)}, u32[]{:S(2)}) copy-start(bf16[4,128,1024]{2,1,0:T(8,128)(2,1)} %cache_ref.1) | copy-start | bytes 3145732
  150.9 1.0 copy-start.2
  152.1 29.4 %all-to-all-start.3 = ((bf16[16,8,3712]{2,1,0:T(8,128)(2,1)}), bf16[16,8,3712]{2,1,0:T(8,128)(2,1)S(1)}, u32[]{:S(2)}, u32[]{:S(2)}) async-start(bf16[16,8,3712]{2,1,0:T(8,128)(2,1)} %bitcast.59), calls=%async_computation.3 | async-start | bytes 1900544 | tf_op jit(solution)/shard_map/all_to_all | solution.py:299
  183.4 22.2 %copy-start.3 = (bf16[16,80,320]{2,1,0:T(8,128)(2,1)S(1)}, bf16[16,80,320]{2,1,0:T(8,128)(2,1)}, u32[]{:S(2)}) copy-start(bf16[16,80,320]{2,1,0:T(8,128)(2,1)} %copy-done.2) | copy-start | bytes 2457604
  245.6 9.4 %collective-permute-start.1 = (bf16[16,320,128]{2,1,0:T(8,128)(2,1)S(1)}, bf16[16,320,128]{2,1,0:T(8,128)(2,1)}, u32[]{:S(2)}, u32[]{:S(2)}) collective-permute-start(bf16[16,320,128]{2,1,0:T(8,128)(2,1)S(1)} %bitcast.53), channel_id=1, source_target_pairs={{0,16},{16,0},{32,48},{48,32},{64,80},{80,64},{96,112},{112,96},{1... | collective-permute-start | bytes 3932168 | tf_op jit(solution)/shard_map/ppermute | solution.py:295
  260.6 37.6 %all-to-all-start.7 = ((bf16[16,272,128]{2,1,0:T(8,128)(2,1)}), bf16[16,272,128]{2,1,0:T(8,128)(2,1)S(1)}, u32[]{:S(2)}, u32[]{:S(2)}) async-start(bf16[16,272,128]{2,1,0:T(8,128)(2,1)} %shard_map.125), calls=%async_computation.7 | async-start | bytes 2228224 | tf_op jit(solution)/shard_map/all_to_all | solution.py:299
  299.4 19.4 %all-to-all-start.8 = ((f32[32,1,32]{2,1,0:T(1,128)}), f32[32,1,32]{2,1,0:T(1,128)S(1)}, u32[]{:S(2)}, u32[]{:S(2)}) async-start(f32[32,1,32]{2,1,0:T(1,128)} %copy.83), calls=%async_computation.8 | async-start | bytes 32768 | tf_op jit(solution)/shard_map/all_to_all | solution.py:299
  319.9 10.3 %all-to-all-start.9 = ((f32[16,4,8]{2,1,0:T(4,128)}), f32[16,4,8]{2,1,0:T(4,128)S(1)}, u32[]{:S(2)}, u32[]{:S(2)}) async-start(f32[16,4,8]{2,1,0:T(4,128)} %bitcast.52), calls=%async_computation.9 | async-start | bytes 65536 | tf_op jit(solution)/shard_map/all_to_all | solution.py:299
Sparse Core Ops, SparseCore 0:
  20.5 110.2 all-gather.2

commit v3 on v2

--- a/solution.py
+++ b/solution.py
@@ -86,23 +86,32 @@
     out_ref[224:288, :] = jnp.concatenate([turned[0:64, 256:320], side], axis=1).astype(bf16)
 
 
-def project_kernel(me_ref, x_ref, gain_ref, pieces_ref, out_ref, meta_ref):
+def project_kernel(me_ref, x_ref, gain_ref, own_ref, other_ref, out_ref, meta_ref):
     me = me_ref[0]
+    core = lax.rem(me, 2)
     wide = x_ref[...].astype(f32)
     scaled = (wide * gain_ref[...].astype(f32)).astype(bf16)
     scaled = jnp.concatenate([scaled, jnp.zeros((128, 64), bf16)], axis=1)
     lane = lax.broadcasted_iota(i32, (16, 128), 1)
     metas = [jnp.zeros((16, 128), f32), jnp.zeros((16, 128), f32)]
+    line = lax.rem(lax.broadcasted_iota(i32, (TP * 8, 128), 0), 8)
+    extra = jnp.zeros((TP * 8, 128), f32)
     for z in range(4):
         pieces = []
-        for g in range(8 * z, 8 * z + 8):
-            piece = pieces_ref[g]
-            pieces.append(unpack(piece, 112))
-            table = piece[272:288].astype(f32)
-            for j in range(2):
-                mine = jnp.where(lane == 64 + 2 * me + j, table, 0.0)
-                column = jnp.sum(mine, axis=1, keepdims=True)
-                metas[j] = jnp.where(lane == 32 + g, column, metas[j])
+        for x in range(4):
+            a = own_ref[x * 4 + z]
+            b = other_ref[x * 4 + z]
+            for c, piece in enumerate((jnp.where(core == 0, a, b), jnp.where(core == 0, b, a))):
+                pieces.append(unpack(piece, 112))
+                table = piece[272:288].astype(f32)
+                for j in range(2):
+                    mine = jnp.where(lane == 64 + 2 * me + j, table, 0.0)
+                    column = jnp.sum(mine, axis=1, keepdims=True)
+                    at = 32 + gen_index(z, x, c)
+                    metas[j] = jnp.where(lane == at, column, metas[j])
+        table = own_ref[lax.rem(me // 2, 4) * 4 + z][272:288].astype(f32)
+        for slot in range(2):
+            extra = jnp.where(line == 2 * z + slot, table[slot : slot + 1], extra)
         part = nt_dot(scaled, jnp.concatenate(pieces, axis=0))
         out_ref[:, z * 896 : (z + 1) * 896] = part.astype(bf16)
     for j in range(2):
@@ -110,32 +119,15 @@
     squares = jnp.sum(wide * wide, axis=1, keepdims=True)
     high = squares.astype(bf16).astype(f32)
     low = squares - high
-    line = lax.rem(lax.broadcasted_iota(i32, (TP * 8, 128), 0), 8)
     lane = lax.broadcasted_iota(i32, (TP * 8, 128), 1)
-    extra = jnp.zeros((TP * 8, 128), f32)
-    for j in range(2):
-        for slot in range(2):
-            extra = jnp.where(line == 2 * j + slot, metas[j][slot : slot + 1], extra)
+    extra = jnp.where(lane < 64, 0.0, extra)
     extra = jnp.where(lane == 0, high, jnp.where(lane == 1, low, extra))
     out_ref[:, QKV:] = extra.astype(bf16)
 
 
-def output_kernel(me_ref, mixed_ref, own_ref, other_ref, x_ref, rows_ref, packed_ref):
-    core = lax.rem(me_ref[0], 2)
-    total = x_ref[...].astype(f32)
-    for z in range(4):
-        pieces = []
-        for x in range(4):
-            a = own_ref[x * 4 + z]
-            b = other_ref[x * 4 + z]
-            pieces += [jnp.where(core == 0, a, b), jnp.where(core == 0, b, a)]
-        depth = 8 * pieces[0].shape[0]
-        total = total + jnp.dot(
-            mixed_ref[:, z * depth : (z + 1) * depth],
-            jnp.concatenate(pieces, axis=0),
-            preferred_element_type=f32,
-        )
-    rows = total.astype(bf16)
+def output_kernel(mixed_ref, weights_ref, x_ref, rows_ref, packed_ref):
+    part = jnp.dot(mixed_ref[...], weights_ref[...], preferred_element_type=f32)
+    rows = (x_ref[...].astype(f32) + part).astype(bf16)
     rows_ref[...] = rows
     packed_ref[0:128, :] = rows[:, 0:128]
     packed_ref[128:256, :] = rows[:, 128:256]
@@ -194,61 +186,64 @@
             mixed_ref[:, to : to + HEAD_SIZE] = mixed[8 * h : 8 * h + 8].astype(bf16)
 
 
-def logits_kernel(own_ref, other_ref, gain_ref, spot_ref, head_ref, out_ref, pairs_ref):
-    lane = lax.broadcasted_iota(i32, (256, 256), 1)
-    features = gain_ref.shape[1]
-    for pair in range(GEN // 2):
-        place = pair % 4 * 4 + pair // 4
-        rows = [unpack(ref[place], 128) for ref in (own_ref, other_ref)]
-        pick = (spot_ref[:, pair : pair + 1] == lane).astype(f32).astype(bf16)
-        taken = jnp.dot(pick, jnp.concatenate(rows, axis=0), preferred_element_type=f32)
-        for b in range(2 * TP):
-            pairs_ref[b, 8 * pair : 8 * pair + 8, :] = taken[8 * b : 8 * b + 8, :features]
-    gain = gain_ref[...].astype(f32)
-    column = lax.broadcasted_iota(i32, (128, 128), 1)
-    squares = jnp.zeros((128, 128), f32)
+def select_kernel(layer_ref, spot_ref, out_ref):
+    owners = out_ref.shape[0]
+    lane = lax.broadcasted_iota(i32, (16 * owners, 256), 1)
+    low = lax.broadcasted_iota(i32, (256, 128), 1) < 64
+    tails = jnp.zeros((16 * owners, 128), f32)
+    for half in range(2):
+        pieces = [layer_ref[2 * half], layer_ref[2 * half + 1]]
+        sides = [jnp.concatenate([p[256:], swap_halves(p[256:].astype(f32)).astype(bf16)], axis=0) for p in pieces]
+        tail = jnp.concatenate(sides, axis=0).astype(f32)
+        if half:
+            tail = swap_halves(tail)
+        tail = jnp.where(low if half == 0 else jnp.logical_not(low), tail, 0.0).astype(bf16)
+        pick = (spot_ref[:, half : half + 1] == lane).astype(f32).astype(bf16)
+        for part in range(2):
+            rows = jnp.concatenate([p[128 * part : 128 * part + 128] for p in pieces], axis=0)
+            taken = jnp.dot(pick, rows, preferred_element_type=f32).astype(bf16)
+            at = 32 * part + 16 * half
+            out_ref[:, at : at + 16, :] = taken.reshape(owners, 16, 128)
+        tails = tails + jnp.dot(pick, tail, preferred_element_type=f32)
+    out_ref[:, 64:80, :] = tails.astype(bf16).reshape(owners, 16, 128)
+
+
+def logits_kernel(rows_ref, gain_ref, head_ref, offset_ref, out_ref):
+    def piece(t):
+        tail = rows_ref[:, t, 64:80, :].reshape(128, 128).astype(f32)
+        tail = [tail.reshape(8, 16, 128), swap_halves(tail).reshape(8, 16, 128)]
+        parts = [rows_ref[:, t, 0:32, :].reshape(256, 128), rows_ref[:, t, 32:64, :].reshape(256, 128)]
+        wide = [p.astype(f32) for p in parts]
+        return wide + [jnp.concatenate(tail, axis=1).reshape(256, 128)[:, :64]]
+
+    squares = jnp.zeros((256, 128), f32)
+    tails = jnp.zeros((256, 64), f32)
     for t in range(TP):
-        for j in range(2):
-            raw = pairs_ref[2 * t + j]
-            squares = jnp.where(
-                column == 2 * t + j, jnp.sum(raw * raw, axis=1, keepdims=True), squares
-            )
-            part = jnp.dot(
-                (raw * gain).astype(bf16),
-                head_ref[t, :, j * BLOCK : (j + 1) * BLOCK],
-                preferred_element_type=f32,
-            )
-            out_ref[t, j * 128 : (j + 1) * 128, :] = part.astype(bf16)
-    squares = squares.T
-    high = squares.astype(bf16).astype(f32)
-    low = squares - high
-    line = lax.broadcasted_iota(i32, (16, 128), 0)
+        a, b, c = piece(t)
+        squares = squares + (a * a + b * b)
+        tails = tails + c * c
+    total = jnp.sum(squares, axis=1, keepdims=True) + jnp.sum(tails, axis=1, keepdims=True)
+    factor = lax.rsqrt(total / D + epsilon)
+    logits = jnp.zeros((256, 2 * BLOCK), f32)
     for t in range(TP):
-        extra = jnp.zeros((16, 128), f32)
-        for j in range(2):
-            b = 2 * t + j
-            extra = jnp.where(line == 2 * j, high[b : b + 1], extra)
-            extra = jnp.where(line == 2 * j + 1, low[b : b + 1], extra)
-        out_ref[t, 256:272, :] = extra.astype(bf16)
-
-
-def stats_kernel(parts_ref, offset_ref, out_ref):
-    total = parts_ref[0].astype(f32)
-    for t in range(1, TP):
-        total = total + parts_ref[t].astype(f32)
+        at = t * 320
+        for value, width in zip(piece(t), (128, 128, 64)):
+            normed = (value * factor * gain_ref[:, at : at + width].astype(f32)).astype(bf16)
+            weights = head_ref[at : at + width, :]
+            logits = logits + jnp.dot(normed, weights, preferred_element_type=f32)
+            at += width
+    pair = lax.broadcasted_iota(i32, (256, BLOCK), 0)
+    logits = jnp.where(lax.rem(pair // 4, 2) == 0, logits[:, :BLOCK], logits[:, BLOCK:])
     token = lax.broadcasted_iota(i32, (BLOCK, 128), 0)
     line = lax.broadcasted_iota(i32, (8, 128), 0)
-    out = jnp.zeros((8, 128), f32)
-    for j in range(2):
-        squares = total[256 + 2 * j : 257 + 2 * j] + total[257 + 2 * j : 258 + 2 * j]
-        logits = total[j * 128 : (j + 1) * 128].T * lax.rsqrt(squares / D + epsilon)
-        peak = jnp.max(logits, axis=0, keepdims=True)
-        mass = jnp.sum(jnp.exp(logits - peak), axis=0, keepdims=True)
-        hit = jnp.where(token == offset_ref[j : j + 1] - 1, logits, 0.0)
-        picked = jnp.sum(hit, axis=0, keepdims=True)
-        for at, value in enumerate((peak, mass, picked)):
-            out = jnp.where(line == 3 * j + at, value, out)
-    out_ref[...] = out
+    for half in range(2):
+        side = logits[128 * half : 128 * half + 128].T
+        peak = jnp.max(side, axis=0, keepdims=True)
+        mass = jnp.sum(jnp.exp(side - peak), axis=0, keepdims=True)
+        target = offset_ref[:, 128 * half : 128 * half + 128] - 1
+        picked = jnp.sum(jnp.where(token == target, side, 0.0), axis=0, keepdims=True)
+        out = jnp.where(line == 0, peak, jnp.where(line == 1, mass, picked))
+        out_ref[:, 128 * half : 128 * half + 128] = out
 
 
 def rows_kernel(stats_ref, row_ref, out_ref):
@@ -261,7 +256,7 @@
         masks = [row_ref[2 * j + slot : 2 * j + slot + 1, :] == mine for j, slot in combos]
 
         def stat(which, j, slot):
-            at = (3 * j + which) * 4 + slot * 2 + s
+            at = which * 8 + j * 4 + slot * 2 + s
             return stats_ref[at : at + 1, :]
 
         for mask, (j, slot) in zip(masks, combos):
@@ -288,6 +283,9 @@
 X_GROUPS = [[gen_index(z, x, c) for x in range(4)] for z in range(4) for c in range(2)]
 
 
+LAYERS = [[z * 128 + i for i in range(128)] for z in range(4)]
+
+
 def gather_gen(piece):
     along_z = spread(piece, "gen", 4, Z_GROUPS)
     along_x = spread(along_z, "gen", 4, X_GROUPS)
@@ -331,14 +329,12 @@
     me = lax.axis_index("gen").astype(i32)
     features = D // TP
 
+    out_whole = lax.all_gather(wout, "gen", axis=0, tiled=True)
     table = jnp.concatenate([kept[0], chosen.T], axis=1)
     piece = call(
         pack_kernel, shape((288, 128), bf16), rank.reshape(1), wqkv, table, scalars=1
     )
-    pieces = lax.all_gather(piece, "gen")
-    head_part = all_to_all(head.reshape(TP, features, 2 * BLOCK), "tp")
-    wout, head_part = lax.optimization_barrier((wout, head_part))
-    own_out, other_out = gather_gen(wout)
+    own_w, other_w = gather_gen(piece)
 
     x = embeddings.reshape(STEPS, TP, OWN, features).transpose(1, 0, 2, 3).reshape(128, features)
     parts, meta = call(
@@ -347,20 +343,19 @@
         me.reshape(1),
         x,
         attn_gain.reshape(1, features),
-        pieces,
+        own_w,
+        other_w,
         scalars=1,
     )
-    parts, own_out, other_out = lax.optimization_barrier((parts, own_out, other_out))
     parts = all_to_all(parts.reshape(TP, 8, QKV + 128), "tp")
 
     meta = meta.reshape(2, 16, 128)[:, :6, 32:64].astype(i32).reshape(2, 3, 2, GEN)
-    offset = meta[:, 1:].transpose(0, 3, 2, 1).reshape(2, 128)
-    routes = parts[:, :4, QKV + 32 : QKV + 64].astype(f32).astype(i32)
-    row = routes.reshape(TP, 2, 2, GEN // 2, 2).transpose(0, 1, 4, 2, 3)
-    side = jnp.bitwise_xor(jnp.arange(2, dtype=i32), jnp.bitwise_and(me, 1))
-    spot = side[:, None, None] * 128 + row // OWN * 8 + row % OWN
-    spot = spot[:, :, :, :, None, :] + jnp.arange(STEPS, dtype=i32)[:, None] * OWN
-    spot = spot.reshape(256, GEN // 2)
+    offset = meta[:, 1:].reshape(2, 2, 2, 4, 8).transpose(4, 3, 0, 2, 1).reshape(1, 256)
+    routes = lax.dynamic_slice_in_dim(parts[:, :, QKV + 64 :], me // 8 * 16, 16, 2)
+    row = routes.astype(f32).astype(i32).reshape(TP, 2, 2, 2, 8, 2).transpose(4, 0, 2, 5, 3, 1)
+    spot = jnp.arange(2, dtype=i32)[:, None, None, None] * 128 + row // OWN * 8 + row % OWN
+    spot = spot[:, :, :, :, :, None, :] + jnp.arange(STEPS, dtype=i32)[:, None] * OWN
+    spot = spot.reshape(16 * 128, 2)
 
     cosine, sine = rotary_tables(lengths)
     wide_lengths = jnp.broadcast_to(jnp.tile(lengths, STEPS)[:, None], (8, 128))
@@ -377,31 +372,25 @@
     layer_out, packed = call(
         output_kernel,
         (shape((128, features), bf16), shape((320, 128), bf16)),
-        me.reshape(1),
         mixed,
-        own_out,
-        other_out,
+        out_whole,
         x,
-        scalars=1,
     )
     last_hidden = layer_out.reshape(TP, STEPS, OWN, features)[:, -1].reshape(ROWS, features)
 
-    own_rows, other_rows = gather_gen(packed)
-    gain = lax.dynamic_slice_in_dim(final_gain, rank * features, features, 0)
-    logits = call(
+    layers = spread(packed, "gen", 4, Z_GROUPS)
+    taken = call(select_kernel, shape((128, 80, 128), bf16), layers, spot)
+    taken = all_to_all(taken, ("gen", "tp"), LAYERS).reshape(8, TP, 80, 128)
+    stats = call(
         logits_kernel,
-        shape((TP, 272, 128), bf16),
-        own_rows,
-        other_rows,
-        gain.reshape(1, features),
-        spot,
-        head_part,
-        scratch=[pltpu.VMEM((2 * TP, 128, features), f32)],
-    )
-    logits = all_to_all(logits, "tp")
-    stats = call(stats_kernel, shape((8, 128), f32), logits, offset)
-    stats = stats.reshape(8, GEN, 4).transpose(1, 0, 2).reshape(GEN, 1, 32)
-    stats = all_to_all(stats, "gen").reshape(GEN, 32).T
+        shape((8, 256), f32),
+        taken,
+        final_gain.reshape(1, D),
+        head,
+        offset,
+    )
+    stats = stats[:3].reshape(3, 8, 4, 8).transpose(2, 1, 0, 3).reshape(GEN, 1, 24)
+    stats = all_to_all(stats, "gen").reshape(GEN, 24).T
     rows_of = row_table(kept[0]).reshape(GEN, 4).T
     row_stats = call(rows_kernel, shape((ROWS, 128), f32), stats, rows_of)
     row_stats = all_to_all(row_stats.reshape(TP, OWN, 128)[:, :, :8], "tp")

time: 339 us -> 308 us (0.909)
  blocking collectives: 123 us -> 44.3 us
  waiting for transfers between devices: 139 us -> 168 us
  starting transfers between devices: 40.9 us -> 55.2 us
  local copies, waits for them, and re-layouts: 8.8 us -> 14.8 us
    all_to_all x5 -> x2, blocking collectives: 123 us -> 44.3 us  [all_to_all(): lax.all_to_all(value, axis, split_axis=0, concat_axis=0, tiled=True, axis...]
    all_gather x1, waiting for transfers between devices: 0.02 us -> 43.3 us  [body(): out_whole = lax.all_gather(wout, 'gen', axis=0, tiled=True)]
    all_to_all x5 -> x6, waiting for transfers between devices: 137 us -> 121 us  [all_to_all(): lax.all_to_all(value, axis, split_axis=0, concat_axis=0, tiled=True, axis...]
    all_to_all x5 -> x6, starting transfers between devices: 30.8 us -> 46.2 us  [all_to_all(): lax.all_to_all(value, axis, split_axis=0, concat_axis=0, tiled=True, axis...]
    unnamed x28 -> x24, local copies, waits for them, and re-layouts: 3.58 us -> 7.29 us
    ppermute x2 -> x1, starting transfers between devices: 10.1 us -> 9.02 us  [gather_gen(): return (own, lax.ppermute(own, 'gen', [(g, g ^ 1) for g in range(GEN)]))]
  transfers between devices with their start and end apart: 8 -> 8, of which waited for: 6 -> 7; matrix products, arithmetic and copies ran while one was open for 1% -> 2% of each run, Pallas kernels for 1% -> 1%
where the time goes in v3:
time: 308 us; the launch traced here: 307 us
  waiting for transfers between devices  168 us (55%)
  starting transfers between devices  55.2 us (18%)
  blocking collectives  44.3 us (14%)
  local copies, waits for them, and re-layouts  14.8 us (5%)
  between operations  14.3 us (5%)
  Pallas kernels  9.37 us (3%)
    all_to_all x6, waiting for transfers between devices, all_to_all(): lax.all_to_all(value, axis, split_axis=0, concat_axis=0, tiled=True, axis...  121 us
    all_to_all x6, starting transfers between devices, all_to_all(): lax.all_to_all(value, axis, split_axis=0, concat_axis=0, tiled=True, axis...  46.2 us
    all_to_all x2, blocking collectives, all_to_all(): lax.all_to_all(value, axis, split_axis=0, concat_axis=0, tiled=True, axis...  44.3 us
    all_gather x1, waiting for transfers between devices, body(): out_whole = lax.all_gather(wout, 'gen', axis=0, tiled=True)  43.3 us
    pallas_call x7, Pallas kernels, call(): pl.pallas_call(kernel, out_shape=out_shape, in_specs=specs, out_specs=jax...  9.37 us
    ppermute x1, starting transfers between devices, gather_gen(): return (own, lax.ppermute(own, 'gen', [(g, g ^ 1) for g in range(GEN)]))  9.02 us
    unnamed x24, local copies, waits for them, and re-layouts  7.29 us
  transfers between devices with their start and end apart: 8, of which 7 were waited for; matrix products, arithmetic and copies ran while one was open for 2% of the time, Pallas kernels for 1%

profile of v3, /device:TPU:1, one launch (start us, length us, event | category | flops | bytes accessed | tf_op | source)
XLA Modules:
  0.0 307.4 jit_solution(12646089885366998331)
XLA Ops:
  7.2 0.7 pad_add_fusion
  8.0 0.9 copy-done.5
  9.2 30.0 %all_to_all.40 = bf16[4,288,128]{2,1,0:T(8,128)(2,1)S(1)} all-to-all(bf16[4,288,128]{2,1,0:T(8,128)(2,1)S(1)} %broadcast_in_dim.28), channel_id=1, replica_groups={{0,128,256,384},{16,144,272,400},{32,160,288,416},{48,176,304,432},{64,..., dimensions={0} | all-to-all | bytes 589824 | tf_op jit(solution)/shard_map/all_to_all | solution.py:297
  39.4 14.3 %all_to_all.41 = bf16[4,4,288,128]{3,2,1,0:T(8,128)(2,1)S(1)} all-to-all(bf16[4,4,288,128]{3,2,1,0:T(8,128)(2,1)S(1)} %broadcast_in_dim.29), channel_id=1, replica_groups={{0,32,64,96},{16,48,80,112},{128,160,192,224},{144,176,208,240},{256,28..., dimensions={0} | all-to-all | bytes 2359296 | tf_op jit(solution)/shard_map/all_to_all | solution.py:297
  53.6 9.0 %collective-permute-start = (bf16[16,288,128]{2,1,0:T(8,128)(2,1)S(1)}, bf16[16,288,128]{2,1,0:T(8,128)(2,1)S(1)}, u32[]{:S(2)}, u32[]{:S(2)}) collective-permute-start(bf16[16,288,128]{2,1,0:T(8,128)(2,1)S(1)} %bitcast.50), channel_id=1, source_target_pairs={{0,16},{16,0},{32,48},{48,32},{64,80},{80,64},{96,112},{112,96},{1... | collective-permute-start | bytes 3538952 | tf_op jit(solution)/shard_map/ppermute | solution.py:293
  62.8 2.3 collective-permute-done.other_ref
  65.1 1.0 shard_map.122
  66.1 0.9 copy-done.4
  67.1 12.8 %all-to-all-start.2 = ((bf16[16,8,3712]{2,1,0:T(8,128)(2,1)}), bf16[16,8,3712]{2,1,0:T(8,128)(2,1)S(1)}, u32[]{:S(2)}, u32[]{:S(2)}) async-start(bf16[16,8,3712]{2,1,0:T(8,128)(2,1)} %bitcast.53), calls=%async_computation.2 | async-start | bytes 1900544 | tf_op jit(solution)/shard_map/all_to_all | solution.py:297
  79.9 0.7 all-gather.2.cloned.1.call-update
  81.0 25.1 %all-to-all-done.2.parts_ref = bf16[16,8,3712]{2,1,0:T(8,128)(2,1)S(1)} async-done(((bf16[16,8,3712]{2,1,0:T(8,128)(2,1)}), bf16[16,8,3712]{2,1,0:T(8,128)(2,1)S(1)}, u32[]{:S(2)}, u32[]{:S(2)}) %all-to-all-start.2) | async-done | bytes 950304 | tf_op jit(solution)/shard_map/all_to_all | solution.py:297
  106.1 1.8 shard_map.123
  107.9 0.9 broadcast_in_dim.32
  108.8 4.1 %all-to-all-start.3 = ((bf16[16,8,2560]{2,1,0:T(8,128)(2,1)}), bf16[16,8,2560]{2,1,0:T(8,128)(2,1)S(1)}, u32[]{:S(2)}, u32[]{:S(2)}) async-start(bf16[16,8,2560]{2,1,0:T(8,128)(2,1)} %broadcast_in_dim.32), calls=%async_computation.3 | async-start | bytes 1310720 | tf_op jit(solution)/shard_map/all_to_all | solution.py:297
  112.9 43.3 %all-gather.2.cloned.1.call-done.weights_ref = bf16[2560,320]{1,0:T(8,128)(2,1)} async-done(((bf16[80,320]{1,0:T(8,128)(2,1)}), bf16[2560,320]{1,0:T(8,128)(2,1)}) %all-gather.2.cloned.1.call-update) | async-done | bytes 1638416 | tf_op jit(solution)/shard_map/all_gather | solution.py:332
  156.2 1.5 copy-done.2
  158.3 0.8 broadcast_in_dim.33
  159.1 5.0 %all-to-all-start.4 = ((bf16[4,320,128]{2,1,0:T(8,128)(2,1)}), bf16[4,320,128]{2,1,0:T(8,128)(2,1)S(1)}, u32[]{:S(2)}, u32[]{:S(2)}) async-start(bf16[4,320,128]{2,1,0:T(8,128)(2,1)} %broadcast_in_dim.33), calls=%async_computation.4 | async-start | bytes 655360 | tf_op jit(solution)/shard_map/all_to_all | solution.py:297
  166.3 15.0 %all-to-all-done.4.layer_ref = bf16[4,320,128]{2,1,0:T(8,128)(2,1)S(1)} async-done(((bf16[4,320,128]{2,1,0:T(8,128)(2,1)}), bf16[4,320,128]{2,1,0:T(8,128)(2,1)S(1)}, u32[]{:S(2)}, u32[]{:S(2)}) %all-to-all-start.4) | async-done | bytes 327712 | tf_op jit(solution)/shard_map/all_to_all | solution.py:297
  181.3 2.2 shard_map.125
  183.5 1.5 copy-done
  185.0 15.8 %all-to-all-start.5 = ((bf16[128,80,128]{2,1,0:T(8,128)(2,1)}), bf16[128,80,128]{2,1,0:T(8,128)(2,1)S(1)}, u32[]{:S(2)}, u32[]{:S(2)}) async-start(bf16[128,80,128]{2,1,0:T(8,128)(2,1)} %copy-done), calls=%async_computation.5 | async-start | bytes 5242880 | tf_op jit(solution)/shard_map/all_to_all | solution.py:297
  201.5 62.0 %all-to-all-done.5 = bf16[128,80,128]{2,1,0:T(8,128)(2,1)S(1)} async-done(((bf16[128,80,128]{2,1,0:T(8,128)(2,1)}), bf16[128,80,128]{2,1,0:T(8,128)(2,1)S(1)}, u32[]{:S(2)}, u32[]{:S(2)}) %all-to-all-start.5) | async-done | bytes 2621472 | tf_op jit(solution)/shard_map/all_to_all | solution.py:297
  263.5 1.7 copy-done.1
  265.2 2.6 shard_map.126
  268.1 0.7 copy.84
  268.8 4.9 %all-to-all-start.6 = ((f32[32,1,24]{2,1,0:T(1,128)}), f32[32,1,24]{2,1,0:T(1,128)S(1)}, u32[]{:S(2)}, u32[]{:S(2)}) async-start(f32[32,1,24]{2,1,0:T(1,128)} %copy.84), calls=%async_computation.6 | async-start | bytes 32768 | tf_op jit(solution)/shard_map/all_to_all | solution.py:297
  274.0 13.8 %all-to-all-done.6 = f32[32,1,24]{2,1,0:T(1,128)S(1)} async-done(((f32[32,1,24]{2,1,0:T(1,128)}), f32[32,1,24]{2,1,0:T(1,128)S(1)}, u32[]{:S(2)}, u32[]{:S(2)}) %all-to-all-start.6) | async-done | bytes 3104 | tf_op jit(solution)/shard_map/all_to_all | solution.py:297
  287.9 1.0 shard_map.127
  288.9 3.7 %all-to-all-start.7 = ((f32[16,4,8]{2,1,0:T(4,128)}), f32[16,4,8]{2,1,0:T(4,128)S(1)}, u32[]{:S(2)}, u32[]{:S(2)}) async-start(f32[16,4,8]{2,1,0:T(4,128)} %bitcast.48), calls=%async_computation.7 | async-start | bytes 65536 | tf_op jit(solution)/shard_map/all_to_all | solution.py:297
  294.0 5.5 %all-to-all-done.7 = f32[16,4,8]{2,1,0:T(4,128)S(1)} async-done(((f32[16,4,8]{2,1,0:T(4,128)}), f32[16,4,8]{2,1,0:T(4,128)S(1)}, u32[]{:S(2)}, u32[]{:S(2)}) %all-to-all-start.7) | async-done | bytes 2080 | tf_op jit(solution)/shard_map/all_to_all | solution.py:297
  299.9 0.7 copy.88
  (78 shorter events, 7.1 us)
Async XLA Ops:
  8.0 0.9 copy-start.5
  39.2 23.5 %copy-start.6 = (bf16[2,64,320]{2,1,0:T(8,128)(2,1)S(1)}, bf16[2,64,320]{2,1,0:T(8,128)(2,1)}, u32[]{:S(2)}) copy-start(bf16[2,64,320]{2,1,0:T(8,128)(2,1)} %param.10) | copy-start | bytes 245764
  39.2 23.6 %copy-start.9 = (bf16[320]{0:T(512)(128)(2,1)S(1)}, bf16[320]{0:T(512)(128)(2,1)}, u32[]{:S(2)}) copy-start(bf16[320]{0:T(512)(128)(2,1)} %param.13) | copy-start | bytes 1924
  53.6 11.5 %collective-permute-start = (bf16[16,288,128]{2,1,0:T(8,128)(2,1)S(1)}, bf16[16,288,128]{2,1,0:T(8,128)(2,1)S(1)}, u32[]{:S(2)}, u32[]{:S(2)}) collective-permute-start(bf16[16,288,128]{2,1,0:T(8,128)(2,1)S(1)} %bitcast.50), channel_id=1, source_target_pairs={{0,16},{16,0},{32,48},{48,32},{64,80},{80,64},{96,112},{112,96},{1... | collective-permute-start | bytes 3538952 | tf_op jit(solution)/shard_map/ppermute | solution.py:293
  65.1 15.4 %copy-start.10 = (s32[4]{0:T(128)S(1)}, s32[4]{0:T(128)}, u32[]{:S(2)}) copy-start(s32[4]{0:T(128)} %param.12) | copy-start | bytes 52
  65.1 41.0 %copy-start.3 = (bf16[4,128,1024]{2,1,0:T(8,128)(2,1)S(1)}, bf16[4,128,1024]{2,1,0:T(8,128)(2,1)}, u32[]{:S(2)}) copy-start(bf16[4,128,1024]{2,1,0:T(8,128)(2,1)} %cache_ref.1) | copy-start | bytes 3145732
  66.1 1.0 copy-start.4
  67.1 39.0 %all-to-all-start.2 = ((bf16[16,8,3712]{2,1,0:T(8,128)(2,1)}), bf16[16,8,3712]{2,1,0:T(8,128)(2,1)S(1)}, u32[]{:S(2)}, u32[]{:S(2)}) async-start(bf16[16,8,3712]{2,1,0:T(8,128)(2,1)} %bitcast.53), calls=%async_computation.2 | async-start | bytes 1900544 | tf_op jit(solution)/shard_map/all_to_all | solution.py:297
  79.8 76.4 %all-gather.2.cloned.1.call-start = ((), (), s32[]{:S(2)}) async-start(), calls=%async_computation.8 | async-start | bytes 2027520 | tf_op jit(solution)/shard_map/all_gather | solution.py:332
  108.8 47.4 %all-to-all-start.3 = ((bf16[16,8,2560]{2,1,0:T(8,128)(2,1)}), bf16[16,8,2560]{2,1,0:T(8,128)(2,1)S(1)}, u32[]{:S(2)}, u32[]{:S(2)}) async-start(bf16[16,8,2560]{2,1,0:T(8,128)(2,1)} %broadcast_in_dim.32), calls=%async_computation.3 | async-start | bytes 1310720 | tf_op jit(solution)/shard_map/all_to_all | solution.py:297
  156.2 1.5 copy-start.2
  159.1 22.3 %all-to-all-start.4 = ((bf16[4,320,128]{2,1,0:T(8,128)(2,1)}), bf16[4,320,128]{2,1,0:T(8,128)(2,1)S(1)}, u32[]{:S(2)}, u32[]{:S(2)}) async-start(bf16[4,320,128]{2,1,0:T(8,128)(2,1)} %broadcast_in_dim.33), calls=%async_computation.4 | async-start | bytes 655360 | tf_op jit(solution)/shard_map/all_to_all | solution.py:297
  183.5 1.5 copy-start
  185.0 15.8 %copy-start.7 = (bf16[5120]{0:T(1024)(128)(2,1)S(1)}, bf16[5120]{0:T(1024)(128)(2,1)}, u32[]{:S(2)}) copy-start(bf16[5120]{0:T(1024)(128)(2,1)} %param.16) | copy-start | bytes 30724
  185.0 15.8 %copy-start.8 = (s32[1,64,2]{1,2,0:T(2,128)S(1)}, s32[1,64,2]{1,2,0:T(2,128)}, u32[]{:S(2)}) copy-start(s32[1,64,2]{1,2,0:T(2,128)} %param.18) | copy-start | bytes 1540
  185.0 78.5 %all-to-all-start.5 = ((bf16[128,80,128]{2,1,0:T(8,128)(2,1)}), bf16[128,80,128]{2,1,0:T(8,128)(2,1)S(1)}, u32[]{:S(2)}, u32[]{:S(2)}) async-start(bf16[128,80,128]{2,1,0:T(8,128)(2,1)} %copy-done), calls=%async_computation.5 | async-start | bytes 5242880 | tf_op jit(solution)/shard_map/all_to_all | solution.py:297
  263.5 1.7 copy-start.1
  268.8 19.0 %all-to-all-start.6 = ((f32[32,1,24]{2,1,0:T(1,128)}), f32[32,1,24]{2,1,0:T(1,128)S(1)}, u32[]{:S(2)}, u32[]{:S(2)}) async-start(f32[32,1,24]{2,1,0:T(1,128)} %copy.84), calls=%async_computation.6 | async-start | bytes 32768 | tf_op jit(solution)/shard_map/all_to_all | solution.py:297
  288.9 10.6 %all-to-all-start.7 = ((f32[16,4,8]{2,1,0:T(4,128)}), f32[16,4,8]{2,1,0:T(4,128)S(1)}, u32[]{:S(2)}, u32[]{:S(2)}) async-start(f32[16,4,8]{2,1,0:T(4,128)} %bitcast.48), calls=%async_computation.7 | async-start | bytes 65536 | tf_op jit(solution)/shard_map/all_to_all | solution.py:297
Sparse Core Ops, SparseCore 0:
  83.9 72.2 all-gather.1

commit v4 on v3

--- a/solution.py
+++ b/solution.py
@@ -61,7 +61,17 @@
     return jnp.concatenate([piece[:rows], piece[rows : 2 * rows], tail], axis=1)
 
 
-def pack_kernel(rank_ref, weights_ref, table_ref, out_ref):
+def pack_kernel(rank_ref, weights_ref, table_ref, wout_ref, out_ref, rest_ref):
+    few, most = wout_ref[0:16].astype(f32), wout_ref[16:80].astype(f32)
+    for at, value in ((288, few), (0, most)):
+        ref = rest_ref if at == 0 else out_ref
+        rows = value.shape[0]
+        ref[at : at + rows, :] = value[:, 0:128].astype(bf16)
+        ref[at + rows : at + 2 * rows, :] = value[:, 128:256].astype(bf16)
+    tail = jnp.concatenate([few[:, 256:320], jnp.zeros((16, 64), f32)], axis=1)
+    out_ref[320:336, :] = tail.astype(bf16)
+    tail = jnp.concatenate([most[0:32, 256:320], most[32:64, 256:320]], axis=1)
+    rest_ref[128:160, :] = tail.astype(bf16)
     turned = weights_ref[...].astype(f32).T
     out_ref[0:112, :] = turned[:, 0:128].astype(bf16)
     out_ref[112:224, :] = turned[:, 128:256].astype(bf16)
@@ -102,7 +112,7 @@
             a = own_ref[x * 4 + z]
             b = other_ref[x * 4 + z]
             for c, piece in enumerate((jnp.where(core == 0, a, b), jnp.where(core == 0, b, a))):
-                pieces.append(unpack(piece, 112))
+                pieces.append(unpack(piece[:288], 112))
                 table = piece[272:288].astype(f32)
                 for j in range(2):
                     mine = jnp.where(lane == 64 + 2 * me + j, table, 0.0)
@@ -125,9 +135,26 @@
     out_ref[:, QKV:] = extra.astype(bf16)
 
 
-def output_kernel(mixed_ref, weights_ref, x_ref, rows_ref, packed_ref):
-    part = jnp.dot(mixed_ref[...], weights_ref[...], preferred_element_type=f32)
-    rows = (x_ref[...].astype(f32) + part).astype(bf16)
+def output_kernel(me_ref, mixed_ref, own_ref, other_ref, rest_ref, x_ref, rows_ref, packed_ref):
+    core = lax.rem(me_ref[0], 2)
+    part = jnp.zeros((128, 384), f32)
+    for z in range(4):
+        weights = []
+        for g in range(8 * z, 8 * z + 8):
+            place = g // 2 % 4 * 4 + z
+            a, b = own_ref[place, 288:336, :], other_ref[place, 288:336, :]
+            few = jnp.where(core == g % 2, a, b)
+            weights.append(jnp.concatenate([few[0:16], few[16:32], few[32:48]], axis=1))
+            rest = rest_ref[g]
+            tail = rest[128:160]
+            tail = jnp.concatenate([tail, swap_halves(tail.astype(f32)).astype(bf16)], axis=0)
+            weights.append(jnp.concatenate([rest[0:64], rest[64:128], tail], axis=1))
+        part = part + jnp.dot(
+            mixed_ref[:, 640 * z : 640 * z + 640],
+            jnp.concatenate(weights, axis=0),
+            preferred_element_type=f32,
+        )
+    rows = (x_ref[...].astype(f32) + part[:, :320]).astype(bf16)
     rows_ref[...] = rows
     packed_ref[0:128, :] = rows[:, 0:128]
     packed_ref[128:256, :] = rows[:, 128:256]
@@ -329,11 +356,17 @@
     me = lax.axis_index("gen").astype(i32)
     features = D // TP
 
-    out_whole = lax.all_gather(wout, "gen", axis=0, tiled=True)
     table = jnp.concatenate([kept[0], chosen.T], axis=1)
-    piece = call(
-        pack_kernel, shape((288, 128), bf16), rank.reshape(1), wqkv, table, scalars=1
-    )
+    piece, rest = call(
+        pack_kernel,
+        (shape((336, 128), bf16), shape((160, 128), bf16)),
+        rank.reshape(1),
+        wqkv,
+        table,
+        wout,
+        scalars=1,
+    )
+    rest = lax.all_gather(rest, "gen")
     own_w, other_w = gather_gen(piece)
 
     x = embeddings.reshape(STEPS, TP, OWN, features).transpose(1, 0, 2, 3).reshape(128, features)
@@ -347,6 +380,7 @@
         other_w,
         scalars=1,
     )
+    parts, rest = lax.optimization_barrier((parts, rest))
     parts = all_to_all(parts.reshape(TP, 8, QKV + 128), "tp")
 
     meta = meta.reshape(2, 16, 128)[:, :6, 32:64].astype(i32).reshape(2, 3, 2, GEN)
@@ -372,9 +406,13 @@
     layer_out, packed = call(
         output_kernel,
         (shape((128, features), bf16), shape((320, 128), bf16)),
+        me.reshape(1),
         mixed,
-        out_whole,
+        own_w,
+        other_w,
+        rest,
         x,
+        scalars=1,
     )
     last_hidden = layer_out.reshape(TP, STEPS, OWN, features)[:, -1].reshape(ROWS, features)
 

time: 308 us -> 317 us (1.029)
  waiting for transfers between devices: 168 us -> 173 us
    all_to_all x6, waiting for transfers between devices: 121 us -> 138 us  [all_to_all(): lax.all_to_all(value, axis, split_axis=0, concat_axis=0, tiled=True, axis...]
    all_gather x1, waiting for transfers between devices: 43.3 us -> 31.3 us  [body(): rest = lax.all_gather(rest, 'gen')]
    all_to_all x6, starting transfers between devices: 46.2 us -> 51.1 us  [all_to_all(): lax.all_to_all(value, axis, split_axis=0, concat_axis=0, tiled=True, axis...]
    unnamed x24 -> x26, local copies, waits for them, and re-layouts: 7.29 us -> 7.8 us
  transfers between devices with their start and end apart: 8 -> 8, of which waited for: 7 -> 8; matrix products, arithmetic and copies ran while one was open for 2% -> 2% of each run, Pallas kernels for 1% -> 0%
where the time goes in v4:
time: 317 us; the launch traced here: 316 us
  waiting for transfers between devices  173 us (55%)
  starting transfers between devices  57.3 us (18%)
  blocking collectives  42.6 us (13%)
  local copies, waits for them, and re-layouts  15.9 us (5%)
  between operations  14.3 us (5%)
  Pallas kernels  11.2 us (4%)
    all_to_all x6, waiting for transfers between devices, all_to_all(): lax.all_to_all(value, axis, split_axis=0, concat_axis=0, tiled=True, axis...  138 us
    all_to_all x6, starting transfers between devices, all_to_all(): lax.all_to_all(value, axis, split_axis=0, concat_axis=0, tiled=True, axis...  51.1 us
    all_to_all x2, blocking collectives, all_to_all(): lax.all_to_all(value, axis, split_axis=0, concat_axis=0, tiled=True, axis...  42.6 us
    all_gather x1, waiting for transfers between devices, body(): rest = lax.all_gather(rest, 'gen')  31.3 us
    pallas_call x7, Pallas kernels, call(): pl.pallas_call(kernel, out_shape=out_shape, in_specs=specs, out_specs=jax...  11.2 us
    unnamed x26, local copies, waits for them, and re-layouts  7.8 us
  transfers between devices with their start and end apart: 8, of which 8 were waited for; matrix products, arithmetic and copies ran while one was open for 2% of the time, Pallas kernels for 0%

profile of v4, /device:TPU:1, one launch (start us, length us, event | category | flops | bytes accessed | tf_op | source)
XLA Modules:
  0.0 315.8 jit_solution(17744645928905355519)
XLA Ops:
  8.0 0.9 copy-done.5
  8.9 0.8 copy-done.6
  9.7 0.8 shard_map.121
  10.5 0.8 broadcast_in_dim.28
  11.3 15.6 %all-to-all-start = ((bf16[4,336,128]{2,1,0:T(8,128)(2,1)}), bf16[4,336,128]{2,1,0:T(8,128)(2,1)S(1)}, u32[]{:S(2)}, u32[]{:S(2)}) async-start(bf16[4,336,128]{2,1,0:T(8,128)(2,1)} %broadcast_in_dim.28), calls=%async_computation | async-start | bytes 688128 | tf_op jit(solution)/shard_map/all_to_all | solution.py:324
  27.6 16.4 %all-to-all-done = bf16[4,336,128]{2,1,0:T(8,128)(2,1)S(1)} async-done(((bf16[4,336,128]{2,1,0:T(8,128)(2,1)}), bf16[4,336,128]{2,1,0:T(8,128)(2,1)S(1)}, u32[]{:S(2)}, u32[]{:S(2)}) %all-to-all-start) | async-done | bytes 344096 | tf_op jit(solution)/shard_map/all_to_all | solution.py:324
  44.3 19.7 %all_to_all.40 = bf16[4,4,336,128]{3,2,1,0:T(8,128)(2,1)S(1)} all-to-all(bf16[4,4,336,128]{3,2,1,0:T(8,128)(2,1)S(1)} %broadcast_in_dim.29), channel_id=1, replica_groups={{0,32,64,96},{16,48,80,112},{128,160,192,224},{144,176,208,240},{256,28..., dimensions={0} | all-to-all | bytes 2752512 | tf_op jit(solution)/shard_map/all_to_all | solution.py:324
  64.0 6.2 %collective-permute-start = (bf16[16,336,128]{2,1,0:T(8,128)(2,1)S(1)}, bf16[16,336,128]{2,1,0:T(8,128)(2,1)S(1)}, u32[]{:S(2)}, u32[]{:S(2)}) collective-permute-start(bf16[16,336,128]{2,1,0:T(8,128)(2,1)S(1)} %bitcast.50), channel_id=1, source_target_pairs={{0,16},{16,0},{32,48},{48,32},{64,80},{80,64},{96,112},{112,96},{1... | collective-permute-start | bytes 4128776 | tf_op jit(solution)/shard_map/ppermute | solution.py:320
  70.4 2.6 collective-permute-done.other_ref
  72.9 1.0 shard_map.122
  73.9 0.9 copy-done.4
  74.9 31.3 %all-gather.3.cloned.1.call-done = bf16[5120,128]{1,0:T(8,128)(2,1)} async-done(((bf16[160,128]{1,0:T(8,128)(2,1)}), bf16[5120,128]{1,0:T(8,128)(2,1)}) %all-gather.3.cloned.1.call-update) | async-done | bytes 1310736 | tf_op jit(solution)/shard_map/all_gather | solution.py:369
  106.2 6.0 %all-to-all-start.2 = ((bf16[16,8,3712]{2,1,0:T(8,128)(2,1)}), bf16[16,8,3712]{2,1,0:T(8,128)(2,1)}, u32[]{:S(2)}, u32[]{:S(2)}) async-start(bf16[16,8,3712]{2,1,0:T(8,128)(2,1)} %bitcast.56), calls=%async_computation.2 | async-start | bytes 1900544 | tf_op jit(solution)/shard_map/all_to_all | solution.py:324
  112.5 24.7 %all-to-all-done.2.parts_ref = bf16[16,8,3712]{2,1,0:T(8,128)(2,1)} async-done(((bf16[16,8,3712]{2,1,0:T(8,128)(2,1)}), bf16[16,8,3712]{2,1,0:T(8,128)(2,1)}, u32[]{:S(2)}, u32[]{:S(2)}) %all-to-all-start.2) | async-done | bytes 950304 | tf_op jit(solution)/shard_map/all_to_all | solution.py:324
  137.3 1.2 copy-done.3
  138.5 3.0 shard_map.123
  141.5 23.0 %all_to_all.41 = bf16[16,8,2560]{2,1,0:T(8,128)(2,1)S(1)} all-to-all(bf16[16,8,2560]{2,1,0:T(8,128)(2,1)S(1)} %broadcast_in_dim.32), channel_id=1, replica_groups=mesh['gen'=32,'tp'=16] {'tp'}, dimensions={0} | all-to-all | bytes 1310720 | tf_op jit(solution)/shard_map/all_to_all | solution.py:324
  165.1 0.8 broadcast_in_dim.33
  165.9 7.4 %all-to-all-start.4 = ((bf16[4,320,128]{2,1,0:T(8,128)(2,1)}), bf16[4,320,128]{2,1,0:T(8,128)(2,1)S(1)}, u32[]{:S(2)}, u32[]{:S(2)}) async-start(bf16[4,320,128]{2,1,0:T(8,128)(2,1)} %broadcast_in_dim.33), calls=%async_computation.4 | async-start | bytes 655360 | tf_op jit(solution)/shard_map/all_to_all | solution.py:324
  174.1 0.8 slice.36
  176.4 15.7 %all-to-all-done.4.layer_ref = bf16[4,320,128]{2,1,0:T(8,128)(2,1)S(1)} async-done(((bf16[4,320,128]{2,1,0:T(8,128)(2,1)}), bf16[4,320,128]{2,1,0:T(8,128)(2,1)S(1)}, u32[]{:S(2)}, u32[]{:S(2)}) %all-to-all-start.4) | async-done | bytes 327712 | tf_op jit(solution)/shard_map/all_to_all | solution.py:324
  192.1 2.2 shard_map.125
  194.2 1.5 copy-done
  195.7 13.4 %all-to-all-start.5 = ((bf16[128,80,128]{2,1,0:T(8,128)(2,1)}), bf16[128,80,128]{2,1,0:T(8,128)(2,1)S(1)}, u32[]{:S(2)}, u32[]{:S(2)}) async-start(bf16[128,80,128]{2,1,0:T(8,128)(2,1)} %copy-done), calls=%async_computation.5 | async-start | bytes 5242880 | tf_op jit(solution)/shard_map/all_to_all | solution.py:324
  209.8 62.0 %all-to-all-done.5 = bf16[128,80,128]{2,1,0:T(8,128)(2,1)S(1)} async-done(((bf16[128,80,128]{2,1,0:T(8,128)(2,1)}), bf16[128,80,128]{2,1,0:T(8,128)(2,1)S(1)}, u32[]{:S(2)}, u32[]{:S(2)}) %all-to-all-start.5) | async-done | bytes 2621472 | tf_op jit(solution)/shard_map/all_to_all | solution.py:324
  271.8 1.7 copy-done.1
  273.5 2.6 shard_map.126
  277.1 5.2 %all-to-all-start.6 = ((f32[32,1,24]{2,1,0:T(1,128)}), f32[32,1,24]{2,1,0:T(1,128)S(1)}, u32[]{:S(2)}, u32[]{:S(2)}) async-start(f32[32,1,24]{2,1,0:T(1,128)} %copy.84), calls=%async_computation.6 | async-start | bytes 32768 | tf_op jit(solution)/shard_map/all_to_all | solution.py:324
  282.6 13.8 %all-to-all-done.6 = f32[32,1,24]{2,1,0:T(1,128)S(1)} async-done(((f32[32,1,24]{2,1,0:T(1,128)}), f32[32,1,24]{2,1,0:T(1,128)S(1)}, u32[]{:S(2)}, u32[]{:S(2)}) %all-to-all-start.6) | async-done | bytes 3104 | tf_op jit(solution)/shard_map/all_to_all | solution.py:324
  296.5 1.0 shard_map.127
  297.5 3.5 %all-to-all-start.7 = ((f32[16,4,8]{2,1,0:T(4,128)}), f32[16,4,8]{2,1,0:T(4,128)S(1)}, u32[]{:S(2)}, u32[]{:S(2)}) async-start(f32[16,4,8]{2,1,0:T(4,128)} %bitcast.49), calls=%async_computation.7 | async-start | bytes 65536 | tf_op jit(solution)/shard_map/all_to_all | solution.py:324
  302.4 5.5 %all-to-all-done.7 = f32[16,4,8]{2,1,0:T(4,128)S(1)} async-done(((f32[16,4,8]{2,1,0:T(4,128)}), f32[16,4,8]{2,1,0:T(4,128)S(1)}, u32[]{:S(2)}, u32[]{:S(2)}) %all-to-all-start.7) | async-done | bytes 2080 | tf_op jit(solution)/shard_map/all_to_all | solution.py:324
  (80 shorter events, 9.5 us)
Async XLA Ops:
  8.0 0.9 copy-start.5
  8.9 0.8 copy-start.6
  11.3 32.8 %all-to-all-start = ((bf16[4,336,128]{2,1,0:T(8,128)(2,1)}), bf16[4,336,128]{2,1,0:T(8,128)(2,1)S(1)}, u32[]{:S(2)}, u32[]{:S(2)}) async-start(bf16[4,336,128]{2,1,0:T(8,128)(2,1)} %broadcast_in_dim.28), calls=%async_computation | async-start | bytes 688128 | tf_op jit(solution)/shard_map/all_to_all | solution.py:324
  26.9 79.3 %all-gather.3.cloned.1.call-start = ((), (), s32[]{:S(2)}) async-start(), calls=%async_computation.8 | async-start | bytes 1351680 | tf_op jit(solution)/shard_map/all_gather | solution.py:369
  44.3 25.9 %copy-start.7 = (bf16[2,64,320]{2,1,0:T(8,128)(2,1)S(1)}, bf16[2,64,320]{2,1,0:T(8,128)(2,1)}, u32[]{:S(2)}) copy-start(bf16[2,64,320]{2,1,0:T(8,128)(2,1)} %param.10) | copy-start | bytes 245764
  44.3 26.1 %copy-start.10 = (bf16[320]{0:T(512)(128)(2,1)S(1)}, bf16[320]{0:T(512)(128)(2,1)}, u32[]{:S(2)}) copy-start(bf16[320]{0:T(512)(128)(2,1)} %param.13) | copy-start | bytes 1924
  64.0 9.0 %collective-permute-start = (bf16[16,336,128]{2,1,0:T(8,128)(2,1)S(1)}, bf16[16,336,128]{2,1,0:T(8,128)(2,1)S(1)}, u32[]{:S(2)}, u32[]{:S(2)}) collective-permute-start(bf16[16,336,128]{2,1,0:T(8,128)(2,1)S(1)} %bitcast.50), channel_id=1, source_target_pairs={{0,16},{16,0},{32,48},{48,32},{64,80},{80,64},{96,112},{112,96},{1... | collective-permute-start | bytes 4128776 | tf_op jit(solution)/shard_map/ppermute | solution.py:320
  73.9 0.9 copy-start.4
  74.8 37.3 %copy-start.11 = (s32[4]{0:T(128)S(1)}, s32[4]{0:T(128)}, u32[]{:S(2)}) copy-start(s32[4]{0:T(128)} %param.12) | copy-start | bytes 52
  106.2 31.0 %all-to-all-start.2 = ((bf16[16,8,3712]{2,1,0:T(8,128)(2,1)}), bf16[16,8,3712]{2,1,0:T(8,128)(2,1)}, u32[]{:S(2)}, u32[]{:S(2)}) async-start(bf16[16,8,3712]{2,1,0:T(8,128)(2,1)} %bitcast.56), calls=%async_computation.2 | async-start | bytes 1900544 | tf_op jit(solution)/shard_map/all_to_all | solution.py:324
  137.3 1.2 copy-start.3
  141.5 23.0 %copy-start.2 = (bf16[5120,128]{1,0:T(8,128)(2,1)S(1)}, bf16[5120,128]{1,0:T(8,128)(2,1)}, u32[]{:S(2)}) copy-start(bf16[5120,128]{1,0:T(8,128)(2,1)} %all-gather.3.cloned.1.call-done) | copy-start | bytes 3932164
  165.9 26.2 %all-to-all-start.4 = ((bf16[4,320,128]{2,1,0:T(8,128)(2,1)}), bf16[4,320,128]{2,1,0:T(8,128)(2,1)S(1)}, u32[]{:S(2)}, u32[]{:S(2)}) async-start(bf16[4,320,128]{2,1,0:T(8,128)(2,1)} %broadcast_in_dim.33), calls=%async_computation.4 | async-start | bytes 655360 | tf_op jit(solution)/shard_map/all_to_all | solution.py:324
  194.2 1.5 copy-start
  195.7 13.4 %copy-start.8 = (bf16[5120]{0:T(1024)(128)(2,1)S(1)}, bf16[5120]{0:T(1024)(128)(2,1)}, u32[]{:S(2)}) copy-start(bf16[5120]{0:T(1024)(128)(2,1)} %param.16) | copy-start | bytes 30724
  195.7 13.4 %copy-start.9 = (s32[1,64,2]{1,2,0:T(2,128)S(1)}, s32[1,64,2]{1,2,0:T(2,128)}, u32[]{:S(2)}) copy-start(s32[1,64,2]{1,2,0:T(2,128)} %param.18) | copy-start | bytes 1540
  195.7 76.0 %all-to-all-start.5 = ((bf16[128,80,128]{2,1,0:T(8,128)(2,1)}), bf16[128,80,128]{2,1,0:T(8,128)(2,1)S(1)}, u32[]{:S(2)}, u32[]{:S(2)}) async-start(bf16[128,80,128]{2,1,0:T(8,128)(2,1)} %copy-done), calls=%async_computation.5 | async-start | bytes 5242880 | tf_op jit(solution)/shard_map/all_to_all | solution.py:324
  271.8 1.7 copy-start.1
  277.1 19.3 %all-to-all-start.6 = ((f32[32,1,24]{2,1,0:T(1,128)}), f32[32,1,24]{2,1,0:T(1,128)S(1)}, u32[]{:S(2)}, u32[]{:S(2)}) async-start(f32[32,1,24]{2,1,0:T(1,128)} %copy.84), calls=%async_computation.6 | async-start | bytes 32768 | tf_op jit(solution)/shard_map/all_to_all | solution.py:324
  297.5 10.3 %all-to-all-start.7 = ((f32[16,4,8]{2,1,0:T(4,128)}), f32[16,4,8]{2,1,0:T(4,128)S(1)}, u32[]{:S(2)}, u32[]{:S(2)}) async-start(f32[16,4,8]{2,1,0:T(4,128)} %bitcast.49), calls=%async_computation.7 | async-start | bytes 65536 | tf_op jit(solution)/shard_map/all_to_all | solution.py:324
Sparse Core Ops, SparseCore 0:
  31.4 74.6 all-gather.2

commit v5 on v3

--- a/solution.py
+++ b/solution.py
@@ -61,7 +61,12 @@
     return jnp.concatenate([piece[:rows], piece[rows : 2 * rows], tail], axis=1)
 
 
-def pack_kernel(rank_ref, weights_ref, table_ref, out_ref):
+def pack_kernel(rank_ref, weights_ref, table_ref, wout_ref, out_ref):
+    wide = wout_ref[...].astype(f32)
+    out_ref[288:368, :] = wide[:, 0:128].astype(bf16)
+    out_ref[368:448, :] = wide[:, 128:256].astype(bf16)
+    tail = jnp.concatenate([wide[0:48, 256:320], wide[32:80, 256:320]], axis=1)
+    out_ref[448:496, :] = tail.astype(bf16)
     turned = weights_ref[...].astype(f32).T
     out_ref[0:112, :] = turned[:, 0:128].astype(bf16)
     out_ref[112:224, :] = turned[:, 128:256].astype(bf16)
@@ -126,8 +131,21 @@
 
 
 def output_kernel(mixed_ref, weights_ref, x_ref, rows_ref, packed_ref):
-    part = jnp.dot(mixed_ref[...], weights_ref[...], preferred_element_type=f32)
-    rows = (x_ref[...].astype(f32) + part).astype(bf16)
+    part = jnp.zeros((128, 384), f32)
+    for z in range(4):
+        weights = []
+        for g in range(8):
+            piece = weights_ref[g, z]
+            tail = piece[160:208]
+            other = swap_halves(tail.astype(f32)).astype(bf16)
+            tail = jnp.concatenate([tail, other[16:48]], axis=0)
+            weights.append(jnp.concatenate([piece[0:80], piece[80:160], tail], axis=1))
+        part = part + jnp.dot(
+            mixed_ref[:, 640 * z : 640 * z + 640],
+            jnp.concatenate(weights, axis=0),
+            preferred_element_type=f32,
+        )
+    rows = (x_ref[...].astype(f32) + part[:, :320]).astype(bf16)
     rows_ref[...] = rows
     packed_ref[0:128, :] = rows[:, 0:128]
     packed_ref[128:256, :] = rows[:, 128:256]
@@ -286,11 +304,7 @@
 LAYERS = [[z * 128 + i for i in range(128)] for z in range(4)]
 
 
-def gather_gen(piece):
-    along_z = spread(piece, "gen", 4, Z_GROUPS)
-    along_x = spread(along_z, "gen", 4, X_GROUPS)
-    own = along_x.reshape((16,) + piece.shape)
-    return own, lax.ppermute(own, "gen", [(g, g ^ 1) for g in range(GEN)])
+XC_GROUPS = [[z * 8 + i for i in range(8)] for z in range(4)]
 
 
 def all_to_all(value, axis, groups=None):
@@ -329,12 +343,14 @@
     me = lax.axis_index("gen").astype(i32)
     features = D // TP
 
-    out_whole = lax.all_gather(wout, "gen", axis=0, tiled=True)
     table = jnp.concatenate([kept[0], chosen.T], axis=1)
     piece = call(
-        pack_kernel, shape((288, 128), bf16), rank.reshape(1), wqkv, table, scalars=1
-    )
-    own_w, other_w = gather_gen(piece)
+        pack_kernel, shape((496, 128), bf16), rank.reshape(1), wqkv, table, wout, scalars=1
+    )
+    along_z = spread(piece, "gen", 4, Z_GROUPS)
+    out_whole = lax.all_gather(along_z[:, 288:], "gen", axis_index_groups=XC_GROUPS)
+    own_w = spread(along_z[:, :288], "gen", 4, X_GROUPS).reshape(16, 288, 128)
+    other_w = lax.ppermute(own_w, "gen", [(g, g ^ 1) for g in range(GEN)])
 
     x = embeddings.reshape(STEPS, TP, OWN, features).transpose(1, 0, 2, 3).reshape(128, features)
     parts, meta = call(

time: 308 us -> 288 us (0.935)
  waiting for transfers between devices: 168 us -> 141 us
  blocking collectives: 44.3 us -> 60 us
  starting transfers between devices: 55.2 us -> 44.5 us
    all_gather x1, waiting for transfers between devices: 43.3 us -> 0.02 us  [body(): lax.all_gather(along_z[:, 288:], 'gen', axis_index_groups=XC_GROUPS)]
    all_to_all x6, waiting for transfers between devices: 121 us -> 138 us  [all_to_all(): lax.all_to_all(value, axis, split_axis=0, concat_axis=0, tiled=True, axis...]
    all_to_all x2, blocking collectives: 44.3 us -> 60 us  [all_to_all(): lax.all_to_all(value, axis, split_axis=0, concat_axis=0, tiled=True, axis...]
    all_to_all x6, starting transfers between devices: 46.2 us -> 40 us  [all_to_all(): lax.all_to_all(value, axis, split_axis=0, concat_axis=0, tiled=True, axis...]
    ppermute x1, starting transfers between devices: 9.02 us -> 4.47 us  [body(): other_w = lax.ppermute(own_w, 'gen', [(g, g ^ 1) for g in range(GEN)])]
where the time goes in v5:
time: 288 us; the launch traced here: 287 us
  waiting for transfers between devices  141 us (49%)
  blocking collectives  60 us (21%)
  starting transfers between devices  44.5 us (15%)
  local copies, waits for them, and re-layouts  15.3 us (5%)
  between operations  14.4 us (5%)
  Pallas kernels  10.4 us (4%)
    all_to_all x6, waiting for transfers between devices, all_to_all(): lax.all_to_all(value, axis, split_axis=0, concat_axis=0, tiled=True, axis...  138 us
    all_to_all x2, blocking collectives, all_to_all(): lax.all_to_all(value, axis, split_axis=0, concat_axis=0, tiled=True, axis...  60 us
    all_to_all x6, starting transfers between devices, all_to_all(): lax.all_to_all(value, axis, split_axis=0, concat_axis=0, tiled=True, axis...  40 us
    pallas_call x7, Pallas kernels, call(): pl.pallas_call(kernel, out_shape=out_shape, in_specs=specs, out_specs=jax...  10.4 us
    unnamed x24, local copies, waits for them, and re-layouts  7.09 us
  transfers between devices with their start and end apart: 8, of which 7 were waited for; matrix products, arithmetic and copies ran while one was open for 2% of the time, Pallas kernels for 1%

profile of v5, /device:TPU:1, one launch (start us, length us, event | category | flops | bytes accessed | tf_op | source)
XLA Modules:
  0.0 287.1 jit_solution(17464488459673116811)
XLA Ops:
  7.2 0.7 pad_add_fusion
  8.0 0.9 copy-done.4
  8.9 0.8 copy-done.5
  10.0 41.3 %all_to_all.40 = bf16[4,496,128]{2,1,0:T(8,128)(2,1)S(1)} all-to-all(bf16[4,496,128]{2,1,0:T(8,128)(2,1)S(1)} %broadcast_in_dim.28), channel_id=1, replica_groups={{0,128,256,384},{16,144,272,400},{32,160,288,416},{48,176,304,432},{64,..., dimensions={0} | all-to-all | bytes 1015808 | tf_op jit(solution)/shard_map/all_to_all | solution.py:311
  51.6 18.7 %all_to_all.41 = bf16[4,4,288,128]{3,2,1,0:T(8,128)(2,1)S(1)} all-to-all(bf16[4,4,288,128]{3,2,1,0:T(8,128)(2,1)S(1)} %broadcast_in_dim.29), channel_id=1, replica_groups={{0,32,64,96},{16,48,80,112},{128,160,192,224},{144,176,208,240},{256,28..., dimensions={0} | all-to-all | bytes 2359296 | tf_op jit(solution)/shard_map/all_to_all | solution.py:311
  70.3 4.5 %collective-permute-start = (bf16[16,288,128]{2,1,0:T(8,128)(2,1)S(1)}, bf16[16,288,128]{2,1,0:T(8,128)(2,1)S(1)}, u32[]{:S(2)}, u32[]{:S(2)}) collective-permute-start(bf16[16,288,128]{2,1,0:T(8,128)(2,1)S(1)} %bitcast.51), channel_id=1, source_target_pairs={{0,16},{16,0},{32,48},{48,32},{64,80},{80,64},{96,112},{112,96},{1... | collective-permute-start | bytes 3538952 | tf_op jit(solution)/shard_map/ppermute | solution.py:353
  74.9 2.3 collective-permute-done.other_ref
  77.2 2.0 shard_map.122
  79.2 10.7 %all-to-all-start.2 = ((bf16[16,8,3712]{2,1,0:T(8,128)(2,1)}), bf16[16,8,3712]{2,1,0:T(8,128)(2,1)S(1)}, u32[]{:S(2)}, u32[]{:S(2)}) async-start(bf16[16,8,3712]{2,1,0:T(8,128)(2,1)} %bitcast.6), calls=%async_computation.2 | async-start | bytes 1900544 | tf_op jit(solution)/shard_map/all_to_all | solution.py:311
  90.2 0.7 slice.45
  91.1 23.7 %all-to-all-done.2.parts_ref = bf16[16,8,3712]{2,1,0:T(8,128)(2,1)S(1)} async-done(((bf16[16,8,3712]{2,1,0:T(8,128)(2,1)}), bf16[16,8,3712]{2,1,0:T(8,128)(2,1)S(1)}, u32[]{:S(2)}, u32[]{:S(2)}) %all-to-all-start.2) | async-done | bytes 950304 | tf_op jit(solution)/shard_map/all_to_all | solution.py:311
  114.9 1.8 shard_map.123
  116.7 0.9 broadcast_in_dim.32
  117.6 4.3 %all-to-all-start.3 = ((bf16[16,8,2560]{2,1,0:T(8,128)(2,1)}), bf16[16,8,2560]{2,1,0:T(8,128)(2,1)S(1)}, u32[]{:S(2)}, u32[]{:S(2)}) async-start(bf16[16,8,2560]{2,1,0:T(8,128)(2,1)} %broadcast_in_dim.32), calls=%async_computation.3 | async-start | bytes 1310720 | tf_op jit(solution)/shard_map/all_to_all | solution.py:311
  122.0 18.5 %all-to-all-done.3 = bf16[16,8,2560]{2,1,0:T(8,128)(2,1)S(1)} async-done(((bf16[16,8,2560]{2,1,0:T(8,128)(2,1)}), bf16[16,8,2560]{2,1,0:T(8,128)(2,1)S(1)}, u32[]{:S(2)}, u32[]{:S(2)}) %all-to-all-start.3) | async-done | bytes 655392 | tf_op jit(solution)/shard_map/all_to_all | solution.py:311
  140.5 1.5 copy-done.2
  142.6 0.8 broadcast_in_dim.33
  143.3 3.5 %all-to-all-start.4 = ((bf16[4,320,128]{2,1,0:T(8,128)(2,1)}), bf16[4,320,128]{2,1,0:T(8,128)(2,1)S(1)}, u32[]{:S(2)}, u32[]{:S(2)}) async-start(bf16[4,320,128]{2,1,0:T(8,128)(2,1)} %broadcast_in_dim.33), calls=%async_computation.4 | async-start | bytes 655360 | tf_op jit(solution)/shard_map/all_to_all | solution.py:311
  149.1 14.8 %all-to-all-done.4.layer_ref = bf16[4,320,128]{2,1,0:T(8,128)(2,1)S(1)} async-done(((bf16[4,320,128]{2,1,0:T(8,128)(2,1)}), bf16[4,320,128]{2,1,0:T(8,128)(2,1)S(1)}, u32[]{:S(2)}, u32[]{:S(2)}) %all-to-all-start.4) | async-done | bytes 327712 | tf_op jit(solution)/shard_map/all_to_all | solution.py:311
  163.9 2.2 shard_map.125
  166.1 1.5 copy-done
  167.6 12.5 %all-to-all-start.5 = ((bf16[128,80,128]{2,1,0:T(8,128)(2,1)}), bf16[128,80,128]{2,1,0:T(8,128)(2,1)S(1)}, u32[]{:S(2)}, u32[]{:S(2)}) async-start(bf16[128,80,128]{2,1,0:T(8,128)(2,1)} %copy-done), calls=%async_computation.5 | async-start | bytes 5242880 | tf_op jit(solution)/shard_map/all_to_all | solution.py:311
  180.8 62.0 %all-to-all-done.5 = bf16[128,80,128]{2,1,0:T(8,128)(2,1)S(1)} async-done(((bf16[128,80,128]{2,1,0:T(8,128)(2,1)}), bf16[128,80,128]{2,1,0:T(8,128)(2,1)S(1)}, u32[]{:S(2)}, u32[]{:S(2)}) %all-to-all-start.5) | async-done | bytes 2621472 | tf_op jit(solution)/shard_map/all_to_all | solution.py:311
  242.8 1.7 copy-done.1
  244.5 2.6 shard_map.126
  247.4 0.7 copy.84
  248.1 5.5 %all-to-all-start.6 = ((f32[32,1,24]{2,1,0:T(1,128)}), f32[32,1,24]{2,1,0:T(1,128)S(1)}, u32[]{:S(2)}, u32[]{:S(2)}) async-start(f32[32,1,24]{2,1,0:T(1,128)} %copy.84), calls=%async_computation.6 | async-start | bytes 32768 | tf_op jit(solution)/shard_map/all_to_all | solution.py:311
  253.9 13.8 %all-to-all-done.6 = f32[32,1,24]{2,1,0:T(1,128)S(1)} async-done(((f32[32,1,24]{2,1,0:T(1,128)}), f32[32,1,24]{2,1,0:T(1,128)S(1)}, u32[]{:S(2)}, u32[]{:S(2)}) %all-to-all-start.6) | async-done | bytes 3104 | tf_op jit(solution)/shard_map/all_to_all | solution.py:311
  267.8 1.0 shard_map.127
  268.9 3.5 %all-to-all-start.7 = ((f32[16,4,8]{2,1,0:T(4,128)}), f32[16,4,8]{2,1,0:T(4,128)S(1)}, u32[]{:S(2)}, u32[]{:S(2)}) async-start(f32[16,4,8]{2,1,0:T(4,128)} %bitcast.49), calls=%async_computation.7 | async-start | bytes 65536 | tf_op jit(solution)/shard_map/all_to_all | solution.py:311
  273.7 5.5 %all-to-all-done.7 = f32[16,4,8]{2,1,0:T(4,128)S(1)} async-done(((f32[16,4,8]{2,1,0:T(4,128)}), f32[16,4,8]{2,1,0:T(4,128)S(1)}, u32[]{:S(2)}, u32[]{:S(2)}) %all-to-all-start.7) | async-done | bytes 2080 | tf_op jit(solution)/shard_map/all_to_all | solution.py:311
  279.6 0.7 copy.88
  (80 shorter events, 7.2 us)
Async XLA Ops:
  8.0 0.9 copy-start.4
  8.9 0.8 copy-start.5
  51.4 23.4 %copy-start.9 = (bf16[320]{0:T(512)(128)(2,1)S(1)}, bf16[320]{0:T(512)(128)(2,1)}, u32[]{:S(2)}) copy-start(bf16[320]{0:T(512)(128)(2,1)} %param.13) | copy-start | bytes 1924
  51.4 23.4 %copy-start.6 = (bf16[2,64,320]{2,1,0:T(8,128)(2,1)S(1)}, bf16[2,64,320]{2,1,0:T(8,128)(2,1)}, u32[]{:S(2)}) copy-start(bf16[2,64,320]{2,1,0:T(8,128)(2,1)} %param.10) | copy-start | bytes 245764
  70.3 6.9 %collective-permute-start = (bf16[16,288,128]{2,1,0:T(8,128)(2,1)S(1)}, bf16[16,288,128]{2,1,0:T(8,128)(2,1)S(1)}, u32[]{:S(2)}, u32[]{:S(2)}) collective-permute-start(bf16[16,288,128]{2,1,0:T(8,128)(2,1)S(1)} %bitcast.51), channel_id=1, source_target_pairs={{0,16},{16,0},{32,48},{48,32},{64,80},{80,64},{96,112},{112,96},{1... | collective-permute-start | bytes 3538952 | tf_op jit(solution)/shard_map/ppermute | solution.py:353
  77.2 12.7 %copy-start.10 = (s32[4]{0:T(128)S(1)}, s32[4]{0:T(128)}, u32[]{:S(2)}) copy-start(s32[4]{0:T(128)} %param.12) | copy-start | bytes 52
  79.2 35.7 %copy-start.3 = (bf16[4,128,1024]{2,1,0:T(8,128)(2,1)S(1)}, bf16[4,128,1024]{2,1,0:T(8,128)(2,1)}, u32[]{:S(2)}) copy-start(bf16[4,128,1024]{2,1,0:T(8,128)(2,1)} %cache_ref.1) | copy-start | bytes 3145732
  79.2 35.7 %all-to-all-start.2 = ((bf16[16,8,3712]{2,1,0:T(8,128)(2,1)}), bf16[16,8,3712]{2,1,0:T(8,128)(2,1)S(1)}, u32[]{:S(2)}, u32[]{:S(2)}) async-start(bf16[16,8,3712]{2,1,0:T(8,128)(2,1)} %bitcast.6), calls=%async_computation.2 | async-start | bytes 1900544 | tf_op jit(solution)/shard_map/all_to_all | solution.py:311
  89.9 32.1 %all-gather.3.cloned.1.call-start = ((), (), s32[]{:S(2)}) async-start(), calls=%async_computation.8 | async-start | bytes 1916928 | tf_op jit(solution)/shard_map/all_gather | solution.py:351
  117.6 22.9 %all-to-all-start.3 = ((bf16[16,8,2560]{2,1,0:T(8,128)(2,1)}), bf16[16,8,2560]{2,1,0:T(8,128)(2,1)S(1)}, u32[]{:S(2)}, u32[]{:S(2)}) async-start(bf16[16,8,2560]{2,1,0:T(8,128)(2,1)} %broadcast_in_dim.32), calls=%async_computation.3 | async-start | bytes 1310720 | tf_op jit(solution)/shard_map/all_to_all | solution.py:311
  140.5 1.5 copy-start.2
  143.3 20.6 %all-to-all-start.4 = ((bf16[4,320,128]{2,1,0:T(8,128)(2,1)}), bf16[4,320,128]{2,1,0:T(8,128)(2,1)S(1)}, u32[]{:S(2)}, u32[]{:S(2)}) async-start(bf16[4,320,128]{2,1,0:T(8,128)(2,1)} %broadcast_in_dim.33), calls=%async_computation.4 | async-start | bytes 655360 | tf_op jit(solution)/shard_map/all_to_all | solution.py:311
  166.1 1.5 copy-start
  167.6 12.5 %copy-start.7 = (bf16[5120]{0:T(1024)(128)(2,1)S(1)}, bf16[5120]{0:T(1024)(128)(2,1)}, u32[]{:S(2)}) copy-start(bf16[5120]{0:T(1024)(128)(2,1)} %param.16) | copy-start | bytes 30724
  167.6 12.5 %copy-start.8 = (s32[1,64,2]{1,2,0:T(2,128)S(1)}, s32[1,64,2]{1,2,0:T(2,128)}, u32[]{:S(2)}) copy-start(s32[1,64,2]{1,2,0:T(2,128)} %param.18) | copy-start | bytes 1540
  167.6 75.2 %all-to-all-start.5 = ((bf16[128,80,128]{2,1,0:T(8,128)(2,1)}), bf16[128,80,128]{2,1,0:T(8,128)(2,1)S(1)}, u32[]{:S(2)}, u32[]{:S(2)}) async-start(bf16[128,80,128]{2,1,0:T(8,128)(2,1)} %copy-done), calls=%async_computation.5 | async-start | bytes 5242880 | tf_op jit(solution)/shard_map/all_to_all | solution.py:311
  242.8 1.7 copy-start.1
  248.1 19.7 %all-to-all-start.6 = ((f32[32,1,24]{2,1,0:T(1,128)}), f32[32,1,24]{2,1,0:T(1,128)S(1)}, u32[]{:S(2)}, u32[]{:S(2)}) async-start(f32[32,1,24]{2,1,0:T(1,128)} %copy.84), calls=%async_computation.6 | async-start | bytes 32768 | tf_op jit(solution)/shard_map/all_to_all | solution.py:311
  268.9 10.3 %all-to-all-start.7 = ((f32[16,4,8]{2,1,0:T(4,128)}), f32[16,4,8]{2,1,0:T(4,128)S(1)}, u32[]{:S(2)}, u32[]{:S(2)}) async-start(f32[16,4,8]{2,1,0:T(4,128)} %bitcast.49), calls=%async_computation.7 | async-start | bytes 65536 | tf_op jit(solution)/shard_map/all_to_all | solution.py:311
Sparse Core Ops, SparseCore 0:
  92.9 25.7 all-gather.2

commit v6 on v5

--- a/solution.py
+++ b/solution.py
@@ -26,19 +26,20 @@
 bf16 = jnp.bfloat16
 f32 = jnp.float32
 i32 = jnp.int32
-VMEM_BYTES = 48 * 1024 * 1024
-
-
-def call(kernel, out_shape, *args, scalars=0, scratch=()):
+MIB = 1024 * 1024
+
+
+def call(kernel, out_shape, *args, scalars=0, away=0, scratch=(), vmem=48):
     specs = [pl.BlockSpec(memory_space=pltpu.SMEM)] * scalars
-    specs += [pl.BlockSpec(memory_space=pltpu.VMEM)] * (len(args) - scalars)
+    specs += [pl.BlockSpec(memory_space=pltpu.VMEM)] * (len(args) - scalars - away)
+    specs += [pl.BlockSpec(memory_space=pl.ANY)] * away
     return pl.pallas_call(
         kernel,
         out_shape=out_shape,
         in_specs=specs,
         out_specs=jax.tree.map(lambda _: pl.BlockSpec(memory_space=pltpu.VMEM), out_shape),
         scratch_shapes=list(scratch),
-        compiler_params=pltpu.CompilerParams(vmem_limit_bytes=VMEM_BYTES),
+        compiler_params=pltpu.CompilerParams(vmem_limit_bytes=vmem * MIB),
     )(*args)
 
 
@@ -61,12 +62,15 @@
     return jnp.concatenate([piece[:rows], piece[rows : 2 * rows], tail], axis=1)
 
 
-def pack_kernel(rank_ref, weights_ref, table_ref, wout_ref, out_ref):
+def pack_out_kernel(wout_ref, out_ref):
     wide = wout_ref[...].astype(f32)
-    out_ref[288:368, :] = wide[:, 0:128].astype(bf16)
-    out_ref[368:448, :] = wide[:, 128:256].astype(bf16)
+    out_ref[0:80, :] = wide[:, 0:128].astype(bf16)
+    out_ref[80:160, :] = wide[:, 128:256].astype(bf16)
     tail = jnp.concatenate([wide[0:48, 256:320], wide[32:80, 256:320]], axis=1)
-    out_ref[448:496, :] = tail.astype(bf16)
+    out_ref[160:208, :] = tail.astype(bf16)
+
+
+def pack_kernel(rank_ref, weights_ref, table_ref, out_ref):
     turned = weights_ref[...].astype(f32).T
     out_ref[0:112, :] = turned[:, 0:128].astype(bf16)
     out_ref[112:224, :] = turned[:, 128:256].astype(bf16)
@@ -91,9 +95,13 @@
     out_ref[224:288, :] = jnp.concatenate([turned[0:64, 256:320], side], axis=1).astype(bf16)
 
 
-def project_kernel(me_ref, x_ref, gain_ref, own_ref, other_ref, out_ref, meta_ref):
+def project_kernel(me_ref, x_ref, gain_ref, away_ref, out_ref, meta_ref, pieces_ref, sems):
+    copies = [
+        pltpu.make_async_copy(away_ref.at[:, z], pieces_ref.at[z], sems.at[z]) for z in range(4)
+    ]
+    for copy in copies:
+        copy.start()
     me = me_ref[0]
-    core = lax.rem(me, 2)
     wide = x_ref[...].astype(f32)
     scaled = (wide * gain_ref[...].astype(f32)).astype(bf16)
     scaled = jnp.concatenate([scaled, jnp.zeros((128, 64), bf16)], axis=1)
@@ -102,19 +110,17 @@
     line = lax.rem(lax.broadcasted_iota(i32, (TP * 8, 128), 0), 8)
     extra = jnp.zeros((TP * 8, 128), f32)
     for z in range(4):
+        copies[z].wait()
         pieces = []
-        for x in range(4):
-            a = own_ref[x * 4 + z]
-            b = other_ref[x * 4 + z]
-            for c, piece in enumerate((jnp.where(core == 0, a, b), jnp.where(core == 0, b, a))):
-                pieces.append(unpack(piece, 112))
-                table = piece[272:288].astype(f32)
-                for j in range(2):
-                    mine = jnp.where(lane == 64 + 2 * me + j, table, 0.0)
-                    column = jnp.sum(mine, axis=1, keepdims=True)
-                    at = 32 + gen_index(z, x, c)
-                    metas[j] = jnp.where(lane == at, column, metas[j])
-        table = own_ref[lax.rem(me // 2, 4) * 4 + z][272:288].astype(f32)
+        for g in range(8):
+            piece = pieces_ref[z, g]
+            pieces.append(unpack(piece, 112))
+            table = piece[272:288].astype(f32)
+            for j in range(2):
+                mine = jnp.where(lane == 64 + 2 * me + j, table, 0.0)
+                column = jnp.sum(mine, axis=1, keepdims=True)
+                metas[j] = jnp.where(lane == 32 + 8 * z + g, column, metas[j])
+        table = pieces_ref[z, lax.rem(me, 8)][272:288].astype(f32)
         for slot in range(2):
             extra = jnp.where(line == 2 * z + slot, table[slot : slot + 1], extra)
         part = nt_dot(scaled, jnp.concatenate(pieces, axis=0))
@@ -130,12 +136,18 @@
     out_ref[:, QKV:] = extra.astype(bf16)
 
 
-def output_kernel(mixed_ref, weights_ref, x_ref, rows_ref, packed_ref):
+def output_kernel(mixed_ref, x_ref, away_ref, rows_ref, packed_ref, weights_ref, sems):
+    copies = [
+        pltpu.make_async_copy(away_ref.at[:, z], weights_ref.at[z], sems.at[z]) for z in range(4)
+    ]
+    for copy in copies:
+        copy.start()
     part = jnp.zeros((128, 384), f32)
     for z in range(4):
+        copies[z].wait()
         weights = []
         for g in range(8):
-            piece = weights_ref[g, z]
+            piece = weights_ref[z, g]
             tail = piece[160:208]
             other = swap_halves(tail.astype(f32)).astype(bf16)
             tail = jnp.concatenate([tail, other[16:48]], axis=0)
@@ -226,22 +238,32 @@
     out_ref[:, 64:80, :] = tails.astype(bf16).reshape(owners, 16, 128)
 
 
-def logits_kernel(rows_ref, gain_ref, head_ref, offset_ref, out_ref):
+def logits_kernel(gain_ref, offset_ref, away_ref, weights_ref, out_ref, rows_ref, head_ref, sems, sem):
+    copies = [
+        pltpu.make_async_copy(away_ref.at[:, t], rows_ref.at[t], sems.at[t]) for t in range(TP)
+    ]
+    for copy in copies:
+        copy.start()
+    head_copy = pltpu.make_async_copy(weights_ref, head_ref, sem.at[0])
+    head_copy.start()
+
     def piece(t):
-        tail = rows_ref[:, t, 64:80, :].reshape(128, 128).astype(f32)
+        tail = rows_ref[t, :, 64:80, :].reshape(128, 128).astype(f32)
         tail = [tail.reshape(8, 16, 128), swap_halves(tail).reshape(8, 16, 128)]
-        parts = [rows_ref[:, t, 0:32, :].reshape(256, 128), rows_ref[:, t, 32:64, :].reshape(256, 128)]
+        parts = [rows_ref[t, :, 0:32, :].reshape(256, 128), rows_ref[t, :, 32:64, :].reshape(256, 128)]
         wide = [p.astype(f32) for p in parts]
         return wide + [jnp.concatenate(tail, axis=1).reshape(256, 128)[:, :64]]
 
     squares = jnp.zeros((256, 128), f32)
     tails = jnp.zeros((256, 64), f32)
     for t in range(TP):
+        copies[t].wait()
         a, b, c = piece(t)
         squares = squares + (a * a + b * b)
         tails = tails + c * c
     total = jnp.sum(squares, axis=1, keepdims=True) + jnp.sum(tails, axis=1, keepdims=True)
     factor = lax.rsqrt(total / D + epsilon)
+    head_copy.wait()
     logits = jnp.zeros((256, 2 * BLOCK), f32)
     for t in range(TP):
         at = t * 320
@@ -298,7 +320,6 @@
 
 
 Z_GROUPS = [[gen_index(z, x, c) for z in range(4)] for x in range(4) for c in range(2)]
-X_GROUPS = [[gen_index(z, x, c) for x in range(4)] for z in range(4) for c in range(2)]
 
 
 LAYERS = [[z * 128 + i for i in range(128)] for z in range(4)]
@@ -345,12 +366,15 @@
 
     table = jnp.concatenate([kept[0], chosen.T], axis=1)
     piece = call(
-        pack_kernel, shape((496, 128), bf16), rank.reshape(1), wqkv, table, wout, scalars=1
+        pack_kernel, shape((288, 128), bf16), rank.reshape(1), wqkv, table, scalars=1
     )
     along_z = spread(piece, "gen", 4, Z_GROUPS)
-    out_whole = lax.all_gather(along_z[:, 288:], "gen", axis_index_groups=XC_GROUPS)
-    own_w = spread(along_z[:, :288], "gen", 4, X_GROUPS).reshape(16, 288, 128)
-    other_w = lax.ppermute(own_w, "gen", [(g, g ^ 1) for g in range(GEN)])
+    out_piece = call(pack_out_kernel, shape((208, 128), bf16), wout)
+    along_z, out_piece = lax.optimization_barrier((along_z, out_piece))
+    pieces = lax.all_gather(along_z, "gen", axis_index_groups=XC_GROUPS)
+    out_along_z = spread(out_piece, "gen", 4, Z_GROUPS)
+    pieces, out_along_z = lax.optimization_barrier((pieces, out_along_z))
+    out_whole = lax.all_gather(out_along_z, "gen", axis_index_groups=XC_GROUPS)
 
     x = embeddings.reshape(STEPS, TP, OWN, features).transpose(1, 0, 2, 3).reshape(128, features)
     parts, meta = call(
@@ -359,9 +383,11 @@
         me.reshape(1),
         x,
         attn_gain.reshape(1, features),
-        own_w,
-        other_w,
+        pieces,
         scalars=1,
+        away=1,
+        scratch=[pltpu.VMEM((4, 8, 288, 128), bf16), pltpu.SemaphoreType.DMA((4,))],
+        vmem=59,
     )
     parts = all_to_all(parts.reshape(TP, 8, QKV + 128), "tp")
 
@@ -389,8 +415,11 @@
         output_kernel,
         (shape((128, features), bf16), shape((320, 128), bf16)),
         mixed,
+        x,
         out_whole,
-        x,
+        away=1,
+        scratch=[pltpu.VMEM((4, 8, 208, 128), bf16), pltpu.SemaphoreType.DMA((4,))],
+        vmem=59,
     )
     last_hidden = layer_out.reshape(TP, STEPS, OWN, features)[:, -1].reshape(ROWS, features)
 
@@ -400,10 +429,18 @@
     stats = call(
         logits_kernel,
         shape((8, 256), f32),
+        final_gain.reshape(1, D),
+        offset,
         taken,
-        final_gain.reshape(1, D),
         head,
-        offset,
+        away=2,
+        scratch=[
+            pltpu.VMEM((TP, 8, 80, 128), bf16),
+            pltpu.VMEM((D, 2 * BLOCK), bf16),
+            pltpu.SemaphoreType.DMA((TP,)),
+            pltpu.SemaphoreType.DMA((1,)),
+        ],
+        vmem=57,
     )
     stats = stats[:3].reshape(3, 8, 4, 8).transpose(2, 1, 0, 3).reshape(GEN, 1, 24)
     stats = all_to_all(stats, "gen").reshape(GEN, 24).T

time: 288 us -> 298 us (1.035)
  blocking collectives: 60 us -> 0 us
  waiting for transfers between devices: 141 us -> 176 us
  starting transfers between devices: 44.5 us -> 65.1 us
  Pallas kernels: 10.4 us -> 21.5 us
  local copies, waits for them, and re-layouts: 15.3 us -> 18.3 us
    all_to_all x2 -> x0, blocking collectives: 60 us -> none  [all_to_all(): lax.all_to_all(value, axis, split_axis=0, concat_axis=0, tiled=True, axis...]
    all_to_all x6 -> x8, starting transfers between devices: 40 us -> 65.1 us  [all_to_all(): lax.all_to_all(value, axis, split_axis=0, concat_axis=0, tiled=True, axis...]
    all_to_all x6 -> x8, waiting for transfers between devices: 138 us -> 158 us  [all_to_all(): lax.all_to_all(value, axis, split_axis=0, concat_axis=0, tiled=True, axis...]
    all_gather x1 -> x2, waiting for transfers between devices: 0.02 us -> 18.1 us  [the longest x1 15.8 us: body(): pieces = lax.all_gather(along_z, 'gen', axis_index_groups=XC_GROUPS)]
    pallas_call x7 -> x8, Pallas kernels: 10.4 us -> 21.5 us  [call(): pl.pallas_call(kernel, out_shape=out_shape, in_specs=specs, out_specs=jax...]
    ppermute x1 -> x0, starting transfers between devices: 4.47 us -> none  [body(): other_w = lax.ppermute(own_w, 'gen', [(g, g ^ 1) for g in range(GEN)])]
    unnamed x24, local copies, waits for them, and re-layouts: 7.09 us -> 3.95 us
  transfers between devices with their start and end apart: 8 -> 10, of which waited for: 7 -> 10; matrix products, arithmetic and copies ran while one was open for 2% -> 4% of each run, Pallas kernels for 1% -> 1%
where the time goes in v6:
time: 298 us; the launch traced here: 297 us
  waiting for transfers between devices  176 us (59%)
  starting transfers between devices  65.1 us (22%)
  Pallas kernels  21.5 us (7%)
  local copies, waits for them, and re-layouts  18.3 us (6%)
  between operations  14.3 us (5%)
    all_to_all x8, waiting for transfers between devices, all_to_all(): lax.all_to_all(value, axis, split_axis=0, concat_axis=0, tiled=True, axis...  158 us
    all_to_all x8, starting transfers between devices, all_to_all(): lax.all_to_all(value, axis, split_axis=0, concat_axis=0, tiled=True, axis...  65.1 us
    pallas_call x8, Pallas kernels, call(): pl.pallas_call(kernel, out_shape=out_shape, in_specs=specs, out_specs=jax...  21.5 us
    all_gather x1, waiting for transfers between devices, body(): pieces = lax.all_gather(along_z, 'gen', axis_index_groups=XC_GROUPS)  15.8 us
  transfers between devices with their start and end apart: 10, of which 10 were waited for; matrix products, arithmetic and copies ran while one was open for 4% of the time, Pallas kernels for 1%

profile of v6, /device:TPU:1, one launch (start us, length us, event | category | flops | bytes accessed | tf_op | source)
XLA Modules:
  0.0 297.3 jit_solution(16347403519201112718)
XLA Ops:
  8.0 0.9 copy-done.1
  9.1 0.8 broadcast_in_dim.28
  9.9 15.6 %all-to-all-start = ((bf16[4,288,128]{2,1,0:T(8,128)(2,1)}), bf16[4,288,128]{2,1,0:T(8,128)(2,1)S(1)}, u32[]{:S(2)}, u32[]{:S(2)}) async-start(bf16[4,288,128]{2,1,0:T(8,128)(2,1)} %broadcast_in_dim.28), calls=%async_computation | async-start | bytes 589824 | tf_op jit(solution)/shard_map/all_to_all | solution.py:332
  25.5 0.8 copy-done.2
  26.4 13.3 %all-to-all-done = bf16[4,288,128]{2,1,0:T(8,128)(2,1)S(1)} async-done(((bf16[4,288,128]{2,1,0:T(8,128)(2,1)}), bf16[4,288,128]{2,1,0:T(8,128)(2,1)S(1)}, u32[]{:S(2)}, u32[]{:S(2)}) %all-to-all-start) | async-done | bytes 294944 | tf_op jit(solution)/shard_map/all_to_all | solution.py:332
  41.2 5.7 %all-to-all-start.1 = ((bf16[4,208,128]{2,1,0:T(8,128)(2,1)}), bf16[4,208,128]{2,1,0:T(8,128)(2,1)S(1)}, u32[]{:S(2)}, u32[]{:S(2)}) async-start(bf16[4,208,128]{2,1,0:T(8,128)(2,1)} %broadcast_in_dim.29), calls=%async_computation.1 | async-start | bytes 425984 | tf_op jit(solution)/shard_map/all_to_all | solution.py:332
  46.9 1.3 reshape.116.gain_ref
  48.2 0.9 reshape.114
  49.9 9.7 %all-to-all-done.1 = bf16[4,208,128]{2,1,0:T(8,128)(2,1)S(1)} async-done(((bf16[4,208,128]{2,1,0:T(8,128)(2,1)}), bf16[4,208,128]{2,1,0:T(8,128)(2,1)S(1)}, u32[]{:S(2)}, u32[]{:S(2)}) %all-to-all-start.1) | async-done | bytes 213024 | tf_op jit(solution)/shard_map/all_to_all | solution.py:332
  59.6 15.8 %all-gather.5.cloned.1.call-done = bf16[32,288,128]{2,1,0:T(8,128)(2,1)} async-done(((bf16[4,288,128]{2,1,0:T(8,128)(2,1)}), bf16[32,288,128]{2,1,0:T(8,128)(2,1)}) %all-gather.5.cloned.1.call-update) | async-done | bytes 2359312 | tf_op jit(solution)/shard_map/all_gather | solution.py:374
  75.4 4.5 %shard_map.123 = (bf16[128,3712]{1,0:T(8,128)(2,1)}, f32[32,128]{1,0:T(8,128)}) custom-call(s32[1]{0:T(128)} %bitcast.me_ref, bf16[128,320]{1,0:T(8,128)(2,1)} %reshape.115.x_ref, bf16[1,320]{1,0:T(2,128)(2,1)} %reshape.116.gain_ref, bf16[8,4,288,128]{3,2,1,0:T(8,128)(2,1)} %bitcast.54), custom_call_target="tpu_custom_call" | custom-call | tf_op jit(solution)/shard_map/pallas_call | solution.py:36
  79.9 7.1 %all-to-all-start.2 = ((bf16[16,8,3712]{2,1,0:T(8,128)(2,1)}), bf16[16,8,3712]{2,1,0:T(8,128)(2,1)S(1)}, u32[]{:S(2)}, u32[]{:S(2)}) async-start(bf16[16,8,3712]{2,1,0:T(8,128)(2,1)} %bitcast.56), calls=%async_computation.2 | async-start | bytes 1900544 | tf_op jit(solution)/shard_map/all_to_all | solution.py:332
  87.9 24.0 %all-to-all-done.2.parts_ref = bf16[16,8,3712]{2,1,0:T(8,128)(2,1)S(1)} async-done(((bf16[16,8,3712]{2,1,0:T(8,128)(2,1)}), bf16[16,8,3712]{2,1,0:T(8,128)(2,1)S(1)}, u32[]{:S(2)}, u32[]{:S(2)}) %all-to-all-start.2) | async-done | bytes 950304 | tf_op jit(solution)/shard_map/all_to_all | solution.py:332
  112.0 1.8 shard_map.124
  113.8 0.9 broadcast_in_dim.32
  114.7 4.2 %all-to-all-start.3 = ((bf16[16,8,2560]{2,1,0:T(8,128)(2,1)}), bf16[16,8,2560]{2,1,0:T(8,128)(2,1)S(1)}, u32[]{:S(2)}, u32[]{:S(2)}) async-start(bf16[16,8,2560]{2,1,0:T(8,128)(2,1)} %broadcast_in_dim.32), calls=%async_computation.3 | async-start | bytes 1310720 | tf_op jit(solution)/shard_map/all_to_all | solution.py:332
  118.9 2.3 all-gather.7.cloned.1.call-done
  121.2 16.2 %all-to-all-done.3 = bf16[16,8,2560]{2,1,0:T(8,128)(2,1)S(1)} async-done(((bf16[16,8,2560]{2,1,0:T(8,128)(2,1)}), bf16[16,8,2560]{2,1,0:T(8,128)(2,1)S(1)}, u32[]{:S(2)}, u32[]{:S(2)}) %all-to-all-start.3) | async-done | bytes 655392 | tf_op jit(solution)/shard_map/all_to_all | solution.py:332
  137.4 0.8 copy-done.3
  138.2 3.9 %shard_map.125 = (bf16[128,320]{1,0:T(8,128)(2,1)}, bf16[320,128]{1,0:T(8,128)(2,1)}) custom-call(bf16[128,2560]{1,0:T(8,128)(2,1)} %bitcast.53, bf16[128,320]{1,0:T(8,128)(2,1)} %reshape.115.x_ref, bf16[8,4,208,128]{3,2,1,0:T(8,128)(2,1)} %bitcast.55), custom_call_target="tpu_custom_call" | custom-call | tf_op jit(solution)/shard_map/pallas_call | solution.py:36
  142.2 1.7 broadcast_in_dim.33
  143.8 9.2 %all-to-all-start.4 = ((bf16[4,320,128]{2,1,0:T(8,128)(2,1)}), bf16[4,320,128]{2,1,0:T(8,128)(2,1)S(1)}, u32[]{:S(2)}, u32[]{:S(2)}) async-start(bf16[4,320,128]{2,1,0:T(8,128)(2,1)} %broadcast_in_dim.33), calls=%async_computation.4 | async-start | bytes 655360 | tf_op jit(solution)/shard_map/all_to_all | solution.py:332
  155.3 14.7 %all-to-all-done.4.layer_ref = bf16[4,320,128]{2,1,0:T(8,128)(2,1)S(1)} async-done(((bf16[4,320,128]{2,1,0:T(8,128)(2,1)}), bf16[4,320,128]{2,1,0:T(8,128)(2,1)S(1)}, u32[]{:S(2)}, u32[]{:S(2)}) %all-to-all-start.4) | async-done | bytes 327712 | tf_op jit(solution)/shard_map/all_to_all | solution.py:332
  170.1 3.7 %shard_map.126 = bf16[128,80,128]{2,1,0:T(8,128)(2,1)} custom-call(bf16[4,320,128]{2,1,0:T(8,128)(2,1)S(1)} %all-to-all-done.4.layer_ref, s32[2048,2]{1,0:T(8,128)S(1)} %broadcast_add_fusion.spot_ref), custom_call_target="tpu_custom_call" | custom-call | tf_op jit(solution)/shard_map/pallas_call | solution.py:36
  173.8 14.0 %all-to-all-start.5 = ((bf16[128,80,128]{2,1,0:T(8,128)(2,1)}), bf16[128,80,128]{2,1,0:T(8,128)(2,1)}, u32[]{:S(2)}, u32[]{:S(2)}) async-start(bf16[128,80,128]{2,1,0:T(8,128)(2,1)} %shard_map.126), calls=%async_computation.5 | async-start | bytes 5242880 | tf_op jit(solution)/shard_map/all_to_all | solution.py:332
  189.6 60.5 %all-to-all-done.5 = bf16[128,80,128]{2,1,0:T(8,128)(2,1)} async-done(((bf16[128,80,128]{2,1,0:T(8,128)(2,1)}), bf16[128,80,128]{2,1,0:T(8,128)(2,1)}, u32[]{:S(2)}, u32[]{:S(2)}) %all-to-all-start.5) | async-done | bytes 2621472 | tf_op jit(solution)/shard_map/all_to_all | solution.py:332
  250.2 6.2 %shard_map.127 = f32[8,256]{1,0:T(8,128)} custom-call(bf16[1,5120]{1,0:T(2,128)(2,1)} %reshape.112.gain_ref, s32[1,256]{1,0:T(1,128)} %reshape.121.offset_ref, bf16[8,16,80,128]{3,2,1,0:T(8,128)(2,1)} %bitcast.15.away_ref, bf16[5120,256]{1,0:T(8,128)(2,1)} %weights_ref.3), custom_call_target="tpu_custom_call" | custom-call | tf_op jit(solution)/shard_map/pallas_call | solution.py:36
  258.1 5.8 %all-to-all-start.6 = ((f32[32,1,24]{2,1,0:T(1,128)}), f32[32,1,24]{2,1,0:T(1,128)S(1)}, u32[]{:S(2)}, u32[]{:S(2)}) async-start(f32[32,1,24]{2,1,0:T(1,128)} %copy.84), calls=%async_computation.6 | async-start | bytes 32768 | tf_op jit(solution)/shard_map/all_to_all | solution.py:332
  264.1 13.8 %all-to-all-done.6 = f32[32,1,24]{2,1,0:T(1,128)S(1)} async-done(((f32[32,1,24]{2,1,0:T(1,128)}), f32[32,1,24]{2,1,0:T(1,128)S(1)}, u32[]{:S(2)}, u32[]{:S(2)}) %all-to-all-start.6) | async-done | bytes 3104 | tf_op jit(solution)/shard_map/all_to_all | solution.py:332
  278.1 1.0 shard_map.128
  279.1 3.5 %all-to-all-start.7 = ((f32[16,4,8]{2,1,0:T(4,128)}), f32[16,4,8]{2,1,0:T(4,128)S(1)}, u32[]{:S(2)}, u32[]{:S(2)}) async-start(f32[16,4,8]{2,1,0:T(4,128)} %bitcast.49), calls=%async_computation.7 | async-start | bytes 65536 | tf_op jit(solution)/shard_map/all_to_all | solution.py:332
  283.9 5.5 %all-to-all-done.7 = f32[16,4,8]{2,1,0:T(4,128)S(1)} async-done(((f32[16,4,8]{2,1,0:T(4,128)}), f32[16,4,8]{2,1,0:T(4,128)S(1)}, u32[]{:S(2)}, u32[]{:S(2)}) %all-to-all-start.7) | async-done | bytes 2080 | tf_op jit(solution)/shard_map/all_to_all | solution.py:332
  (82 shorter events, 12.9 us)
Async XLA Ops:
  8.0 0.9 copy-start.1
  9.9 29.8 %all-to-all-start = ((bf16[4,288,128]{2,1,0:T(8,128)(2,1)}), bf16[4,288,128]{2,1,0:T(8,128)(2,1)S(1)}, u32[]{:S(2)}, u32[]{:S(2)}) async-start(bf16[4,288,128]{2,1,0:T(8,128)(2,1)} %broadcast_in_dim.28), calls=%async_computation | async-start | bytes 589824 | tf_op jit(solution)/shard_map/all_to_all | solution.py:332
  25.5 49.9 %all-gather.5.cloned.1.call-start = ((), (), s32[]{:S(2)}) async-start(), calls=%async_computation.8 | async-start | bytes 2654208 | tf_op jit(solution)/shard_map/all_gather | solution.py:374
  25.5 0.8 copy-start.2
  39.7 0.7 copy-start.4
  41.2 45.9 %copy-start.10 = (s32[4]{0:T(128)S(1)}, s32[4]{0:T(128)}, u32[]{:S(2)}) copy-start(s32[4]{0:T(128)} %param.12) | copy-start | bytes 52
  41.2 18.4 %all-to-all-start.1 = ((bf16[4,208,128]{2,1,0:T(8,128)(2,1)}), bf16[4,208,128]{2,1,0:T(8,128)(2,1)S(1)}, u32[]{:S(2)}, u32[]{:S(2)}) async-start(bf16[4,208,128]{2,1,0:T(8,128)(2,1)} %broadcast_in_dim.29), calls=%async_computation.1 | async-start | bytes 425984 | tf_op jit(solution)/shard_map/all_to_all | solution.py:332
  46.9 65.2 %copy-start = (bf16[4,128,1024]{2,1,0:T(8,128)(2,1)S(1)}, bf16[4,128,1024]{2,1,0:T(8,128)(2,1)}, u32[]{:S(2)}) copy-start(bf16[4,128,1024]{2,1,0:T(8,128)(2,1)} %cache_ref.1) | copy-start | bytes 3145732
  59.6 27.7 %copy-start.5 = (bf16[4,208,128]{2,1,0:T(8,128)(2,1)}, bf16[4,208,128]{2,1,0:T(8,128)(2,1)S(1)}, u32[]{:S(2)}) copy-start(bf16[4,208,128]{2,1,0:T(8,128)(2,1)S(1)} %all-to-all-done.1) | copy-start | bytes 638980
  79.9 32.1 %all-to-all-start.2 = ((bf16[16,8,3712]{2,1,0:T(8,128)(2,1)}), bf16[16,8,3712]{2,1,0:T(8,128)(2,1)S(1)}, u32[]{:S(2)}, u32[]{:S(2)}) async-start(bf16[16,8,3712]{2,1,0:T(8,128)(2,1)} %bitcast.56), calls=%async_computation.2 | async-start | bytes 1900544 | tf_op jit(solution)/shard_map/all_to_all | solution.py:332
  87.0 34.2 %all-gather.7.cloned.1.call-start = ((), (), s32[]{:S(2)}) async-start(), calls=%async_computation.9 | async-start | bytes 1916928 | tf_op jit(solution)/shard_map/all_gather | solution.py:377
  114.7 22.7 %all-to-all-start.3 = ((bf16[16,8,2560]{2,1,0:T(8,128)(2,1)}), bf16[16,8,2560]{2,1,0:T(8,128)(2,1)S(1)}, u32[]{:S(2)}, u32[]{:S(2)}) async-start(bf16[16,8,2560]{2,1,0:T(8,128)(2,1)} %broadcast_in_dim.32), calls=%async_computation.3 | async-start | bytes 1310720 | tf_op jit(solution)/shard_map/all_to_all | solution.py:332
  137.4 0.8 copy-start.3
  143.8 26.2 %all-to-all-start.4 = ((bf16[4,320,128]{2,1,0:T(8,128)(2,1)}), bf16[4,320,128]{2,1,0:T(8,128)(2,1)S(1)}, u32[]{:S(2)}, u32[]{:S(2)}) async-start(bf16[4,320,128]{2,1,0:T(8,128)(2,1)} %broadcast_in_dim.33), calls=%async_computation.4 | async-start | bytes 655360 | tf_op jit(solution)/shard_map/all_to_all | solution.py:332
  173.8 14.0 %copy-start.7 = (bf16[5120]{0:T(1024)(128)(2,1)S(1)}, bf16[5120]{0:T(1024)(128)(2,1)}, u32[]{:S(2)}) copy-start(bf16[5120]{0:T(1024)(128)(2,1)} %param.16) | copy-start | bytes 30724
  173.8 14.6 %copy-start.9 = (s32[1,64,2]{1,2,0:T(2,128)S(1)}, s32[1,64,2]{1,2,0:T(2,128)}, u32[]{:S(2)}) copy-start(s32[1,64,2]{1,2,0:T(2,128)} %param.18) | copy-start | bytes 1540
  173.8 14.8 %copy-start.8 = (f32[32,128]{1,0:T(8,128)S(1)}, f32[32,128]{1,0:T(8,128)}, u32[]{:S(2)}) copy-start(f32[32,128]{1,0:T(8,128)} %get-tuple-element.16) | copy-start | bytes 49156
  173.8 76.4 %all-to-all-start.5 = ((bf16[128,80,128]{2,1,0:T(8,128)(2,1)}), bf16[128,80,128]{2,1,0:T(8,128)(2,1)}, u32[]{:S(2)}, u32[]{:S(2)}) async-start(bf16[128,80,128]{2,1,0:T(8,128)(2,1)} %shard_map.126), calls=%async_computation.5 | async-start | bytes 5242880 | tf_op jit(solution)/shard_map/all_to_all | solution.py:332
  250.2 33.0 %copy-start.6 = (bf16[128,320]{1,0:T(8,128)(2,1)S(1)}, bf16[128,320]{1,0:T(8,128)(2,1)}, u32[]{:S(2)}) copy-start(bf16[128,320]{1,0:T(8,128)(2,1)} %get-tuple-element.21) | copy-start | bytes 245764
  258.1 19.9 %all-to-all-start.6 = ((f32[32,1,24]{2,1,0:T(1,128)}), f32[32,1,24]{2,1,0:T(1,128)S(1)}, u32[]{:S(2)}, u32[]{:S(2)}) async-start(f32[32,1,24]{2,1,0:T(1,128)} %copy.84), calls=%async_computation.6 | async-start | bytes 32768 | tf_op jit(solution)/shard_map/all_to_all | solution.py:332
  279.1 10.3 %all-to-all-start.7 = ((f32[16,4,8]{2,1,0:T(4,128)}), f32[16,4,8]{2,1,0:T(4,128)S(1)}, u32[]{:S(2)}, u32[]{:S(2)}) async-start(f32[16,4,8]{2,1,0:T(4,128)} %bitcast.49), calls=%async_computation.7 | async-start | bytes 65536 | tf_op jit(solution)/shard_map/all_to_all | solution.py:332
Sparse Core Ops, SparseCore 0:
  40.6 34.7 all-gather.4
  89.9 31.2 all-gather.6

commit v7 on v5

--- a/solution.py
+++ b/solution.py
@@ -61,7 +61,8 @@
     return jnp.concatenate([piece[:rows], piece[rows : 2 * rows], tail], axis=1)
 
 
-def pack_kernel(rank_ref, weights_ref, table_ref, wout_ref, out_ref):
+def pack_kernel(rank_ref, weights_ref, table_ref, wout_ref, copies_ref):
+    out_ref = copies_ref.at[0]
     wide = wout_ref[...].astype(f32)
     out_ref[288:368, :] = wide[:, 0:128].astype(bf16)
     out_ref[368:448, :] = wide[:, 128:256].astype(bf16)
@@ -89,6 +90,8 @@
             meta = jnp.where(line == 2 + 2 * s + slot, value, meta)
     side = jnp.concatenate([turned[64:112, 256:320], meta.astype(f32)], axis=0)
     out_ref[224:288, :] = jnp.concatenate([turned[0:64, 256:320], side], axis=1).astype(bf16)
+    for z in range(1, 4):
+        copies_ref[z] = copies_ref[0]
 
 
 def project_kernel(me_ref, x_ref, gain_ref, own_ref, other_ref, out_ref, meta_ref):
@@ -147,10 +150,12 @@
         )
     rows = (x_ref[...].astype(f32) + part[:, :320]).astype(bf16)
     rows_ref[...] = rows
-    packed_ref[0:128, :] = rows[:, 0:128]
-    packed_ref[128:256, :] = rows[:, 128:256]
     tail = rows[:, 256:320].astype(f32)
-    packed_ref[256:320, :] = jnp.concatenate([tail[0:64], tail[64:128]], axis=1).astype(bf16)
+    tail = jnp.concatenate([tail[0:64], tail[64:128]], axis=1).astype(bf16)
+    for z in range(4):
+        packed_ref[z, 0:128, :] = rows[:, 0:128]
+        packed_ref[z, 128:256, :] = rows[:, 128:256]
+        packed_ref[z, 256:320, :] = tail
 
 
 def attend_kernel(parts_ref, cache_ref, lengths_ref, cos_ref, sin_ref, mixed_ref, entry_ref):
@@ -201,7 +206,9 @@
         mixed = mixed + jnp.dot(new_w, new_v, preferred_element_type=f32)
         for h in range(GROUP):
             to = (k * GROUP + h) * HEAD_SIZE
-            mixed_ref[:, to : to + HEAD_SIZE] = mixed[8 * h : 8 * h + 8].astype(bf16)
+            part = mixed[8 * h : 8 * h + 8].astype(bf16)
+            for t in range(TP):
+                mixed_ref[t, :, to : to + HEAD_SIZE] = part
 
 
 def select_kernel(layer_ref, spot_ref, out_ref):
@@ -345,9 +352,9 @@
 
     table = jnp.concatenate([kept[0], chosen.T], axis=1)
     piece = call(
-        pack_kernel, shape((496, 128), bf16), rank.reshape(1), wqkv, table, wout, scalars=1
-    )
-    along_z = spread(piece, "gen", 4, Z_GROUPS)
+        pack_kernel, shape((4, 496, 128), bf16), rank.reshape(1), wqkv, table, wout, scalars=1
+    )
+    along_z = all_to_all(piece, "gen", Z_GROUPS)
     out_whole = lax.all_gather(along_z[:, 288:], "gen", axis_index_groups=XC_GROUPS)
     own_w = spread(along_z[:, :288], "gen", 4, X_GROUPS).reshape(16, 288, 128)
     other_w = lax.ppermute(own_w, "gen", [(g, g ^ 1) for g in range(GEN)])
@@ -377,24 +384,24 @@
     wide_lengths = jnp.broadcast_to(jnp.tile(lengths, STEPS)[:, None], (8, 128))
     mixed, entries = call(
         attend_kernel,
-        (shape((8, QUERY_HEADS * HEAD_SIZE), bf16), shape((8, 1024), bf16)),
+        (shape((TP, 8, QUERY_HEADS * HEAD_SIZE), bf16), shape((8, 1024), bf16)),
         parts,
         cache,
         wide_lengths,
         cosine,
         sine,
     )
-    mixed = spread(mixed, "tp", TP).reshape(128, QUERY_HEADS * HEAD_SIZE)
+    mixed = all_to_all(mixed, "tp").reshape(128, QUERY_HEADS * HEAD_SIZE)
     layer_out, packed = call(
         output_kernel,
-        (shape((128, features), bf16), shape((320, 128), bf16)),
+        (shape((128, features), bf16), shape((4, 320, 128), bf16)),
         mixed,
         out_whole,
         x,
     )
     last_hidden = layer_out.reshape(TP, STEPS, OWN, features)[:, -1].reshape(ROWS, features)
 
-    layers = spread(packed, "gen", 4, Z_GROUPS)
+    layers = all_to_all(packed, "gen", Z_GROUPS)
     taken = call(select_kernel, shape((128, 80, 128), bf16), layers, spot)
     taken = all_to_all(taken, ("gen", "tp"), LAYERS).reshape(8, TP, 80, 128)
     stats = call(

time: 288 us -> 288 us (level)
  no operation moved by 1% of the time
where the time goes in v7:
time: 288 us; the launch traced here: 287 us
  waiting for transfers between devices  141 us (49%)
  blocking collectives  60 us (21%)
  starting transfers between devices  44.5 us (15%)
  between operations  14.4 us (5%)
  local copies, waits for them, and re-layouts  13.6 us (5%)
  Pallas kernels  12 us (4%)
    all_to_all x6, waiting for transfers between devices, all_to_all(): lax.all_to_all(value, axis, split_axis=0, concat_axis=0, tiled=True, axis...  138 us
    all_to_all x2, blocking collectives, all_to_all(): lax.all_to_all(value, axis, split_axis=0, concat_axis=0, tiled=True, axis...  60 us
    all_to_all x6, starting transfers between devices, all_to_all(): lax.all_to_all(value, axis, split_axis=0, concat_axis=0, tiled=True, axis...  40 us
    pallas_call x7, Pallas kernels, call(): pl.pallas_call(kernel, out_shape=out_shape, in_specs=specs, out_specs=jax...  12 us
    unnamed x24, local copies, waits for them, and re-layouts  7.09 us
  transfers between devices with their start and end apart: 8, of which 7 were waited for; matrix products, arithmetic and copies ran while one was open for 2% of the time, Pallas kernels for 1%

profile of v7, /device:TPU:1, one launch (start us, length us, event | category | flops | bytes accessed | tf_op | source)
XLA Modules:
  0.0 287.0 jit_solution(8041023221118832603)
XLA Ops:
  7.2 0.7 pad_add_fusion
  8.0 0.9 copy-done.4
  8.9 0.8 copy-done.5
  10.0 41.3 %all_to_all.40 = bf16[4,496,128]{2,1,0:T(8,128)(2,1)S(1)} all-to-all(bf16[4,496,128]{2,1,0:T(8,128)(2,1)S(1)} %shard_map.121), channel_id=1, replica_groups={{0,128,256,384},{16,144,272,400},{32,160,288,416},{48,176,304,432},{64,..., dimensions={0} | all-to-all | bytes 1015808 | tf_op jit(solution)/shard_map/all_to_all | solution.py:318
  51.5 18.7 %all_to_all.41 = bf16[4,4,288,128]{3,2,1,0:T(8,128)(2,1)S(1)} all-to-all(bf16[4,4,288,128]{3,2,1,0:T(8,128)(2,1)S(1)} %broadcast_in_dim.26), channel_id=1, replica_groups={{0,32,64,96},{16,48,80,112},{128,160,192,224},{144,176,208,240},{256,28..., dimensions={0} | all-to-all | bytes 2359296 | tf_op jit(solution)/shard_map/all_to_all | solution.py:318
  70.2 4.5 %collective-permute-start = (bf16[16,288,128]{2,1,0:T(8,128)(2,1)S(1)}, bf16[16,288,128]{2,1,0:T(8,128)(2,1)S(1)}, u32[]{:S(2)}, u32[]{:S(2)}) collective-permute-start(bf16[16,288,128]{2,1,0:T(8,128)(2,1)S(1)} %bitcast.51), channel_id=1, source_target_pairs={{0,16},{16,0},{32,48},{48,32},{64,80},{80,64},{96,112},{112,96},{1... | collective-permute-start | bytes 3538952 | tf_op jit(solution)/shard_map/ppermute | solution.py:360
  74.9 2.3 collective-permute-done.other_ref
  77.2 2.0 shard_map.122
  79.1 10.7 %all-to-all-start.2 = ((bf16[16,8,3712]{2,1,0:T(8,128)(2,1)}), bf16[16,8,3712]{2,1,0:T(8,128)(2,1)S(1)}, u32[]{:S(2)}, u32[]{:S(2)}) async-start(bf16[16,8,3712]{2,1,0:T(8,128)(2,1)} %bitcast.6), calls=%async_computation.2 | async-start | bytes 1900544 | tf_op jit(solution)/shard_map/all_to_all | solution.py:318
  90.1 0.7 slice.45
  91.0 23.7 %all-to-all-done.2.parts_ref = bf16[16,8,3712]{2,1,0:T(8,128)(2,1)S(1)} async-done(((bf16[16,8,3712]{2,1,0:T(8,128)(2,1)}), bf16[16,8,3712]{2,1,0:T(8,128)(2,1)S(1)}, u32[]{:S(2)}, u32[]{:S(2)}) %all-to-all-start.2) | async-done | bytes 950304 | tf_op jit(solution)/shard_map/all_to_all | solution.py:318
  114.9 2.7 shard_map.123
  117.5 4.3 %all-to-all-start.3 = ((bf16[16,8,2560]{2,1,0:T(8,128)(2,1)}), bf16[16,8,2560]{2,1,0:T(8,128)(2,1)S(1)}, u32[]{:S(2)}, u32[]{:S(2)}) async-start(bf16[16,8,2560]{2,1,0:T(8,128)(2,1)} %get-tuple-element.10), calls=%async_computation.3 | async-start | bytes 1310720 | tf_op jit(solution)/shard_map/all_to_all | solution.py:318
  121.9 18.5 %all-to-all-done.3 = bf16[16,8,2560]{2,1,0:T(8,128)(2,1)S(1)} async-done(((bf16[16,8,2560]{2,1,0:T(8,128)(2,1)}), bf16[16,8,2560]{2,1,0:T(8,128)(2,1)S(1)}, u32[]{:S(2)}, u32[]{:S(2)}) %all-to-all-start.3) | async-done | bytes 655392 | tf_op jit(solution)/shard_map/all_to_all | solution.py:318
  140.4 1.5 copy-done.2
  141.8 1.4 shard_map.124
  143.2 3.5 %all-to-all-start.4 = ((bf16[4,320,128]{2,1,0:T(8,128)(2,1)}), bf16[4,320,128]{2,1,0:T(8,128)(2,1)S(1)}, u32[]{:S(2)}, u32[]{:S(2)}) async-start(bf16[4,320,128]{2,1,0:T(8,128)(2,1)} %get-tuple-element.11), calls=%async_computation.4 | async-start | bytes 655360 | tf_op jit(solution)/shard_map/all_to_all | solution.py:318
  149.0 14.8 %all-to-all-done.4.layer_ref = bf16[4,320,128]{2,1,0:T(8,128)(2,1)S(1)} async-done(((bf16[4,320,128]{2,1,0:T(8,128)(2,1)}), bf16[4,320,128]{2,1,0:T(8,128)(2,1)S(1)}, u32[]{:S(2)}, u32[]{:S(2)}) %all-to-all-start.4) | async-done | bytes 327712 | tf_op jit(solution)/shard_map/all_to_all | solution.py:318
  163.8 2.2 shard_map.125
  166.0 1.5 copy-done
  167.5 12.5 %all-to-all-start.5 = ((bf16[128,80,128]{2,1,0:T(8,128)(2,1)}), bf16[128,80,128]{2,1,0:T(8,128)(2,1)S(1)}, u32[]{:S(2)}, u32[]{:S(2)}) async-start(bf16[128,80,128]{2,1,0:T(8,128)(2,1)} %copy-done), calls=%async_computation.5 | async-start | bytes 5242880 | tf_op jit(solution)/shard_map/all_to_all | solution.py:318
  180.7 62.0 %all-to-all-done.5 = bf16[128,80,128]{2,1,0:T(8,128)(2,1)S(1)} async-done(((bf16[128,80,128]{2,1,0:T(8,128)(2,1)}), bf16[128,80,128]{2,1,0:T(8,128)(2,1)S(1)}, u32[]{:S(2)}, u32[]{:S(2)}) %all-to-all-start.5) | async-done | bytes 2621472 | tf_op jit(solution)/shard_map/all_to_all | solution.py:318
  242.7 1.7 copy-done.1
  244.4 2.6 shard_map.126
  247.3 0.7 copy.84
  248.0 5.5 %all-to-all-start.6 = ((f32[32,1,24]{2,1,0:T(1,128)}), f32[32,1,24]{2,1,0:T(1,128)S(1)}, u32[]{:S(2)}, u32[]{:S(2)}) async-start(f32[32,1,24]{2,1,0:T(1,128)} %copy.84), calls=%async_computation.6 | async-start | bytes 32768 | tf_op jit(solution)/shard_map/all_to_all | solution.py:318
  253.8 13.8 %all-to-all-done.6 = f32[32,1,24]{2,1,0:T(1,128)S(1)} async-done(((f32[32,1,24]{2,1,0:T(1,128)}), f32[32,1,24]{2,1,0:T(1,128)S(1)}, u32[]{:S(2)}, u32[]{:S(2)}) %all-to-all-start.6) | async-done | bytes 3104 | tf_op jit(solution)/shard_map/all_to_all | solution.py:318
  267.7 1.0 shard_map.127
  268.7 3.5 %all-to-all-start.7 = ((f32[16,4,8]{2,1,0:T(4,128)}), f32[16,4,8]{2,1,0:T(4,128)S(1)}, u32[]{:S(2)}, u32[]{:S(2)}) async-start(f32[16,4,8]{2,1,0:T(4,128)} %bitcast.49), calls=%async_computation.7 | async-start | bytes 65536 | tf_op jit(solution)/shard_map/all_to_all | solution.py:318
  272.9 0.6 reshape_squeeze.3
  273.5 5.5 %all-to-all-done.7 = f32[16,4,8]{2,1,0:T(4,128)S(1)} async-done(((f32[16,4,8]{2,1,0:T(4,128)}), f32[16,4,8]{2,1,0:T(4,128)S(1)}, u32[]{:S(2)}, u32[]{:S(2)}) %all-to-all-start.7) | async-done | bytes 2080 | tf_op jit(solution)/shard_map/all_to_all | solution.py:318
  279.4 0.7 copy.88
  (77 shorter events, 5.9 us)
Async XLA Ops:
  8.0 0.9 copy-start.4
  8.9 0.8 copy-start.5
  51.3 23.4 %copy-start.9 = (bf16[320]{0:T(512)(128)(2,1)S(1)}, bf16[320]{0:T(512)(128)(2,1)}, u32[]{:S(2)}) copy-start(bf16[320]{0:T(512)(128)(2,1)} %param.13) | copy-start | bytes 1924
  51.4 23.4 %copy-start.6 = (bf16[2,64,320]{2,1,0:T(8,128)(2,1)S(1)}, bf16[2,64,320]{2,1,0:T(8,128)(2,1)}, u32[]{:S(2)}) copy-start(bf16[2,64,320]{2,1,0:T(8,128)(2,1)} %param.10) | copy-start | bytes 245764
  70.2 6.9 %collective-permute-start = (bf16[16,288,128]{2,1,0:T(8,128)(2,1)S(1)}, bf16[16,288,128]{2,1,0:T(8,128)(2,1)S(1)}, u32[]{:S(2)}, u32[]{:S(2)}) collective-permute-start(bf16[16,288,128]{2,1,0:T(8,128)(2,1)S(1)} %bitcast.51), channel_id=1, source_target_pairs={{0,16},{16,0},{32,48},{48,32},{64,80},{80,64},{96,112},{112,96},{1... | collective-permute-start | bytes 3538952 | tf_op jit(solution)/shard_map/ppermute | solution.py:360
  77.2 12.7 %copy-start.10 = (s32[4]{0:T(128)S(1)}, s32[4]{0:T(128)}, u32[]{:S(2)}) copy-start(s32[4]{0:T(128)} %param.12) | copy-start | bytes 52
  79.1 35.7 %copy-start.3 = (bf16[4,128,1024]{2,1,0:T(8,128)(2,1)S(1)}, bf16[4,128,1024]{2,1,0:T(8,128)(2,1)}, u32[]{:S(2)}) copy-start(bf16[4,128,1024]{2,1,0:T(8,128)(2,1)} %cache_ref.1) | copy-start | bytes 3145732
  79.1 35.7 %all-to-all-start.2 = ((bf16[16,8,3712]{2,1,0:T(8,128)(2,1)}), bf16[16,8,3712]{2,1,0:T(8,128)(2,1)S(1)}, u32[]{:S(2)}, u32[]{:S(2)}) async-start(bf16[16,8,3712]{2,1,0:T(8,128)(2,1)} %bitcast.6), calls=%async_computation.2 | async-start | bytes 1900544 | tf_op jit(solution)/shard_map/all_to_all | solution.py:318
  89.9 32.0 %all-gather.3.cloned.1.call-start = ((), (), s32[]{:S(2)}) async-start(), calls=%async_computation.8 | async-start | bytes 1916928 | tf_op jit(solution)/shard_map/all_gather | solution.py:358
  117.5 22.9 %all-to-all-start.3 = ((bf16[16,8,2560]{2,1,0:T(8,128)(2,1)}), bf16[16,8,2560]{2,1,0:T(8,128)(2,1)S(1)}, u32[]{:S(2)}, u32[]{:S(2)}) async-start(bf16[16,8,2560]{2,1,0:T(8,128)(2,1)} %get-tuple-element.10), calls=%async_computation.3 | async-start | bytes 1310720 | tf_op jit(solution)/shard_map/all_to_all | solution.py:318
  140.4 1.5 copy-start.2
  143.2 20.6 %all-to-all-start.4 = ((bf16[4,320,128]{2,1,0:T(8,128)(2,1)}), bf16[4,320,128]{2,1,0:T(8,128)(2,1)S(1)}, u32[]{:S(2)}, u32[]{:S(2)}) async-start(bf16[4,320,128]{2,1,0:T(8,128)(2,1)} %get-tuple-element.11), calls=%async_computation.4 | async-start | bytes 655360 | tf_op jit(solution)/shard_map/all_to_all | solution.py:318
  166.0 1.5 copy-start
  167.5 12.5 %copy-start.7 = (bf16[5120]{0:T(1024)(128)(2,1)S(1)}, bf16[5120]{0:T(1024)(128)(2,1)}, u32[]{:S(2)}) copy-start(bf16[5120]{0:T(1024)(128)(2,1)} %param.16) | copy-start | bytes 30724
  167.5 12.5 %copy-start.8 = (s32[1,64,2]{1,2,0:T(2,128)S(1)}, s32[1,64,2]{1,2,0:T(2,128)}, u32[]{:S(2)}) copy-start(s32[1,64,2]{1,2,0:T(2,128)} %param.18) | copy-start | bytes 1540
  167.5 75.2 %all-to-all-start.5 = ((bf16[128,80,128]{2,1,0:T(8,128)(2,1)}), bf16[128,80,128]{2,1,0:T(8,128)(2,1)S(1)}, u32[]{:S(2)}, u32[]{:S(2)}) async-start(bf16[128,80,128]{2,1,0:T(8,128)(2,1)} %copy-done), calls=%async_computation.5 | async-start | bytes 5242880 | tf_op jit(solution)/shard_map/all_to_all | solution.py:318
  242.7 1.7 copy-start.1
  248.0 19.7 %all-to-all-start.6 = ((f32[32,1,24]{2,1,0:T(1,128)}), f32[32,1,24]{2,1,0:T(1,128)S(1)}, u32[]{:S(2)}, u32[]{:S(2)}) async-start(f32[32,1,24]{2,1,0:T(1,128)} %copy.84), calls=%async_computation.6 | async-start | bytes 32768 | tf_op jit(solution)/shard_map/all_to_all | solution.py:318
  268.7 10.3 %all-to-all-start.7 = ((f32[16,4,8]{2,1,0:T(4,128)}), f32[16,4,8]{2,1,0:T(4,128)S(1)}, u32[]{:S(2)}, u32[]{:S(2)}) async-start(f32[16,4,8]{2,1,0:T(4,128)} %bitcast.49), calls=%async_computation.7 | async-start | bytes 65536 | tf_op jit(solution)/shard_map/all_to_all | solution.py:318
Sparse Core Ops, SparseCore 0:
  92.8 25.7 all-gather.2

commit v8 on v7

--- a/solution.py
+++ b/solution.py
@@ -94,7 +94,7 @@
         copies_ref[z] = copies_ref[0]
 
 
-def project_kernel(me_ref, x_ref, gain_ref, own_ref, other_ref, out_ref, meta_ref):
+def project_kernel(me_ref, x_ref, gain_ref, own_ref, other_ref, late_ref, out_ref, meta_ref):
     me = me_ref[0]
     core = lax.rem(me, 2)
     wide = x_ref[...].astype(f32)
@@ -110,6 +110,7 @@
             a = own_ref[x * 4 + z]
             b = other_ref[x * 4 + z]
             for c, piece in enumerate((jnp.where(core == 0, a, b), jnp.where(core == 0, b, a))):
+                piece = jnp.concatenate([piece, late_ref[2 * x + c, z]], axis=0)
                 pieces.append(unpack(piece, 112))
                 table = piece[272:288].astype(f32)
                 for j in range(2):
@@ -117,7 +118,7 @@
                     column = jnp.sum(mine, axis=1, keepdims=True)
                     at = 32 + gen_index(z, x, c)
                     metas[j] = jnp.where(lane == at, column, metas[j])
-        table = own_ref[lax.rem(me // 2, 4) * 4 + z][272:288].astype(f32)
+        table = late_ref[lax.rem(me, 8), z][112:128].astype(f32)
         for slot in range(2):
             extra = jnp.where(line == 2 * z + slot, table[slot : slot + 1], extra)
         part = nt_dot(scaled, jnp.concatenate(pieces, axis=0))
@@ -356,7 +357,8 @@
     )
     along_z = all_to_all(piece, "gen", Z_GROUPS)
     out_whole = lax.all_gather(along_z[:, 288:], "gen", axis_index_groups=XC_GROUPS)
-    own_w = spread(along_z[:, :288], "gen", 4, X_GROUPS).reshape(16, 288, 128)
+    late_w = lax.all_gather(along_z[:, 160:288], "gen", axis_index_groups=XC_GROUPS)
+    own_w = spread(along_z[:, :160], "gen", 4, X_GROUPS).reshape(16, 160, 128)
     other_w = lax.ppermute(own_w, "gen", [(g, g ^ 1) for g in range(GEN)])
 
     x = embeddings.reshape(STEPS, TP, OWN, features).transpose(1, 0, 2, 3).reshape(128, features)
@@ -368,6 +370,7 @@
         attn_gain.reshape(1, features),
         own_w,
         other_w,
+        late_w,
         scalars=1,
     )
     parts = all_to_all(parts.reshape(TP, 8, QKV + 128), "tp")

time: 288 us -> 297 us (1.031)
  waiting for transfers between devices: 141 us -> 151 us
  blocking collectives: 60 us -> 54.4 us
    all_gather x0 -> x1, waiting for transfers between devices: none -> 10.7 us  [body(): lax.all_gather(along_z[:, 160:288], 'gen', axis_index_groups=XC_GROUPS)]
    all_to_all x2, blocking collectives: 60 us -> 54.4 us  [all_to_all(): lax.all_to_all(value, axis, split_axis=0, concat_axis=0, tiled=True, axis...]
    unnamed x24 -> x26, local copies, waits for them, and re-layouts: 7.09 us -> 8.31 us
  transfers between devices with their start and end apart: 8 -> 9, of which waited for: 7 -> 9; matrix products, arithmetic and copies ran while one was open for 2% -> 2% of each run, Pallas kernels for 1% -> 1%
where the time goes in v8:
time: 297 us; the launch traced here: 296 us
  waiting for transfers between devices  151 us (51%)
  blocking collectives  54.4 us (18%)
  starting transfers between devices  47.2 us (16%)
  local copies, waits for them, and re-layouts  15.4 us (5%)
  between operations  14.3 us (5%)
  Pallas kernels  12 us (4%)
    all_to_all x6, waiting for transfers between devices, all_to_all(): lax.all_to_all(value, axis, split_axis=0, concat_axis=0, tiled=True, axis...  137 us
    all_to_all x2, blocking collectives, all_to_all(): lax.all_to_all(value, axis, split_axis=0, concat_axis=0, tiled=True, axis...  54.4 us
    all_to_all x6, starting transfers between devices, all_to_all(): lax.all_to_all(value, axis, split_axis=0, concat_axis=0, tiled=True, axis...  42.5 us
    pallas_call x7, Pallas kernels, call(): pl.pallas_call(kernel, out_shape=out_shape, in_specs=specs, out_specs=jax...  12 us
    all_gather x1, waiting for transfers between devices, body(): lax.all_gather(along_z[:, 160:288], 'gen', axis_index_groups=XC_GROUPS)  10.7 us
    unnamed x26, local copies, waits for them, and re-layouts  8.31 us
  transfers between devices with their start and end apart: 9, of which 9 were waited for; matrix products, arithmetic and copies ran while one was open for 2% of the time, Pallas kernels for 1%

profile of v8, /device:TPU:1, one launch (start us, length us, event | category | flops | bytes accessed | tf_op | source)
XLA Modules:
  0.0 295.7 jit_solution(4348038749644071488)
XLA Ops:
  7.2 0.7 pad_add_fusion
  8.0 0.9 copy-done.5
  8.9 0.8 copy-done.6
  10.0 41.3 %all_to_all.40 = bf16[4,496,128]{2,1,0:T(8,128)(2,1)S(1)} all-to-all(bf16[4,496,128]{2,1,0:T(8,128)(2,1)S(1)} %shard_map.121), channel_id=1, replica_groups={{0,128,256,384},{16,144,272,400},{32,160,288,416},{48,176,304,432},{64,..., dimensions={0} | all-to-all | bytes 1015808 | tf_op jit(solution)/shard_map/all_to_all | solution.py:319
  52.2 13.1 %all_to_all.41 = bf16[4,4,160,128]{3,2,1,0:T(8,128)(2,1)S(1)} all-to-all(bf16[4,4,160,128]{3,2,1,0:T(8,128)(2,1)S(1)} %broadcast_in_dim.26), channel_id=1, replica_groups={{0,32,64,96},{16,48,80,112},{128,160,192,224},{144,176,208,240},{256,28..., dimensions={0} | all-to-all | bytes 1310720 | tf_op jit(solution)/shard_map/all_to_all | solution.py:319
  65.3 4.6 %collective-permute-start = (bf16[16,160,128]{2,1,0:T(8,128)(2,1)S(1)}, bf16[16,160,128]{2,1,0:T(8,128)(2,1)S(1)}, u32[]{:S(2)}, u32[]{:S(2)}) collective-permute-start(bf16[16,160,128]{2,1,0:T(8,128)(2,1)S(1)} %bitcast.52), channel_id=1, source_target_pairs={{0,16},{16,0},{32,48},{48,32},{64,80},{80,64},{96,112},{112,96},{1... | collective-permute-start | bytes 1966088 | tf_op jit(solution)/shard_map/ppermute | solution.py:362
  70.1 1.5 collective-permute-done.other_ref
  71.6 10.7 %all-gather.5.cloned.1.call-done = bf16[32,128,128]{2,1,0:T(8,128)(2,1)} async-done(((bf16[4,128,128]{2,1,0:T(8,128)(2,1)}), bf16[32,128,128]{2,1,0:T(8,128)(2,1)}) %all-gather.5.cloned.1.call-update) | async-done | bytes 1048592 | tf_op jit(solution)/shard_map/all_gather | solution.py:360
  82.3 1.2 copy-done.4
  83.5 1.9 shard_map.122
  85.5 6.9 %all-to-all-start.2 = ((bf16[16,8,3712]{2,1,0:T(8,128)(2,1)}), bf16[16,8,3712]{2,1,0:T(8,128)(2,1)S(1)}, u32[]{:S(2)}, u32[]{:S(2)}) async-start(bf16[16,8,3712]{2,1,0:T(8,128)(2,1)} %bitcast.7), calls=%async_computation.2 | async-start | bytes 1900544 | tf_op jit(solution)/shard_map/all_to_all | solution.py:319
  92.6 0.7 slice.50
  93.6 23.8 %all-to-all-done.2.parts_ref = bf16[16,8,3712]{2,1,0:T(8,128)(2,1)S(1)} async-done(((bf16[16,8,3712]{2,1,0:T(8,128)(2,1)}), bf16[16,8,3712]{2,1,0:T(8,128)(2,1)S(1)}, u32[]{:S(2)}, u32[]{:S(2)}) %all-to-all-start.2) | async-done | bytes 950304 | tf_op jit(solution)/shard_map/all_to_all | solution.py:319
  117.4 2.6 shard_map.123
  120.1 4.2 %all-to-all-start.3 = ((bf16[16,8,2560]{2,1,0:T(8,128)(2,1)}), bf16[16,8,2560]{2,1,0:T(8,128)(2,1)S(1)}, u32[]{:S(2)}, u32[]{:S(2)}) async-start(bf16[16,8,2560]{2,1,0:T(8,128)(2,1)} %get-tuple-element.10), calls=%async_computation.3 | async-start | bytes 1310720 | tf_op jit(solution)/shard_map/all_to_all | solution.py:319
  124.3 1.6 all-gather.7.cloned.1.call-done
  125.9 16.9 %all-to-all-done.3 = bf16[16,8,2560]{2,1,0:T(8,128)(2,1)S(1)} async-done(((bf16[16,8,2560]{2,1,0:T(8,128)(2,1)}), bf16[16,8,2560]{2,1,0:T(8,128)(2,1)S(1)}, u32[]{:S(2)}, u32[]{:S(2)}) %all-to-all-start.3) | async-done | bytes 655392 | tf_op jit(solution)/shard_map/all_to_all | solution.py:319
  142.8 1.5 copy-done.2
  144.2 1.4 shard_map.124
  145.6 9.2 %all-to-all-start.4 = ((bf16[4,320,128]{2,1,0:T(8,128)(2,1)}), bf16[4,320,128]{2,1,0:T(8,128)(2,1)S(1)}, u32[]{:S(2)}, u32[]{:S(2)}) async-start(bf16[4,320,128]{2,1,0:T(8,128)(2,1)} %get-tuple-element.11), calls=%async_computation.4 | async-start | bytes 655360 | tf_op jit(solution)/shard_map/all_to_all | solution.py:319
  157.1 14.7 %all-to-all-done.4.layer_ref = bf16[4,320,128]{2,1,0:T(8,128)(2,1)S(1)} async-done(((bf16[4,320,128]{2,1,0:T(8,128)(2,1)}), bf16[4,320,128]{2,1,0:T(8,128)(2,1)S(1)}, u32[]{:S(2)}, u32[]{:S(2)}) %all-to-all-start.4) | async-done | bytes 327712 | tf_op jit(solution)/shard_map/all_to_all | solution.py:319
  171.8 2.2 shard_map.125
  174.0 1.5 copy-done
  175.5 12.9 %all-to-all-start.5 = ((bf16[128,80,128]{2,1,0:T(8,128)(2,1)}), bf16[128,80,128]{2,1,0:T(8,128)(2,1)S(1)}, u32[]{:S(2)}, u32[]{:S(2)}) async-start(bf16[128,80,128]{2,1,0:T(8,128)(2,1)} %copy-done), calls=%async_computation.5 | async-start | bytes 5242880 | tf_op jit(solution)/shard_map/all_to_all | solution.py:319
  189.1 62.0 %all-to-all-done.5 = bf16[128,80,128]{2,1,0:T(8,128)(2,1)S(1)} async-done(((bf16[128,80,128]{2,1,0:T(8,128)(2,1)}), bf16[128,80,128]{2,1,0:T(8,128)(2,1)S(1)}, u32[]{:S(2)}, u32[]{:S(2)}) %all-to-all-start.5) | async-done | bytes 2621472 | tf_op jit(solution)/shard_map/all_to_all | solution.py:319
  251.1 1.7 copy-done.1
  252.9 2.6 shard_map.126
  256.4 5.8 %all-to-all-start.6 = ((f32[32,1,24]{2,1,0:T(1,128)}), f32[32,1,24]{2,1,0:T(1,128)S(1)}, u32[]{:S(2)}, u32[]{:S(2)}) async-start(f32[32,1,24]{2,1,0:T(1,128)} %copy.84), calls=%async_computation.6 | async-start | bytes 32768 | tf_op jit(solution)/shard_map/all_to_all | solution.py:319
  262.5 13.8 %all-to-all-done.6 = f32[32,1,24]{2,1,0:T(1,128)S(1)} async-done(((f32[32,1,24]{2,1,0:T(1,128)}), f32[32,1,24]{2,1,0:T(1,128)S(1)}, u32[]{:S(2)}, u32[]{:S(2)}) %all-to-all-start.6) | async-done | bytes 3104 | tf_op jit(solution)/shard_map/all_to_all | solution.py:319
  276.4 1.0 shard_map.127
  277.5 3.5 %all-to-all-start.7 = ((f32[16,4,8]{2,1,0:T(4,128)}), f32[16,4,8]{2,1,0:T(4,128)S(1)}, u32[]{:S(2)}, u32[]{:S(2)}) async-start(f32[16,4,8]{2,1,0:T(4,128)} %bitcast.50), calls=%async_computation.7 | async-start | bytes 65536 | tf_op jit(solution)/shard_map/all_to_all | solution.py:319
  282.3 5.5 %all-to-all-done.7 = f32[16,4,8]{2,1,0:T(4,128)S(1)} async-done(((f32[16,4,8]{2,1,0:T(4,128)}), f32[16,4,8]{2,1,0:T(4,128)S(1)}, u32[]{:S(2)}, u32[]{:S(2)}) %all-to-all-start.7) | async-done | bytes 2080 | tf_op jit(solution)/shard_map/all_to_all | solution.py:319
  (83 shorter events, 8.5 us)
Async XLA Ops:
  7.2 62.7 %copy-start.10 = (bf16[320]{0:T(512)(128)(2,1)S(1)}, bf16[320]{0:T(512)(128)(2,1)}, u32[]{:S(2)}) copy-start(bf16[320]{0:T(512)(128)(2,1)} %param.13) | copy-start | bytes 1924
  7.2 75.1 %all-gather.5.cloned.1.call-start = ((), (), s32[]{:S(2)}) async-start(), calls=%async_computation.8 | async-start | bytes 1179648 | tf_op jit(solution)/shard_map/all_gather | solution.py:360
  8.0 0.9 copy-start.5
  8.9 0.8 copy-start.6
  9.7 60.2 %copy-start.7 = (bf16[2,64,320]{2,1,0:T(8,128)(2,1)S(1)}, bf16[2,64,320]{2,1,0:T(8,128)(2,1)}, u32[]{:S(2)}) copy-start(bf16[2,64,320]{2,1,0:T(8,128)(2,1)} %param.10) | copy-start | bytes 245764
  65.3 27.2 %copy-start.11 = (s32[4]{0:T(128)S(1)}, s32[4]{0:T(128)}, u32[]{:S(2)}) copy-start(s32[4]{0:T(128)} %param.12) | copy-start | bytes 52
  65.3 6.3 %collective-permute-start = (bf16[16,160,128]{2,1,0:T(8,128)(2,1)S(1)}, bf16[16,160,128]{2,1,0:T(8,128)(2,1)S(1)}, u32[]{:S(2)}, u32[]{:S(2)}) collective-permute-start(bf16[16,160,128]{2,1,0:T(8,128)(2,1)S(1)} %bitcast.52), channel_id=1, source_target_pairs={{0,16},{16,0},{32,48},{48,32},{64,80},{80,64},{96,112},{112,96},{1... | collective-permute-start | bytes 1966088 | tf_op jit(solution)/shard_map/ppermute | solution.py:362
  70.0 47.4 %copy-start.3 = (bf16[4,128,1024]{2,1,0:T(8,128)(2,1)S(1)}, bf16[4,128,1024]{2,1,0:T(8,128)(2,1)}, u32[]{:S(2)}) copy-start(bf16[4,128,1024]{2,1,0:T(8,128)(2,1)} %cache_ref.1) | copy-start | bytes 3145732
  82.3 1.2 copy-start.4
  85.5 31.9 %all-to-all-start.2 = ((bf16[16,8,3712]{2,1,0:T(8,128)(2,1)}), bf16[16,8,3712]{2,1,0:T(8,128)(2,1)S(1)}, u32[]{:S(2)}, u32[]{:S(2)}) async-start(bf16[16,8,3712]{2,1,0:T(8,128)(2,1)} %bitcast.7), calls=%async_computation.2 | async-start | bytes 1900544 | tf_op jit(solution)/shard_map/all_to_all | solution.py:319
  92.4 33.5 %all-gather.7.cloned.1.call-start = ((), (), s32[]{:S(2)}) async-start(), calls=%async_computation.9 | async-start | bytes 1916928 | tf_op jit(solution)/shard_map/all_gather | solution.py:359
  120.1 22.7 %all-to-all-start.3 = ((bf16[16,8,2560]{2,1,0:T(8,128)(2,1)}), bf16[16,8,2560]{2,1,0:T(8,128)(2,1)S(1)}, u32[]{:S(2)}, u32[]{:S(2)}) async-start(bf16[16,8,2560]{2,1,0:T(8,128)(2,1)} %get-tuple-element.10), calls=%async_computation.3 | async-start | bytes 1310720 | tf_op jit(solution)/shard_map/all_to_all | solution.py:319
  142.8 1.5 copy-start.2
  145.6 26.2 %all-to-all-start.4 = ((bf16[4,320,128]{2,1,0:T(8,128)(2,1)}), bf16[4,320,128]{2,1,0:T(8,128)(2,1)S(1)}, u32[]{:S(2)}, u32[]{:S(2)}) async-start(bf16[4,320,128]{2,1,0:T(8,128)(2,1)} %get-tuple-element.11), calls=%async_computation.4 | async-start | bytes 655360 | tf_op jit(solution)/shard_map/all_to_all | solution.py:319
  174.0 1.5 copy-start
  175.5 12.9 %copy-start.8 = (bf16[5120]{0:T(1024)(128)(2,1)S(1)}, bf16[5120]{0:T(1024)(128)(2,1)}, u32[]{:S(2)}) copy-start(bf16[5120]{0:T(1024)(128)(2,1)} %param.16) | copy-start | bytes 30724
  175.5 12.9 %copy-start.9 = (s32[1,64,2]{1,2,0:T(2,128)S(1)}, s32[1,64,2]{1,2,0:T(2,128)}, u32[]{:S(2)}) copy-start(s32[1,64,2]{1,2,0:T(2,128)} %param.18) | copy-start | bytes 1540
  175.5 75.6 %all-to-all-start.5 = ((bf16[128,80,128]{2,1,0:T(8,128)(2,1)}), bf16[128,80,128]{2,1,0:T(8,128)(2,1)S(1)}, u32[]{:S(2)}, u32[]{:S(2)}) async-start(bf16[128,80,128]{2,1,0:T(8,128)(2,1)} %copy-done), calls=%async_computation.5 | async-start | bytes 5242880 | tf_op jit(solution)/shard_map/all_to_all | solution.py:319
  251.1 1.7 copy-start.1
  256.4 19.9 %all-to-all-start.6 = ((f32[32,1,24]{2,1,0:T(1,128)}), f32[32,1,24]{2,1,0:T(1,128)S(1)}, u32[]{:S(2)}, u32[]{:S(2)}) async-start(f32[32,1,24]{2,1,0:T(1,128)} %copy.84), calls=%async_computation.6 | async-start | bytes 32768 | tf_op jit(solution)/shard_map/all_to_all | solution.py:319
  277.5 10.3 %all-to-all-start.7 = ((f32[16,4,8]{2,1,0:T(4,128)}), f32[16,4,8]{2,1,0:T(4,128)S(1)}, u32[]{:S(2)}, u32[]{:S(2)}) async-start(f32[16,4,8]{2,1,0:T(4,128)} %bitcast.50), calls=%async_computation.7 | async-start | bytes 65536 | tf_op jit(solution)/shard_map/all_to_all | solution.py:319
Sparse Core Ops, SparseCore 0:
  52.2 30.0 all-gather.4
  95.3 30.5 all-gather.6

commit v9 on v5

--- a/solution.py
+++ b/solution.py
@@ -26,10 +26,10 @@
 bf16 = jnp.bfloat16
 f32 = jnp.float32
 i32 = jnp.int32
-VMEM_BYTES = 48 * 1024 * 1024
-
-
-def call(kernel, out_shape, *args, scalars=0, scratch=()):
+MIB = 1024 * 1024
+
+
+def call(kernel, out_shape, *args, scalars=0, scratch=(), vmem=48):
     specs = [pl.BlockSpec(memory_space=pltpu.SMEM)] * scalars
     specs += [pl.BlockSpec(memory_space=pltpu.VMEM)] * (len(args) - scalars)
     return pl.pallas_call(
@@ -38,7 +38,7 @@
         in_specs=specs,
         out_specs=jax.tree.map(lambda _: pl.BlockSpec(memory_space=pltpu.VMEM), out_shape),
         scratch_shapes=list(scratch),
-        compiler_params=pltpu.CompilerParams(vmem_limit_bytes=VMEM_BYTES),
+        compiler_params=pltpu.CompilerParams(vmem_limit_bytes=vmem * MIB),
     )(*args)
 
 
@@ -404,6 +404,7 @@
         final_gain.reshape(1, D),
         head,
         offset,
+        vmem=60,
     )
     stats = stats[:3].reshape(3, 8, 4, 8).transpose(2, 1, 0, 3).reshape(GEN, 1, 24)
     stats = all_to_all(stats, "gen").reshape(GEN, 24).T

time: 288 us -> 290 us (level)
  Pallas kernels: 10.4 us -> 15.1 us
    pallas_call x7, Pallas kernels: 10.4 us -> 15.1 us  [call(): pl.pallas_call(kernel, out_shape=out_shape, in_specs=specs, out_specs=jax...]
    unnamed x24 -> x20, local copies, waits for them, and re-layouts: 7.09 us -> 3.86 us
  transfers between devices with their start and end apart: 8 -> 8, of which waited for: 7 -> 7; matrix products, arithmetic and copies ran while one was open for 2% -> 3% of each run, Pallas kernels for 1% -> 1%
where the time goes in v9:
time: 290 us; the launch traced here: 289 us
  waiting for transfers between devices  139 us (48%)
  blocking collectives  60 us (21%)
  starting transfers between devices  44.9 us (15%)
  Pallas kernels  15.1 us (5%)
  between operations  14.4 us (5%)
  local copies, waits for them, and re-layouts  13.9 us (5%)
    all_to_all x6, waiting for transfers between devices, all_to_all(): lax.all_to_all(value, axis, split_axis=0, concat_axis=0, tiled=True, axis...  137 us
    all_to_all x2, blocking collectives, all_to_all(): lax.all_to_all(value, axis, split_axis=0, concat_axis=0, tiled=True, axis...  60 us
    all_to_all x6, starting transfers between devices, all_to_all(): lax.all_to_all(value, axis, split_axis=0, concat_axis=0, tiled=True, axis...  40.4 us
    pallas_call x7, Pallas kernels, call(): pl.pallas_call(kernel, out_shape=out_shape, in_specs=specs, out_specs=jax...  15.1 us
  transfers between devices with their start and end apart: 8, of which 7 were waited for; matrix products, arithmetic and copies ran while one was open for 3% of the time, Pallas kernels for 1%

profile of v9, /device:TPU:1, one launch (start us, length us, event | category | flops | bytes accessed | tf_op | source)
XLA Modules:
  0.0 289.3 jit_solution(4931115007995527385)
XLA Ops:
  7.2 0.7 pad_add_fusion
  8.0 0.9 copy-done.2
  8.9 0.8 copy-done.3
  10.0 41.3 %all_to_all.40 = bf16[4,496,128]{2,1,0:T(8,128)(2,1)S(1)} all-to-all(bf16[4,496,128]{2,1,0:T(8,128)(2,1)S(1)} %broadcast_in_dim.28), channel_id=1, replica_groups={{0,128,256,384},{16,144,272,400},{32,160,288,416},{48,176,304,432},{64,..., dimensions={0} | all-to-all | bytes 1015808 | tf_op jit(solution)/shard_map/all_to_all | solution.py:311
  51.6 18.7 %all_to_all.41 = bf16[4,4,288,128]{3,2,1,0:T(8,128)(2,1)S(1)} all-to-all(bf16[4,4,288,128]{3,2,1,0:T(8,128)(2,1)S(1)} %broadcast_in_dim.29), channel_id=1, replica_groups={{0,32,64,96},{16,48,80,112},{128,160,192,224},{144,176,208,240},{256,28..., dimensions={0} | all-to-all | bytes 2359296 | tf_op jit(solution)/shard_map/all_to_all | solution.py:311
  70.3 4.5 %collective-permute-start = (bf16[16,288,128]{2,1,0:T(8,128)(2,1)S(1)}, bf16[16,288,128]{2,1,0:T(8,128)(2,1)S(1)}, u32[]{:S(2)}, u32[]{:S(2)}) collective-permute-start(bf16[16,288,128]{2,1,0:T(8,128)(2,1)S(1)} %bitcast.50), channel_id=1, source_target_pairs={{0,16},{16,0},{32,48},{48,32},{64,80},{80,64},{96,112},{112,96},{1... | collective-permute-start | bytes 3538952 | tf_op jit(solution)/shard_map/ppermute | solution.py:353
  74.9 2.3 collective-permute-done.other_ref
  77.2 1.9 shard_map.122
  79.2 10.7 %all-to-all-start.2 = ((bf16[16,8,3712]{2,1,0:T(8,128)(2,1)}), bf16[16,8,3712]{2,1,0:T(8,128)(2,1)S(1)}, u32[]{:S(2)}, u32[]{:S(2)}) async-start(bf16[16,8,3712]{2,1,0:T(8,128)(2,1)} %bitcast.6), calls=%async_computation.2 | async-start | bytes 1900544 | tf_op jit(solution)/shard_map/all_to_all | solution.py:311
  90.2 0.7 slice.45
  91.1 23.8 %all-to-all-done.2.parts_ref = bf16[16,8,3712]{2,1,0:T(8,128)(2,1)S(1)} async-done(((bf16[16,8,3712]{2,1,0:T(8,128)(2,1)}), bf16[16,8,3712]{2,1,0:T(8,128)(2,1)S(1)}, u32[]{:S(2)}, u32[]{:S(2)}) %all-to-all-start.2) | async-done | bytes 950304 | tf_op jit(solution)/shard_map/all_to_all | solution.py:311
  114.9 1.8 shard_map.123
  116.7 0.9 broadcast_in_dim.32
  117.6 4.3 %all-to-all-start.3 = ((bf16[16,8,2560]{2,1,0:T(8,128)(2,1)}), bf16[16,8,2560]{2,1,0:T(8,128)(2,1)S(1)}, u32[]{:S(2)}, u32[]{:S(2)}) async-start(bf16[16,8,2560]{2,1,0:T(8,128)(2,1)} %broadcast_in_dim.32), calls=%async_computation.3 | async-start | bytes 1310720 | tf_op jit(solution)/shard_map/all_to_all | solution.py:311
  122.0 18.5 %all-to-all-done.3 = bf16[16,8,2560]{2,1,0:T(8,128)(2,1)S(1)} async-done(((bf16[16,8,2560]{2,1,0:T(8,128)(2,1)}), bf16[16,8,2560]{2,1,0:T(8,128)(2,1)S(1)}, u32[]{:S(2)}, u32[]{:S(2)}) %all-to-all-start.3) | async-done | bytes 655392 | tf_op jit(solution)/shard_map/all_to_all | solution.py:311
  140.5 1.5 copy-done
  142.5 0.8 broadcast_in_dim.33
  143.3 3.5 %all-to-all-start.4 = ((bf16[4,320,128]{2,1,0:T(8,128)(2,1)}), bf16[4,320,128]{2,1,0:T(8,128)(2,1)S(1)}, u32[]{:S(2)}, u32[]{:S(2)}) async-start(bf16[4,320,128]{2,1,0:T(8,128)(2,1)} %broadcast_in_dim.33), calls=%async_computation.4 | async-start | bytes 655360 | tf_op jit(solution)/shard_map/all_to_all | solution.py:311
  149.1 14.8 %all-to-all-done.4.layer_ref = bf16[4,320,128]{2,1,0:T(8,128)(2,1)S(1)} async-done(((bf16[4,320,128]{2,1,0:T(8,128)(2,1)}), bf16[4,320,128]{2,1,0:T(8,128)(2,1)S(1)}, u32[]{:S(2)}, u32[]{:S(2)}) %all-to-all-start.4) | async-done | bytes 327712 | tf_op jit(solution)/shard_map/all_to_all | solution.py:311
  163.9 3.7 %shard_map.125 = bf16[128,80,128]{2,1,0:T(8,128)(2,1)} custom-call(bf16[4,320,128]{2,1,0:T(8,128)(2,1)S(1)} %all-to-all-done.4.layer_ref, s32[2048,2]{1,0:T(8,128)S(1)} %broadcast_add_fusion.spot_ref), custom_call_target="tpu_custom_call" | custom-call | tf_op jit(solution)/shard_map/pallas_call | solution.py:35
  167.6 12.9 %all-to-all-start.5 = ((bf16[128,80,128]{2,1,0:T(8,128)(2,1)}), bf16[128,80,128]{2,1,0:T(8,128)(2,1)}, u32[]{:S(2)}, u32[]{:S(2)}) async-start(bf16[128,80,128]{2,1,0:T(8,128)(2,1)} %shard_map.125), calls=%async_computation.5 | async-start | bytes 5242880 | tf_op jit(solution)/shard_map/all_to_all | solution.py:311
  181.6 0.7 reshape.129.offset_ref
  182.3 60.5 %all-to-all-done.5 = bf16[128,80,128]{2,1,0:T(8,128)(2,1)} async-done(((bf16[128,80,128]{2,1,0:T(8,128)(2,1)}), bf16[128,80,128]{2,1,0:T(8,128)(2,1)}, u32[]{:S(2)}, u32[]{:S(2)}) %all-to-all-start.5) | async-done | bytes 2621472 | tf_op jit(solution)/shard_map/all_to_all | solution.py:311
  242.9 5.8 %shard_map.126 = f32[8,256]{1,0:T(8,128)} custom-call(bf16[8,16,80,128]{3,2,1,0:T(8,128)(2,1)} %bitcast.12.rows_ref, bf16[1,5120]{1,0:T(2,128)(2,1)} %reshape.125.gain_ref, bf16[5120,256]{1,0:T(8,128)(2,1)} %head_ref.1, s32[1,256]{1,0:T(1,128)} %reshape.129.offset_ref), custom_call_target="tpu_custom_call" | custom-call | tf_op jit(solution)/shard_map/pallas_call | solution.py:35
  248.6 0.7 slice.49
  249.6 0.7 copy.84
  250.3 5.5 %all-to-all-start.6 = ((f32[32,1,24]{2,1,0:T(1,128)}), f32[32,1,24]{2,1,0:T(1,128)S(1)}, u32[]{:S(2)}, u32[]{:S(2)}) async-start(f32[32,1,24]{2,1,0:T(1,128)} %copy.84), calls=%async_computation.6 | async-start | bytes 32768 | tf_op jit(solution)/shard_map/all_to_all | solution.py:311
  256.1 13.8 %all-to-all-done.6 = f32[32,1,24]{2,1,0:T(1,128)S(1)} async-done(((f32[32,1,24]{2,1,0:T(1,128)}), f32[32,1,24]{2,1,0:T(1,128)S(1)}, u32[]{:S(2)}, u32[]{:S(2)}) %all-to-all-start.6) | async-done | bytes 3104 | tf_op jit(solution)/shard_map/all_to_all | solution.py:311
  270.1 1.0 shard_map.127
  271.1 3.5 %all-to-all-start.7 = ((f32[16,4,8]{2,1,0:T(4,128)}), f32[16,4,8]{2,1,0:T(4,128)S(1)}, u32[]{:S(2)}, u32[]{:S(2)}) async-start(f32[16,4,8]{2,1,0:T(4,128)} %bitcast.49), calls=%async_computation.7 | async-start | bytes 65536 | tf_op jit(solution)/shard_map/all_to_all | solution.py:311
  275.9 5.5 %all-to-all-done.7 = f32[16,4,8]{2,1,0:T(4,128)S(1)} async-done(((f32[16,4,8]{2,1,0:T(4,128)}), f32[16,4,8]{2,1,0:T(4,128)S(1)}, u32[]{:S(2)}, u32[]{:S(2)}) %all-to-all-start.7) | async-done | bytes 2080 | tf_op jit(solution)/shard_map/all_to_all | solution.py:311
  281.8 0.7 copy.88
  (76 shorter events, 7.7 us)
Async XLA Ops:
  8.0 0.9 copy-start.2
  8.9 0.8 copy-start.3
  51.4 23.4 %copy-start.7 = (bf16[320]{0:T(512)(128)(2,1)S(1)}, bf16[320]{0:T(512)(128)(2,1)}, u32[]{:S(2)}) copy-start(bf16[320]{0:T(512)(128)(2,1)} %param.13) | copy-start | bytes 1924
  51.4 23.4 %copy-start.4 = (bf16[2,64,320]{2,1,0:T(8,128)(2,1)S(1)}, bf16[2,64,320]{2,1,0:T(8,128)(2,1)}, u32[]{:S(2)}) copy-start(bf16[2,64,320]{2,1,0:T(8,128)(2,1)} %param.10) | copy-start | bytes 245764
  70.3 6.9 %collective-permute-start = (bf16[16,288,128]{2,1,0:T(8,128)(2,1)S(1)}, bf16[16,288,128]{2,1,0:T(8,128)(2,1)S(1)}, u32[]{:S(2)}, u32[]{:S(2)}) collective-permute-start(bf16[16,288,128]{2,1,0:T(8,128)(2,1)S(1)} %bitcast.50), channel_id=1, source_target_pairs={{0,16},{16,0},{32,48},{48,32},{64,80},{80,64},{96,112},{112,96},{1... | collective-permute-start | bytes 3538952 | tf_op jit(solution)/shard_map/ppermute | solution.py:353
  77.2 12.7 %copy-start.8 = (s32[4]{0:T(128)S(1)}, s32[4]{0:T(128)}, u32[]{:S(2)}) copy-start(s32[4]{0:T(128)} %param.12) | copy-start | bytes 52
  79.2 35.7 %copy-start.1 = (bf16[4,128,1024]{2,1,0:T(8,128)(2,1)S(1)}, bf16[4,128,1024]{2,1,0:T(8,128)(2,1)}, u32[]{:S(2)}) copy-start(bf16[4,128,1024]{2,1,0:T(8,128)(2,1)} %cache_ref.1) | copy-start | bytes 3145732
  79.2 35.7 %all-to-all-start.2 = ((bf16[16,8,3712]{2,1,0:T(8,128)(2,1)}), bf16[16,8,3712]{2,1,0:T(8,128)(2,1)S(1)}, u32[]{:S(2)}, u32[]{:S(2)}) async-start(bf16[16,8,3712]{2,1,0:T(8,128)(2,1)} %bitcast.6), calls=%async_computation.2 | async-start | bytes 1900544 | tf_op jit(solution)/shard_map/all_to_all | solution.py:311
  89.9 32.0 %all-gather.3.cloned.1.call-start = ((), (), s32[]{:S(2)}) async-start(), calls=%async_computation.8 | async-start | bytes 1916928 | tf_op jit(solution)/shard_map/all_gather | solution.py:351
  117.6 22.9 %all-to-all-start.3 = ((bf16[16,8,2560]{2,1,0:T(8,128)(2,1)}), bf16[16,8,2560]{2,1,0:T(8,128)(2,1)S(1)}, u32[]{:S(2)}, u32[]{:S(2)}) async-start(bf16[16,8,2560]{2,1,0:T(8,128)(2,1)} %broadcast_in_dim.32), calls=%async_computation.3 | async-start | bytes 1310720 | tf_op jit(solution)/shard_map/all_to_all | solution.py:311
  140.5 1.5 copy-start
  143.3 20.6 %all-to-all-start.4 = ((bf16[4,320,128]{2,1,0:T(8,128)(2,1)}), bf16[4,320,128]{2,1,0:T(8,128)(2,1)S(1)}, u32[]{:S(2)}, u32[]{:S(2)}) async-start(bf16[4,320,128]{2,1,0:T(8,128)(2,1)} %broadcast_in_dim.33), calls=%async_computation.4 | async-start | bytes 655360 | tf_op jit(solution)/shard_map/all_to_all | solution.py:311
  167.6 12.9 %copy-start.5 = (bf16[5120]{0:T(1024)(128)(2,1)S(1)}, bf16[5120]{0:T(1024)(128)(2,1)}, u32[]{:S(2)}) copy-start(bf16[5120]{0:T(1024)(128)(2,1)} %param.16) | copy-start | bytes 30724
  167.6 13.5 %copy-start.6 = (s32[1,64,2]{1,2,0:T(2,128)S(1)}, s32[1,64,2]{1,2,0:T(2,128)}, u32[]{:S(2)}) copy-start(s32[1,64,2]{1,2,0:T(2,128)} %param.18) | copy-start | bytes 1540
  167.6 75.3 %all-to-all-start.5 = ((bf16[128,80,128]{2,1,0:T(8,128)(2,1)}), bf16[128,80,128]{2,1,0:T(8,128)(2,1)}, u32[]{:S(2)}, u32[]{:S(2)}) async-start(bf16[128,80,128]{2,1,0:T(8,128)(2,1)} %shard_map.125), calls=%async_computation.5 | async-start | bytes 5242880 | tf_op jit(solution)/shard_map/all_to_all | solution.py:311
  250.3 19.7 %all-to-all-start.6 = ((f32[32,1,24]{2,1,0:T(1,128)}), f32[32,1,24]{2,1,0:T(1,128)S(1)}, u32[]{:S(2)}, u32[]{:S(2)}) async-start(f32[32,1,24]{2,1,0:T(1,128)} %copy.84), calls=%async_computation.6 | async-start | bytes 32768 | tf_op jit(solution)/shard_map/all_to_all | solution.py:311
  271.1 10.3 %all-to-all-start.7 = ((f32[16,4,8]{2,1,0:T(4,128)}), f32[16,4,8]{2,1,0:T(4,128)S(1)}, u32[]{:S(2)}, u32[]{:S(2)}) async-start(f32[16,4,8]{2,1,0:T(4,128)} %bitcast.49), calls=%async_computation.7 | async-start | bytes 65536 | tf_op jit(solution)/shard_map/all_to_all | solution.py:311
Sparse Core Ops, SparseCore 0:
  92.9 25.7 all-gather.2
